TPU v7x, 32 devices: a whole 2x2x4 slice. The times are simulated.
32 devices in a mesh: groups: 2 (over x), tile: 4 (over y, core), sect: 4 (over z).
Axes of the slice: x: 2, y: 2, z: 4, core: 2. Of those that a mesh axis runs over, the one named last changes fastest.
Arguments:
- source_probes: float32 [2, 32, 8192], P(None, 'groups', ('tile', 'sect')), parts along dimension 1, may hold values from -6 to 6
- near_blocks: bfloat16 [4, 9, 512, 8192], P('groups', None, None, ('tile', 'sect')), parts along dimension 0, may hold values from -0.0625 to 0.0625
- bloch_angle: float32 [4], P('groups'), parts along dimension 0, may hold values from -3.140625 to 3.140625
- grid_row: int32 [8192], P(('tile', 'sect')), may hold values from 0 to 511, as said below
- grid_col: int32 [8192], P(('tile', 'sect')), may hold values from 0 to 511, as said below
- stencil: bfloat16 [4, 4, 8192], P(None, None, ('tile', 'sect')), may hold values from 0.19921875 to 1
- recip_kernel: float32 [1024, 512], P('groups', ('tile', 'sect')), parts along dimension 0, may hold values from 0.1 to 2
Outputs:
- first_image: float32 [2, 32, 8192], P(None, 'groups', ('tile', 'sect')), parts along dimension 1
- second_image: float32 [2, 32, 8192], P(None, 'groups', ('tile', 'sect')), parts along dimension 1
There are 2 independent parts, one for each index of `groups`. A program takes and returns all parts, laid end to end along the dimension named above; an argument that names none is the same for every part. Nothing has to cross between parts.
Inputs may be any that keep to these rules, and one draw needn't show every extreme that they name: `grid_row`: panel i has its first stencil row among the 32 grid rows (i // 512) * 32 to (i // 512 + 1) * 32 - 1, and every grid row is the first row of some panel. `grid_col`: every grid column is the first column of some panel.
All inputs are finite; a program needn't handle non-finite values.
Results may differ from a plain program's by a relative error of at most 0.0032.
Values may be sent and summed in bfloat16 or wider, within the bound.
No kernel may reach another device: no remote copies, remote signals or barrier semaphores. Data moves between devices by JAX's collectives and lax.ppermute only.
A program may use at most 128 MiB of HBM per device.

v0:
```python
import math

import jax
import jax.numpy as jnp
from jax import lax
from jax.sharding import PartitionSpec as P

STENCIL = 4
NG1 = 512
NG2 = 512


HIGHEST = lax.Precision.HIGHEST


def with_halo(cells, sides, width):
    for axis, dim in sides:
        count = lax.axis_size(axis)
        head = lax.slice_in_dim(cells, 0, width, axis=dim)
        tail = lax.slice_in_dim(cells, cells.shape[dim] - width, cells.shape[dim], axis=dim)
        cells = jnp.concatenate(
            [
                lax.ppermute(tail, axis, [(i, (i + 1) % count) for i in range(count)]),
                cells,
                lax.ppermute(head, axis, [((i + 1) % count, i) for i in range(count)]),
            ],
            axis=dim,
        )
    return cells


def shifted(array, axis, by):
    count = lax.axis_size(axis)
    return lax.ppermute(array, axis, [(i, (i + by) % count) for i in range(count)])


def twiddle(first_index, second_index, length):
    product = first_index[:, None] * second_index[None, :] % length
    phase_angle = 2.0 * math.pi / length * product.astype(jnp.float32)
    return (jnp.cos(phase_angle), jnp.sin(phase_angle))


def spread_matrix(grid_row, grid_col, stencil, rows_dev):
    panels = grid_row.shape[0]
    span = (rows_dev + STENCIL - 1) * NG2
    local_row = grid_row % rows_dev
    cells = lax.broadcasted_iota(jnp.int32, (panels, span), 1)
    matrix = jnp.zeros((panels, span), jnp.float32)
    for row_off in range(STENCIL):
        for col_off in range(STENCIL):
            target = (local_row + row_off) * NG2 + (grid_col + col_off) % NG2
            matrix = matrix + jnp.where(
                cells == target[:, None],
                stencil[row_off, col_off].astype(jnp.float32)[:, None],
                0.0,
            )
    return matrix.astype(jnp.bfloat16)


def near_term(rounded, near_blocks, bloch_angle):
    probe_rows = rounded.shape[1]
    panels = rounded.shape[2]
    packed = rounded.reshape(2 * probe_rows, 1, 1, panels)
    widened = with_halo(packed, (("tile", 1), ("sect", 2)), 1)
    tile_pos = lax.axis_index("tile")
    tile_count = lax.axis_size("tile")
    sect_pos = lax.axis_index("sect")
    sect_count = lax.axis_size("sect")
    total_real = jnp.zeros((probe_rows, panels), jnp.float32)
    total_imag = jnp.zeros((probe_rows, panels), jnp.float32)
    for tile_off in (-1, 0, 1):
        for sect_off in (-1, 0, 1):
            index = (tile_off + 1) * 3 + sect_off + 1
            piece = widened[:, tile_off + 1, sect_off + 1, :]
            with_real = jnp.dot(piece, near_blocks[0, index], preferred_element_type=jnp.float32)
            with_imag = jnp.dot(piece, near_blocks[1, index], preferred_element_type=jnp.float32)
            part_real = with_real[:probe_rows] - with_imag[probe_rows:]
            part_imag = with_real[probe_rows:] + with_imag[:probe_rows]
            if tile_off != 0 or sect_off != 0:
                phase_angle = jnp.float32(0.0)
                if tile_off != 0:
                    border = tile_pos == (tile_count - 1 if tile_off == 1 else 0)
                    phase_angle = jnp.where(border, bloch_angle[0] * tile_off, 0.0)
                if sect_off != 0:
                    border = sect_pos == (sect_count - 1 if sect_off == 1 else 0)
                    phase_angle = phase_angle + jnp.where(border, bloch_angle[1] * sect_off, 0.0)
                cos_part = jnp.cos(phase_angle)
                sin_part = jnp.sin(phase_angle)
                part_real, part_imag = (
                    part_real * cos_part - part_imag * sin_part,
                    part_real * sin_part + part_imag * cos_part,
                )
            total_real = total_real + part_real
            total_imag = total_imag + part_imag
    return jnp.stack([total_real, total_imag])


def recip_term(rounded, matrix, recip_kernel, col_table, row_forward, row_inverse):
    probe_rows = rounded.shape[1]
    extended = matrix.shape[1] // NG2
    rows_dev = extended - (STENCIL - 1)
    flat = rounded.reshape(2 * probe_rows, rounded.shape[2])
    spread = jnp.dot(flat, matrix, preferred_element_type=jnp.float32)
    spread = spread.reshape(2 * probe_rows, extended, NG2)
    overflow = spread[:, rows_dev:]
    incoming = shifted(overflow, ("tile", "sect"), 1)
    grid = jnp.concatenate(
        [spread[:, : STENCIL - 1] + incoming, spread[:, STENCIL - 1 : rows_dev]], axis=1
    )
    grid = grid.transpose(1, 0, 2).reshape(rows_dev * 2 * probe_rows, NG2)
    mixed = jnp.dot(grid, col_table, precision=HIGHEST, preferred_element_type=jnp.float32)
    mixed = mixed.reshape(rows_dev, 2, probe_rows, 2, NG2)
    spec_real = mixed[:, 0, :, 0] + mixed[:, 1, :, 1]
    spec_imag = mixed[:, 1, :, 0] - mixed[:, 0, :, 1]
    spectrum = jnp.stack([spec_real, spec_imag], axis=1).reshape(rows_dev, 2 * probe_rows, NG2)
    columns = lax.all_to_all(spectrum, ("tile", "sect"), split_axis=2, concat_axis=0, tiled=True)
    cols_dev = columns.shape[2]
    stacked = jnp.dot(
        row_forward,
        columns.reshape(NG1, 2 * probe_rows * cols_dev),
        precision=HIGHEST,
        preferred_element_type=jnp.float32,
    )
    stacked = stacked.reshape(2, NG1, 2, probe_rows, cols_dev)
    scale = recip_kernel[:, None, :] / (NG1 * NG2)
    freq_real = (stacked[0, :, 0] + stacked[1, :, 1]) * scale
    freq_imag = (stacked[0, :, 1] - stacked[1, :, 0]) * scale
    freq = jnp.stack([freq_real, freq_imag], axis=1).reshape(NG1, 2 * probe_rows * cols_dev)
    back = jnp.dot(row_inverse, freq, precision=HIGHEST, preferred_element_type=jnp.float32)
    back = back.reshape(2, NG1, 2, probe_rows, cols_dev)
    out_real = back[0, :, 0] - back[1, :, 1]
    out_imag = back[0, :, 1] + back[1, :, 0]
    spatial = jnp.stack([out_real, out_imag], axis=1).reshape(NG1, 2 * probe_rows, cols_dev)
    row_blocks = lax.all_to_all(spatial, ("tile", "sect"), split_axis=0, concat_axis=2, tiled=True)
    mixed = jnp.dot(
        row_blocks.reshape(rows_dev * 2 * probe_rows, NG2),
        col_table,
        precision=HIGHEST,
        preferred_element_type=jnp.float32,
    )
    mixed = mixed.reshape(rows_dev, 2, probe_rows, 2, NG2)
    field_real = mixed[:, 0, :, 0] - mixed[:, 1, :, 1]
    field_imag = mixed[:, 1, :, 0] + mixed[:, 0, :, 1]
    field = (
        jnp.stack([field_real, field_imag], axis=0)
        .transpose(0, 2, 1, 3)
        .reshape(2 * probe_rows, rows_dev, NG2)
    )
    field_low = field.astype(jnp.bfloat16)
    following = shifted(field_low[:, : STENCIL - 1], ("tile", "sect"), -1)
    whole = jnp.concatenate([field_low, following], axis=1).reshape(2 * probe_rows, extended * NG2)
    result = lax.dot_general(
        whole, matrix, (((1,), (1,)), ((), ())), preferred_element_type=jnp.float32
    )
    return result.reshape(2, probe_rows, rounded.shape[2])


def local(source_probes, near_blocks, bloch_angle, grid_row, grid_col, stencil, recip_kernel):
    tile_count = lax.axis_size("tile")
    sect_count = lax.axis_size("sect")
    rows_dev = NG1 // (tile_count * sect_count)
    matrix = spread_matrix(grid_row, grid_col, stencil, rows_dev)
    col_index = jnp.arange(NG2, dtype=jnp.int32)
    col_cos, col_sin = twiddle(col_index, col_index, NG2)
    col_table = jnp.concatenate([col_cos, col_sin], axis=1)
    position = jnp.arange(NG1, dtype=jnp.int32)
    forward_cos, forward_sin = twiddle(position, position, NG1)
    row_forward = jnp.concatenate([forward_cos, forward_sin], axis=0)
    inverse_cos, inverse_sin = twiddle(position, position, NG1)
    row_inverse = jnp.concatenate([inverse_cos, inverse_sin], axis=0)

    def apply_operator(source):
        rounded = source.astype(jnp.bfloat16)
        near_part = near_term(rounded, near_blocks, bloch_angle)
        recip_part = recip_term(rounded, matrix, recip_kernel, col_table, row_forward, row_inverse)
        return 0.5 * source + near_part + recip_part

    first_image = apply_operator(source_probes)
    second_image = apply_operator(first_image)
    return (first_image, second_image)


def solution(mesh):
    return jax.shard_map(
        local,
        mesh=mesh,
        in_specs=(
            P(None, "groups", ("tile", "sect")),
            P("groups", None, None, ("tile", "sect")),
            P("groups"),
            P(("tile", "sect")),
            P(("tile", "sect")),
            P(None, None, ("tile", "sect")),
            P("groups", ("tile", "sect")),
        ),
        out_specs=(P(None, "groups", ("tile", "sect")), P(None, "groups", ("tile", "sect"))),
        check_vma=False,
    )
```

profile of v0, /device:TPU:0, one launch (start us, length us, event | category | flops | bytes accessed | tf_op | source)
XLA Modules:
  0.0 693.7 jit_solution(1476247298819674760)
XLA Ops:
  3.3 62.7 %add_convert_fusion.1 = bf16[512,17920]{1,0:T(8,128)(2,1)S(1)} fusion(f32[512]{0:T(512)S(1)} %bitcast.479, s32[512]{0:T(512)S(1)} %get-tuple-element.29, f32[512]{0:T(512)S(1)} %bitcast.481, s32[512]{0:T(512)S(1)} %get-tuple-element.32, f32[512]{0:T(512)S(1)} %bitcast.453, s32[512]{0:T(512)S(1)} %get-tuple-element.35, f32[512]{0:T(512)S(1)} %bitcast.455, ...), kind=kLoop, calls=%fused_computation.1 | loop fusion | flops 440401920 | bytes 18415616 | tf_op jit(solution)/shard_map/convert_element_type | solution.py:57
  66.0 6.3 copy-done
  72.3 4.6 convolution_bitcast_fusion
  92.5 7.7 %fusion.217 = f32[32,2,16,2,512]{4,2,3,1,0:T(8,128)S(1)} fusion(f32[32,2,16,512,1]{3,2,4,1,0:T(8,128)S(1)} %bitcast.426, f32[2,512,512,1,1]{2,1,0,4,3:T(8,128)S(1)} %bitcast.413), kind=kOutput, calls=%fused_computation.367 | convolution fusion | flops 6442450944 | bytes 8388608 | tf_op jit(solution)/shard_map/dot_general | solution.py:111
  101.2 7.7 %copy.62 = f32[32,32,512]{1,0,2:T(8,128)} copy(f32[32,32,512]{2,1,0:T(8,128)S(1)} %bitcast.431) | data formatting | bytes 4194304 | tf_op jit(solution)/shard_map/reshape | solution.py:115
  108.8 8.7 %reshape.811 = f32[16,1,32768]{2,1,0:T(1,128)} reshape(f32[512,32,32]{2,1,0:T(8,128)} %bitcast.417) | data formatting | bytes 4194304
  117.6 4.4 all-to-all-start
  140.8 32.8 %all-to-all-done = f32[16,1,32768]{2,1,0:T(1,128)} async-done(((f32[16,1,32768]{2,1,0:T(1,128)}), f32[16,1,32768]{2,1,0:T(1,128)}, u32[]{:S(2)}, u32[]{:S(2)}) %all-to-all-start) | async-done | bytes 2097184 | tf_op jit(solution)/shard_map/all_to_all | solution.py:116
  174.1 8.6 %reduce = f32[16,32768]{1,0:T(8,128)} reduce(f32[16,1,32768]{2,1,0:T(1,128)} %all-to-all-done, f32[]{:T(128)} %broadcast.850), dimensions={1}, to_apply=%all_to_all.44.reduce_sub_computation | reduce | bytes 4194308 | tf_op jit(solution)/shard_map/all_to_all | solution.py:116
  182.7 6.1 reshape.812
  188.7 10.2 %copy.64 = f32[16,32,32,32]{3,2,1,0:T(8,128)} copy(f32[16,32,32,32]{2,1,3,0:T(8,128)} %bitcast.419) | data formatting | bytes 4194304 | tf_op jit(solution)/shard_map/all_to_all | solution.py:116
  198.9 7.7 %reshape.773 = f32[512,1024]{1,0:T(8,128)} reshape(f32[16,32,32,32]{3,2,1,0:T(8,128)} %copy.64) | data formatting | bytes 4194304 | tf_op jit(solution)/shard_map/reshape | solution.py:120
  209.7 8.8 %fusion.218 = f32[2,512,2,16,32]{1,4,3,2,0:T(8,128)S(1)} fusion(f32[2,512,512,1,1]{2,1,4,3,0:T(8,128)S(1)} %bitcast.409, f32[2,16,32,512,1]{3,2,1,0,4:T(8,128)} %bitcast.427), kind=kOutput, calls=%fused_computation.368 | convolution fusion | flops 6442450944 | bytes 8388608 | tf_op jit(solution)/shard_map/dot_general | solution.py:118
  219.2 7.5 %fusion.5 = f32[2,512,2,16,32]{1,4,3,2,0:T(8,128)S(1)} fusion(f32[2,512,512,1,1]{2,1,4,3,0:T(8,128)S(1)} %bitcast.410, f32[512,1,16,32]{0,3,2,1:T(8,128)S(1)} %get-tuple-element.5, f32[512,1,16,32]{0,3,2,1:T(8,128)S(1)} %get-tuple-element.4), kind=kOutput, calls=%fused_computation.31 | convolution fusion | flops 6442975232 | bytes 8388608 | tf_op jit(solution)/shard_map/dot_general | solution.py:129
  227.5 7.7 %copy.66 = f32[512,32,32]{2,1,0:T(8,128)} copy(f32[512,32,32]{0,2,1:T(8,128)S(1)} %bitcast.429) | data formatting | bytes 4194304 | tf_op jit(solution)/shard_map/reshape | solution.py:133
  235.2 8.6 %reshape.813 = f32[16,1,32768]{2,1,0:T(1,128)} reshape(f32[512,32,32]{2,1,0:T(8,128)} %copy.66) | data formatting | bytes 4194304
  243.8 4.4 all-to-all-start.1
  268.2 29.5 %all-to-all-done.1 = f32[16,1,32768]{2,1,0:T(1,128)} async-done(((f32[16,1,32768]{2,1,0:T(1,128)}), f32[16,1,32768]{2,1,0:T(1,128)}, u32[]{:S(2)}, u32[]{:S(2)}) %all-to-all-start.1) | async-done | bytes 2097184 | tf_op jit(solution)/shard_map/all_to_all | solution.py:134
  297.6 7.3 %reduce.1 = f32[16,32768]{1,0:T(8,128)S(1)} reduce(f32[16,1,32768]{2,1,0:T(1,128)} %all-to-all-done.1, f32[]{:T(128)} %broadcast.850), dimensions={1}, to_apply=%all_to_all.47.reduce_sub_computation | reduce | bytes 4194308 | tf_op jit(solution)/shard_map/all_to_all | solution.py:134
  304.9 5.1 reshape.814
  310.0 14.3 %copy.104 = f32[16,32,32,32]{3,0,2,1:T(8,128)} copy(f32[16,32,32,32]{3,2,1,0:T(8,128)} %bitcast.420) | data formatting | bytes 4194304 | tf_op jit(solution)/shard_map/all_to_all | solution.py:134
  324.4 7.7 %reshape.802 = f32[32,2,16,512,1]{3,2,1,0,4:T(8,128)} reshape(f32[32,32,16,32]{3,2,1,0:T(8,128)} %bitcast.421) | data formatting | bytes 4194304 | tf_op jit(solution)/shard_map/dot_general | solution.py:135
  332.0 8.8 %fusion.13 = f32[32,2,16,2,512]{4,2,3,1,0:T(8,128)S(1)} fusion(f32[2,512,512,1,1]{2,1,0,4,3:T(8,128)S(1)} %bitcast.414, f32[32,2,16,512,1]{3,2,1,0,4:T(8,128)} %reshape.802), kind=kOutput, calls=%fused_computation.44 | convolution fusion | flops 6442450944 | bytes 8388608 | tf_op jit(solution)/shard_map/dot_general | solution.py:135
  348.0 12.3 %fusion.216 = (bf16[2,16,512]{2,1,0:T(8,128)(2,1)S(1)}, f32[2,16,512]{2,1,0:T(8,128)}) fusion(bf16[2,16,17920]{2,1,0:T(8,128)(2,1)S(1)} %dot_general.213, bf16[512,17920]{1,0:T(8,128)(2,1)} %copy-done, f32[1,16,512]{2,1,0:T(8,128)S(1)} %fusion.180, f32[1,16,512]{2,1,0:T(8,128)S(1)} %fusion.186, f32[2,16,512]{2,1,0:T(8,128)S(1)} %copy-done.14), kind=kOutput, calls=%fused_computation.366 | convolution fusion | flops 587284480 | bytes 19726336 | tf_op jit(solution)/shard_map/dot_general | solution.py:152
  360.4 58.9 %fusion.4 = f32[32,35,512]{2,0,1:T(8,128)S(1)} fusion(bf16[32,512,1]{1,0,2:T(8,128)(2,1)S(1)} %bitcast.445, f32[512]{0:T(512)S(1)} %bitcast.480, s32[512]{0:T(512)S(1)} %copy-done.23, f32[512]{0:T(512)S(1)} %bitcast.482, s32[512]{0:T(512)S(1)} %copy-done.29, f32[512]{0:T(512)S(1)} %bitcast.454, s32[512]{0:T(512)S(1)} %copy-done.35, f32[512]{0:T(512)S(1)} %bitcast.456, ...), kind=kOutput, calls=%fused_computation.23 | convolution fusion | flops 1027604480 | bytes 2463744 | tf_op jit(solution)/shard_map/dot_general | solution.py:103
  419.6 9.4 %collective-permute-done.10 = f32[32,3,512]{2,0,1:T(8,128)S(1)} collective-permute-done((f32[32,3,512]{2,0,1:T(8,128)S(1)}, f32[32,3,512]{2,0,1:T(8,128)S(1)}, u32[]{:S(2)}, u32[]{:S(2)}) %collective-permute-start.10) | collective-permute-done | bytes 196640 | tf_op jit(solution)/shard_map/ppermute | solution.py:34
  429.3 7.2 %fusion.219 = f32[32,2,16,2,512]{4,2,3,1,0:T(8,128)S(1)} fusion(f32[32,2,16,512,1]{3,2,4,1,0:T(8,128)S(1)} %bitcast.425, f32[2,512,512,1,1]{2,1,0,4,3:T(8,128)S(1)} %bitcast.415), kind=kOutput, calls=%fused_computation.369 | convolution fusion | flops 6442450944 | bytes 8388608 | tf_op jit(solution)/shard_map/dot_general | solution.py:111
  437.4 7.7 %copy.74 = f32[32,32,512]{1,0,2:T(8,128)} copy(f32[32,32,512]{2,1,0:T(8,128)S(1)} %bitcast.433) | data formatting | bytes 4194304 | tf_op jit(solution)/shard_map/reshape | solution.py:115
  445.1 8.6 %reshape.815 = f32[16,1,32768]{2,1,0:T(1,128)} reshape(f32[512,32,32]{2,1,0:T(8,128)} %bitcast.418) | data formatting | bytes 4194304
  453.7 4.4 all-to-all-start.2
  462.4 12.7 %collective-permute-done.6 = bf16[32,1,1,512]{3,0,2,1:T(8,128)(2,1)S(1)} collective-permute-done((bf16[32,1,1,512]{3,0,2,1:T(8,128)(2,1)S(1)}, bf16[32,1,1,512]{3,0,2,1:T(8,128)(2,1)S(1)}, u32[]{:S(2)}, u32[]{:S(2)}) %collective-permute-start.6) | collective-permute-done | bytes 32800 | tf_op jit(solution)/shard_map/ppermute | solution.py:23
  477.4 32.3 %all-to-all-done.2 = f32[16,1,32768]{2,1,0:T(1,128)} async-done(((f32[16,1,32768]{2,1,0:T(1,128)}), f32[16,1,32768]{2,1,0:T(1,128)}, u32[]{:S(2)}, u32[]{:S(2)}) %all-to-all-start.2) | async-done | bytes 2097184 | tf_op jit(solution)/shard_map/all_to_all | solution.py:116
  509.6 7.3 %reduce.2 = f32[16,32768]{1,0:T(8,128)S(1)} reduce(f32[16,1,32768]{2,1,0:T(1,128)} %all-to-all-done.2, f32[]{:T(128)} %broadcast.850), dimensions={1}, to_apply=%all_to_all.50.reduce_sub_computation | reduce | bytes 4194308 | tf_op jit(solution)/shard_map/all_to_all | solution.py:116
  516.9 4.7 reshape.816
  521.7 10.2 %copy.76 = f32[16,32,32,32]{3,2,1,0:T(8,128)} copy(f32[16,32,32,32]{2,1,3,0:T(8,128)} %bitcast.422) | data formatting | bytes 4194304 | tf_op jit(solution)/shard_map/all_to_all | solution.py:116
  531.9 7.9 %reshape.778 = f32[512,1024]{1,0:T(8,128)} reshape(f32[16,32,32,32]{3,2,1,0:T(8,128)} %copy.76) | data formatting | bytes 4194304 | tf_op jit(solution)/shard_map/reshape | solution.py:120
  543.1 8.8 %fusion.220 = f32[2,512,2,16,32]{1,4,3,2,0:T(8,128)S(1)} fusion(f32[2,512,512,1,1]{2,1,4,3,0:T(8,128)S(1)} %bitcast.411, f32[2,16,32,512,1]{3,2,1,0,4:T(8,128)} %bitcast.428), kind=kOutput, calls=%fused_computation.370 | convolution fusion | flops 6442450944 | bytes 8388608 | tf_op jit(solution)/shard_map/dot_general | solution.py:118
  552.5 7.5 %fusion.8 = f32[2,512,2,16,32]{1,4,3,2,0:T(8,128)S(1)} fusion(f32[2,512,512,1,1]{2,1,4,3,0:T(8,128)S(1)} %bitcast.412, f32[512,1,16,32]{0,3,2,1:T(8,128)S(1)} %get-tuple-element.3, f32[512,1,16,32]{0,3,2,1:T(8,128)S(1)} %get-tuple-element.2), kind=kOutput, calls=%fused_computation.38 | convolution fusion | flops 6442975232 | bytes 8388608 | tf_op jit(solution)/shard_map/dot_general | solution.py:129
  560.8 7.7 %copy.78 = f32[512,32,32]{2,1,0:T(8,128)} copy(f32[512,32,32]{0,2,1:T(8,128)S(1)} %bitcast.430) | data formatting | bytes 4194304 | tf_op jit(solution)/shard_map/reshape | solution.py:133
  568.5 8.6 %reshape.817 = f32[16,1,32768]{2,1,0:T(1,128)} reshape(f32[512,32,32]{2,1,0:T(8,128)} %copy.78) | data formatting | bytes 4194304
  577.0 4.4 all-to-all-start.3
  601.4 29.5 %all-to-all-done.3 = f32[16,1,32768]{2,1,0:T(1,128)} async-done(((f32[16,1,32768]{2,1,0:T(1,128)}), f32[16,1,32768]{2,1,0:T(1,128)}, u32[]{:S(2)}, u32[]{:S(2)}) %all-to-all-start.3) | async-done | bytes 2097184 | tf_op jit(solution)/shard_map/all_to_all | solution.py:134
  630.9 7.3 %reduce.3 = f32[16,32768]{1,0:T(8,128)S(1)} reduce(f32[16,1,32768]{2,1,0:T(1,128)} %all-to-all-done.3, f32[]{:T(128)} %broadcast.850), dimensions={1}, to_apply=%all_to_all.53.reduce_sub_computation | reduce | bytes 4194308 | tf_op jit(solution)/shard_map/all_to_all | solution.py:134
  638.2 4.9 reshape.818
  643.1 14.3 %copy.103 = f32[16,32,32,32]{3,0,2,1:T(8,128)} copy(f32[16,32,32,32]{3,2,1,0:T(8,128)} %bitcast.423) | data formatting | bytes 4194304 | tf_op jit(solution)/shard_map/all_to_all | solution.py:134
  657.4 7.7 %reshape.808 = f32[32,2,16,512,1]{3,2,1,0,4:T(8,128)} reshape(f32[32,32,16,32]{3,2,1,0:T(8,128)} %bitcast.424) | data formatting | bytes 4194304 | tf_op jit(solution)/shard_map/dot_general | solution.py:135
  665.2 8.8 %fusion.11 = f32[32,2,16,2,512]{4,2,3,1,0:T(8,128)S(1)} fusion(f32[2,512,512,1,1]{2,1,0,4,3:T(8,128)S(1)} %bitcast.416, f32[32,2,16,512,1]{3,2,1,0,4:T(8,128)} %reshape.808), kind=kOutput, calls=%fused_computation.42 | convolution fusion | flops 6442450944 | bytes 8388608 | tf_op jit(solution)/shard_map/dot_general | solution.py:135
  681.0 12.3 %fusion.162 = f32[2,16,512]{2,1,0:T(8,128)} fusion(f32[1,16,512]{2,1,0:T(8,128)S(1)} %fusion.168, f32[1,16,512]{2,1,0:T(8,128)S(1)} %fusion.174, f32[2,16,512]{2,1,0:T(8,128)S(1)} %copy-done.13, bf16[2,16,17920]{2,1,0:T(8,128)(2,1)S(1)} %dot_general.244, bf16[512,17920]{1,0:T(8,128)(2,1)} %copy-done), kind=kOutput, calls=%fused_computation.225 | convolution fusion | flops 587268096 | bytes 19693568 | tf_op jit(solution)/shard_map/dot_general | solution.py:152
  (212 shorter events, 105.2 us)
Async XLA Ops:
  3.1 73.8 %copy-start.16 = (s32[512]{0:T(512)}, s32[512]{0:T(512)S(1)}, u32[]{:S(2)}) copy-start(s32[512]{0:T(512)S(1)} %get-tuple-element.26) | copy-start | bytes 6148
  3.1 73.8 %copy-start.18 = (s32[512]{0:T(512)}, s32[512]{0:T(512)S(1)}, u32[]{:S(2)}) copy-start(s32[512]{0:T(512)S(1)} %get-tuple-element.27) | copy-start | bytes 6148
  3.1 73.8 %copy-start.20 = (s32[512]{0:T(512)}, s32[512]{0:T(512)S(1)}, u32[]{:S(2)}) copy-start(s32[512]{0:T(512)S(1)} %get-tuple-element.28) | copy-start | bytes 6148
  3.1 73.8 %copy-start.22 = (s32[512]{0:T(512)}, s32[512]{0:T(512)S(1)}, u32[]{:S(2)}) copy-start(s32[512]{0:T(512)S(1)} %get-tuple-element.29) | copy-start | bytes 6148
  3.2 73.8 %copy-start.24 = (s32[512]{0:T(512)}, s32[512]{0:T(512)S(1)}, u32[]{:S(2)}) copy-start(s32[512]{0:T(512)S(1)} %get-tuple-element.30) | copy-start | bytes 6148
  3.2 73.8 %copy-start.26 = (s32[512]{0:T(512)}, s32[512]{0:T(512)S(1)}, u32[]{:S(2)}) copy-start(s32[512]{0:T(512)S(1)} %get-tuple-element.31) | copy-start | bytes 6148
  3.2 73.8 %copy-start.28 = (s32[512]{0:T(512)}, s32[512]{0:T(512)S(1)}, u32[]{:S(2)}) copy-start(s32[512]{0:T(512)S(1)} %get-tuple-element.32) | copy-start | bytes 6148
  3.2 73.8 %copy-start.30 = (s32[512]{0:T(512)}, s32[512]{0:T(512)S(1)}, u32[]{:S(2)}) copy-start(s32[512]{0:T(512)S(1)} %get-tuple-element.33) | copy-start | bytes 6148
  3.2 73.8 %copy-start.32 = (s32[512]{0:T(512)}, s32[512]{0:T(512)S(1)}, u32[]{:S(2)}) copy-start(s32[512]{0:T(512)S(1)} %get-tuple-element.34) | copy-start | bytes 6148
  3.2 73.8 %copy-start.34 = (s32[512]{0:T(512)}, s32[512]{0:T(512)S(1)}, u32[]{:S(2)}) copy-start(s32[512]{0:T(512)S(1)} %get-tuple-element.35) | copy-start | bytes 6148
  3.2 73.8 %copy-start.36 = (s32[512]{0:T(512)}, s32[512]{0:T(512)S(1)}, u32[]{:S(2)}) copy-start(s32[512]{0:T(512)S(1)} %get-tuple-element.36) | copy-start | bytes 6148
  3.2 73.8 %copy-start.38 = (s32[512]{0:T(512)}, s32[512]{0:T(512)S(1)}, u32[]{:S(2)}) copy-start(s32[512]{0:T(512)S(1)} %get-tuple-element.37) | copy-start | bytes 6148
  3.2 73.8 %copy-start.40 = (s32[512]{0:T(512)}, s32[512]{0:T(512)S(1)}, u32[]{:S(2)}) copy-start(s32[512]{0:T(512)S(1)} %get-tuple-element.38) | copy-start | bytes 6148
  3.2 73.8 %copy-start.42 = (s32[512]{0:T(512)}, s32[512]{0:T(512)S(1)}, u32[]{:S(2)}) copy-start(s32[512]{0:T(512)S(1)} %get-tuple-element.39) | copy-start | bytes 6148
  3.3 73.8 %copy-start.44 = (s32[512]{0:T(512)}, s32[512]{0:T(512)S(1)}, u32[]{:S(2)}) copy-start(s32[512]{0:T(512)S(1)} %get-tuple-element.40) | copy-start | bytes 6148
  3.3 73.8 %copy-start.46 = (s32[512]{0:T(512)}, s32[512]{0:T(512)S(1)}, u32[]{:S(2)}) copy-start(s32[512]{0:T(512)S(1)} %get-tuple-element.41) | copy-start | bytes 6148
  79.0 11.7 %collective-permute-start.4 = (f32[32,3,512]{2,1,0:T(4,128)S(1)}, f32[32,3,512]{2,1,0:T(4,128)S(1)}, u32[]{:S(2)}, u32[]{:S(2)}) collective-permute-start(f32[32,3,512]{2,1,0:T(4,128)S(1)} %slice.723), channel_id=1, source_target_pairs={{0,1},{1,2},{2,3},{3,4},{4,5},{5,6},{6,7},{7,8},{8,9},{9,10},{10,1... | collective-permute-start | bytes 589832 | tf_op jit(solution)/shard_map/ppermute | solution.py:34
  86.9 13.4 %copy-start.3 = (f32[512,1024]{0,1:T(8,128)}, f32[512,1024]{0,1:T(8,128)S(1)}, u32[]{:S(2)}) copy-start(f32[512,1024]{0,1:T(8,128)S(1)} %pad_maximum_fusion.1) | copy-start | bytes 6291460
  108.8 15.0 %copy-start.8 = (f32[512,512]{0,1:T(8,128)S(1)}, f32[512,512]{0,1:T(8,128)}, u32[]{:S(2)}) copy-start(f32[512,512]{0,1:T(8,128)} %copy-done.7) | copy-start | bytes 3145732
  108.8 15.0 %copy-start.10 = (f32[512,512]{0,1:T(8,128)S(1)}, f32[512,512]{0,1:T(8,128)}, u32[]{:S(2)}) copy-start(f32[512,512]{0,1:T(8,128)} %copy-done.9) | copy-start | bytes 3145732
  108.8 16.6 %copy-start.15 = (f32[512,32]{0,1:T(8,128)S(1)}, f32[512,32]{0,1:T(8,128)}, u32[]{:S(2)}) copy-start(f32[512,32]{0,1:T(8,128)} %param.13) | copy-start | bytes 196612
  108.8 19.1 %copy-start.48 = (f32[2]{0:T(128)S(1)}, f32[2]{0:T(128)}, u32[]{:S(2)}) copy-start(f32[2]{0:T(128)} %param.9) | copy-start | bytes 28
  117.6 56.0 %all-to-all-start = ((f32[16,1,32768]{2,1,0:T(1,128)}), f32[16,1,32768]{2,1,0:T(1,128)}, u32[]{:S(2)}, u32[]{:S(2)}) async-start(f32[16,1,32768]{2,1,0:T(1,128)} %reshape.811), calls=%async_computation | async-start | bytes 4194304 | tf_op jit(solution)/shard_map/all_to_all | solution.py:116
  122.0 16.7 %collective-permute-start = (bf16[32,1,1,512]{3,0,2,1:T(8,128)(2,1)S(1)}, bf16[32,1,1,512]{3,0,2,1:T(8,128)(2,1)S(1)}, u32[]{:S(2)}, u32[]{:S(2)}) collective-permute-start(bf16[32,1,1,512]{3,0,2,1:T(8,128)(2,1)S(1)} %bitcast.440), channel_id=1, source_target_pairs={{0,4},{4,8},{8,12},{12,0},{1,5},{5,9},{9,13},{13,1},{2,6},{6,10},{... | collective-permute-start | bytes 98312 | tf_op jit(solution)/shard_map/ppermute | solution.py:23
  122.3 16.4 %collective-permute-start.1 = (bf16[32,1,1,512]{3,0,2,1:T(8,128)(2,1)S(1)}, bf16[32,1,1,512]{3,0,2,1:T(8,128)(2,1)S(1)}, u32[]{:S(2)}, u32[]{:S(2)}) collective-permute-start(bf16[32,1,1,512]{3,0,2,1:T(8,128)(2,1)S(1)} %bitcast.441), channel_id=1, source_target_pairs={{4,0},{8,4},{12,8},{0,12},{5,1},{9,5},{13,9},{1,13},{6,2},{10,6},{... | collective-permute-start | bytes 98312 | tf_op jit(solution)/shard_map/ppermute | solution.py:25
  125.4 93.1 %copy-start.11 = (f32[512,32]{0,1:T(8,128)}, f32[512,32]{0,1:T(8,128)S(1)}, u32[]{:S(2)}) copy-start(f32[512,32]{0,1:T(8,128)S(1)} %broadcast_multiply_fusion) | copy-start | bytes 196612
  134.3 84.9 %copy-start.1 = (f32[1024,512]{1,0:T(8,128)}, f32[1024,512]{1,0:T(8,128)S(1)}, u32[]{:S(2)}) copy-start(f32[1024,512]{1,0:T(8,128)S(1)} %copy.57) | copy-start | bytes 6291460
  138.7 114.5 %collective-permute-start.3 = (bf16[32,3,1,512]{3,0,2,1:T(8,128)(2,1)S(1)}, bf16[32,3,1,512]{3,0,2,1:T(8,128)(2,1)S(1)}, u32[]{:S(2)}, u32[]{:S(2)}) collective-permute-start(bf16[32,3,1,512]{3,0,2,1:T(8,128)(2,1)S(1)} %pad_maximum_fusion.9), channel_id=1, source_target_pairs={{1,0},{2,1},{3,2},{0,3},{5,4},{6,5},{7,6},{4,7},{9,8},{10,9},{11,1... | collective-permute-start | bytes 294920 | tf_op jit(solution)/shard_map/ppermute | solution.py:25
  139.5 116.1 %collective-permute-start.2 = (bf16[32,3,1,512]{3,0,2,1:T(8,128)(2,1)S(1)}, bf16[32,3,1,512]{3,0,2,1:T(8,128)(2,1)S(1)}, u32[]{:S(2)}, u32[]{:S(2)}) collective-permute-start(bf16[32,3,1,512]{3,0,2,1:T(8,128)(2,1)S(1)} %pad_maximum_fusion.9), channel_id=1, source_target_pairs={{0,1},{1,2},{2,3},{3,0},{4,5},{5,6},{6,7},{7,4},{8,9},{9,10},{10,1... | collective-permute-start | bytes 294920 | tf_op jit(solution)/shard_map/ppermute | solution.py:23
  243.8 53.9 %all-to-all-start.1 = ((f32[16,1,32768]{2,1,0:T(1,128)}), f32[16,1,32768]{2,1,0:T(1,128)}, u32[]{:S(2)}, u32[]{:S(2)}) async-start(f32[16,1,32768]{2,1,0:T(1,128)} %reshape.813), calls=%async_computation.1 | async-start | bytes 4194304 | tf_op jit(solution)/shard_map/all_to_all | solution.py:134
  342.0 5.1 collective-permute-start.5
  347.9 12.4 %copy-start.17 = (s32[512]{0:T(512)S(1)}, s32[512]{0:T(512)}, u32[]{:S(2)}) copy-start(s32[512]{0:T(512)} %copy-done.16) | copy-start | bytes 6148
  347.9 12.4 %copy-start.19 = (s32[512]{0:T(512)S(1)}, s32[512]{0:T(512)}, u32[]{:S(2)}) copy-start(s32[512]{0:T(512)} %copy-done.18) | copy-start | bytes 6148
  347.9 12.4 %copy-start.21 = (s32[512]{0:T(512)S(1)}, s32[512]{0:T(512)}, u32[]{:S(2)}) copy-start(s32[512]{0:T(512)} %copy-done.20) | copy-start | bytes 6148
  347.9 12.4 %copy-start.23 = (s32[512]{0:T(512)S(1)}, s32[512]{0:T(512)}, u32[]{:S(2)}) copy-start(s32[512]{0:T(512)} %copy-done.22) | copy-start | bytes 6148
  347.9 12.4 %copy-start.25 = (s32[512]{0:T(512)S(1)}, s32[512]{0:T(512)}, u32[]{:S(2)}) copy-start(s32[512]{0:T(512)} %copy-done.24) | copy-start | bytes 6148
  347.9 12.4 %copy-start.27 = (s32[512]{0:T(512)S(1)}, s32[512]{0:T(512)}, u32[]{:S(2)}) copy-start(s32[512]{0:T(512)} %copy-done.26) | copy-start | bytes 6148
  347.9 12.4 %copy-start.29 = (s32[512]{0:T(512)S(1)}, s32[512]{0:T(512)}, u32[]{:S(2)}) copy-start(s32[512]{0:T(512)} %copy-done.28) | copy-start | bytes 6148
  347.9 12.4 %copy-start.31 = (s32[512]{0:T(512)S(1)}, s32[512]{0:T(512)}, u32[]{:S(2)}) copy-start(s32[512]{0:T(512)} %copy-done.30) | copy-start | bytes 6148
  347.9 12.4 %copy-start.33 = (s32[512]{0:T(512)S(1)}, s32[512]{0:T(512)}, u32[]{:S(2)}) copy-start(s32[512]{0:T(512)} %copy-done.32) | copy-start | bytes 6148
  419.3 9.6 %collective-permute-start.10 = (f32[32,3,512]{2,0,1:T(8,128)S(1)}, f32[32,3,512]{2,0,1:T(8,128)S(1)}, u32[]{:S(2)}, u32[]{:S(2)}) collective-permute-start(f32[32,3,512]{2,0,1:T(8,128)S(1)} %slice.785), channel_id=1, source_target_pairs={{0,1},{1,2},{2,3},{3,4},{4,5},{5,6},{6,7},{7,8},{8,9},{9,10},{10,1... | collective-permute-start | bytes 589832 | tf_op jit(solution)/shard_map/ppermute | solution.py:34
  453.7 56.0 %all-to-all-start.2 = ((f32[16,1,32768]{2,1,0:T(1,128)}), f32[16,1,32768]{2,1,0:T(1,128)}, u32[]{:S(2)}, u32[]{:S(2)}) async-start(f32[16,1,32768]{2,1,0:T(1,128)} %reshape.815), calls=%async_computation.2 | async-start | bytes 4194304 | tf_op jit(solution)/shard_map/all_to_all | solution.py:116
  458.1 17.0 %collective-permute-start.6 = (bf16[32,1,1,512]{3,0,2,1:T(8,128)(2,1)S(1)}, bf16[32,1,1,512]{3,0,2,1:T(8,128)(2,1)S(1)}, u32[]{:S(2)}, u32[]{:S(2)}) collective-permute-start(bf16[32,1,1,512]{3,0,2,1:T(8,128)(2,1)S(1)} %bitcast.446), channel_id=1, source_target_pairs={{0,4},{4,8},{8,12},{12,0},{1,5},{5,9},{9,13},{13,1},{2,6},{6,10},{... | collective-permute-start | bytes 98312 | tf_op jit(solution)/shard_map/ppermute | solution.py:23
  458.4 16.7 %collective-permute-start.7 = (bf16[32,1,1,512]{3,0,2,1:T(8,128)(2,1)S(1)}, bf16[32,1,1,512]{3,0,2,1:T(8,128)(2,1)S(1)}, u32[]{:S(2)}, u32[]{:S(2)}) collective-permute-start(bf16[32,1,1,512]{3,0,2,1:T(8,128)(2,1)S(1)} %bitcast.447), channel_id=1, source_target_pairs={{4,0},{8,4},{12,8},{0,12},{5,1},{9,5},{13,9},{1,13},{6,2},{10,6},{... | collective-permute-start | bytes 98312 | tf_op jit(solution)/shard_map/ppermute | solution.py:25
  475.1 111.3 %collective-permute-start.9 = (bf16[32,3,1,512]{3,0,2,1:T(8,128)(2,1)S(1)}, bf16[32,3,1,512]{3,0,2,1:T(8,128)(2,1)S(1)}, u32[]{:S(2)}, u32[]{:S(2)}) collective-permute-start(bf16[32,3,1,512]{3,0,2,1:T(8,128)(2,1)S(1)} %pad_maximum_fusion.10), channel_id=1, source_target_pairs={{1,0},{2,1},{3,2},{0,3},{5,4},{6,5},{7,6},{4,7},{9,8},{10,9},{11,1... | collective-permute-start | bytes 294920 | tf_op jit(solution)/shard_map/ppermute | solution.py:25
  475.7 113.2 %collective-permute-start.8 = (bf16[32,3,1,512]{3,0,2,1:T(8,128)(2,1)S(1)}, bf16[32,3,1,512]{3,0,2,1:T(8,128)(2,1)S(1)}, u32[]{:S(2)}, u32[]{:S(2)}) collective-permute-start(bf16[32,3,1,512]{3,0,2,1:T(8,128)(2,1)S(1)} %pad_maximum_fusion.10), channel_id=1, source_target_pairs={{0,1},{1,2},{2,3},{3,0},{4,5},{5,6},{6,7},{7,4},{8,9},{9,10},{10,1... | collective-permute-start | bytes 294920 | tf_op jit(solution)/shard_map/ppermute | solution.py:23
  577.0 53.9 %all-to-all-start.3 = ((f32[16,1,32768]{2,1,0:T(1,128)}), f32[16,1,32768]{2,1,0:T(1,128)}, u32[]{:S(2)}, u32[]{:S(2)}) async-start(f32[16,1,32768]{2,1,0:T(1,128)} %reshape.817), calls=%async_computation.3 | async-start | bytes 4194304 | tf_op jit(solution)/shard_map/all_to_all | solution.py:134
  675.1 5.1 collective-permute-start.11
  (17 other events, 167.9 us)
where the time goes:
time: 701 us; the launch traced here: 694 us
  matrix products  198 us (28%)
  local copies, waits for them, and re-layouts  188 us (27%)
  waiting for transfers between devices  161 us (23%)
  other arithmetic  108 us (15%)
  starting transfers between devices  32.4 us (5%)
    all_to_all x2, waiting for transfers between devices, recip_term(): lax.all_to_all(spectrum, ('tile', 'sect'), split_axis=2, concat_axis=0, t...  65 us
    dot_general x2, matrix products, recip_term(): spread = jnp.dot(flat, matrix, preferred_element_type=jnp.float32)  63.5 us
    convert_element_type x1, other arithmetic, spread_matrix(): return matrix.astype(jnp.bfloat16)  62.7 us
    unnamed x106, local copies, waits for them, and re-layouts  61.7 us
    all_to_all x2, waiting for transfers between devices, recip_term(): lax.all_to_all(spatial, ('tile', 'sect'), split_axis=0, concat_axis=2, ti...  58.9 us
    all_to_all x2, local copies, waits for them, and re-layouts, recip_term(): lax.all_to_all(spatial, ('tile', 'sect'), split_axis=0, concat_axis=2, ti...  28.7 us
    dot_general x2, matrix products, recip_term(): lax.dot_general(whole, matrix, (((1,), (1,)), ((), ())), preferred_elemen...  24.5 us
    dot_general x18, matrix products, near_term(): jnp.dot(piece, near_blocks[0, index], preferred_element_type=jnp.float32)  22.3 us
  transfers between devices with their start and end apart: 16, of which 10 were waited for; matrix products, arithmetic and copies ran while one was open for 28% of the time, Pallas kernels for 0%

commit v1 on v0

v1 whole, which is shorter than its diff:
```python
import functools

import jax
import jax.numpy as jnp
import ml_dtypes
import numpy as np
from jax import lax
from jax.experimental import pallas as pl
from jax.experimental.pallas import tpu as pltpu
from jax.sharding import PartitionSpec as P

STENCIL = 4
RADIX = 4
F32 = jnp.float32
BF = jnp.bfloat16
AXES = ("tile", "sect")


def split_host(x):
    hi=x.astype(ml_dtypes.bfloat16); lo=(x-hi.astype(np.float64)).astype(ml_dtypes.bfloat16)
    return hi,lo

def tables(n):
    q=n//RADIX
    k=np.arange(q)
    ang=2*np.pi*((k[:,None]*k[None,:])%q)/q
    c,s=np.cos(ang),np.sin(ang)
    A=np.block([[c,-s],[s,c]]); B=np.block([[c,s],[-s,c]])
    ah,al=split_host(A); bh,bl=split_host(B)
    mats=np.stack([ah,al,bh,bl])
    r=np.arange(RADIX)
    t=2*np.pi*(r[:,None]*k[None,:])/n
    tw=np.stack([np.cos(t),np.sin(t)],1).astype(np.float32)
    return mats,tw

def dot(a,b): return jnp.dot(a,b,preferred_element_type=F32)
def split(x):
    hi=x.astype(BF); return hi,(x-hi.astype(F32)).astype(BF)
def rdot(x,mh,ml):
    h,l=split(x)
    return dot(h,mh)+dot(l,mh)+dot(h,ml)
def ldot(mh,ml,x):
    h,l=split(x)
    return dot(mh,h)+dot(mh,l)+dot(ml,h)

def butterfly(parts, sign):
    (ar,ai),(br,bi),(cr,ci),(dr,di)=parts
    s0r,s0i=ar+cr,ai+ci; s1r,s1i=ar-cr,ai-ci
    t0r,t0i=br+dr,bi+di; t1r,t1i=br-dr,bi-di
    if sign>0: u=(-t1i,t1r)
    else: u=(t1i,-t1r)
    return [(s0r+t0r,s0i+t0i),(s1r+u[0],s1i+u[1]),(s0r-t0r,s0i-t0i),(s1r-u[0],s1i-u[1])]

def layout(rows_dev):
    span=rows_dev+STENCIL-1
    off=max((b*rows_dev)%8 for b in range(8))
    win=-(-(span+off)//8)*8
    return win

def recip_kernel_body(first, nb, rows_dev, n1, n2, pb, win, *refs):
    if first:
        meta,add,kern,mats,twl,tws,out,G,Z,F0,F1=refs
    else:
        meta,vin,kern,mats,twl,tws,out,G,Z,F0,F1=refs
    q2=n2//RADIX; q1=n1//RADIX
    w=2*q2
    def panels(b):
        m=meta[b].astype(F32)
        st=m[2:2+STENCIL*STENCIL]
        lrow=m[18:19]; colq=m[19:20]; colr=m[20:21]
        base=(b*rows_dev)//8*8
        if isinstance(base,int): base=base
        lrow=lrow+(b*rows_dev-base).astype(F32) if rows_dev%8 else lrow
        iq=lax.broadcasted_iota(jnp.int32,(q2,pb),0).astype(F32)
        cols=[jnp.where(colr==float(r),colq,-1.0) for r in range(RADIX)]
        hits=[iq==c for c in cols]
        ir=lax.broadcasted_iota(jnp.int32,(win,pb),0).astype(F32)
        rel=ir-lrow
        rm=[rel==float(a) for a in range(STENCIL)]
        ls=[]
        for b_ in range(STENCIL):
            l=jnp.where(rm[0],st[b_:b_+1],0.0)
            for a in range(1,STENCIL):
                l=jnp.where(rm[a],st[a*STENCIL+b_:a*STENCIL+b_+1],l)
            ls.append(l)
        L=jnp.concatenate(ls,0)
        return m,base,hits,L
    G[...]=jnp.zeros_like(G)
    def spread(b,_):
        m,base,hits,L=panels(b)
        if first:
            vr,vi=m[0:1],m[1:2]
        else:
            v=vin[b].astype(BF).astype(F32); vr,vi=v[0:1],v[1:2]
        ev=[]
        for r in range(RADIX):
            ev.append(jnp.where(hits[r],vr,0.0)); ev.append(jnp.where(hits[r],vi,0.0))
        ev=jnp.concatenate(ev,0).astype(BF)
        S=lax.dot_general(L.astype(BF),ev,(((1,),(1,)),((),())),preferred_element_type=F32)
        start=pl.multiple_of(base,8)
        for r in range(RADIX):
            for c in range(2):
                acc=None
                for b_ in range(STENCIL):
                    rr=(r-b_)%RADIX
                    x=S[b_*win:(b_+1)*win, (rr*2+c)*q2:(rr*2+c+1)*q2]
                    if r-b_<0: x=pltpu.roll(x,1,1)
                    acc=x if acc is None else acc+x
                sl=slice((r*2+c)*q2,(r*2+c+1)*q2)
                G[pl.ds(start,win),sl]=G[pl.ds(start,win),sl]+acc
        return 0
    lax.fori_loop(0,nb,spread,0)
    extra=G.shape[0]-n1
    G[0:extra,:]=G[0:extra,:]+G[n1:n1+extra,:]
    Ah,Al,Bh,Bl=(mats.at[k] for k in range(4))
    ch=128
    def s1(j,_):
        rows=pl.ds(pl.multiple_of(j*ch,ch),ch)
        parts=[]
        for r in range(RADIX):
            y=rdot(G[rows,r*w:(r+1)*w],Ah[...],Al[...])
            re,im=y[:,:q2],y[:,q2:]
            if r:
                c=twl[r,0:1]; s=twl[r,1:2]
                re,im=re*c+im*s, im*c-re*s
            parts.append((re,im))
        for m_,(re,im) in enumerate(butterfly(parts,-1)):
            Z[2*m_,rows,:]=re; Z[2*m_+1,rows,:]=im
        return 0
    lax.fori_loop(0,n1//ch,s1,0)
    def tile2(x): return jnp.concatenate([x,x],1)
    for pair in range(RADIX//2):
        lo=pair*4
        def get(r):
            rr=pl.ds(r,q1,stride=RADIX)
            re=jnp.concatenate([Z[lo,rr,:],Z[lo+2,rr,:]],1)
            im=jnp.concatenate([Z[lo+1,rr,:],Z[lo+3,rr,:]],1)
            return re,im
        parts=[]
        for r in range(RADIX):
            re,im=get(r)
            y=ldot(Bh[...],Bl[...],jnp.concatenate([re,im],0))
            re,im=y[:q1],y[q1:]
            if r:
                c=tile2(tws[r,0]); s=tile2(tws[r,1])
                re,im=re*c+im*s, im*c-re*s
            parts.append((re,im))
        sp=[]
        for m_,(re,im) in enumerate(butterfly(parts,-1)):
            kk=kern[m_*q1:(m_+1)*q1,pair*2*q2:(pair+1)*2*q2]
            sp.append((re*kk,im*kk))
        for r,(re,im) in enumerate(butterfly(sp,1)):
            if r:
                c=tile2(tws[r,0]); s=tile2(tws[r,1])
                re,im=re*c-im*s, im*c+re*s
            y=ldot(Ah[...],Al[...],jnp.concatenate([re,im],0))
            rr=pl.ds(r,q1,stride=RADIX)
            Z[lo,rr,:]=y[:q1,:q2]; Z[lo+2,rr,:]=y[:q1,q2:]
            Z[lo+1,rr,:]=y[q1:,:q2]; Z[lo+3,rr,:]=y[q1:,q2:]
    def s3(j,_):
        rows=pl.ds(pl.multiple_of(j*ch,ch),ch)
        parts=[(Z[2*m_,rows,:],Z[2*m_+1,rows,:]) for m_ in range(RADIX)]
        for r,(re,im) in enumerate(butterfly(parts,1)):
            if r:
                c=twl[r,0:1]; s=twl[r,1:2]
                re,im=re*c-im*s, im*c+re*s
            y=rdot(jnp.concatenate([re,im],1),Bh[...],Bl[...])
            F0[rows,r*w:(r+1)*w]=y
            if r<STENCIL-1:
                F1[rows,r*w:r*w+q2]=pltpu.roll(y[:,:q2],q2-1,1)
                F1[rows,r*w+q2:(r+1)*w]=pltpu.roll(y[:,q2:],q2-1,1)
        return 0
    lax.fori_loop(0,n1//ch,s3,0)
    F0[n1:n1+extra,:]=F0[0:extra,:]
    F1[n1:n1+extra,:]=F1[0:extra,:]
    def gather(b,_):
        m,base,hits,L=panels(b)
        E=jnp.concatenate([jnp.where(h,1.0,0.0) for h in hits],0).astype(BF)
        start=pl.multiple_of(base,8)
        pieces=[]
        for b_ in range(STENCIL):
            for c in range(2):
                blk=[]
                for r in range(RADIX):
                    rr=r+b_
                    src=F0 if rr<RADIX else F1
                    rr%=RADIX
                    blk.append(src[pl.ds(start,win),(rr*2+c)*q2:(rr*2+c+1)*q2])
                pieces.append(jnp.concatenate(blk,1))
        X=jnp.concatenate(pieces,0).astype(BF)
        Pm=dot(X,E)
        for c in range(2):
            acc=None
            for b_ in range(STENCIL):
                x=Pm[(b_*2+c)*win:(b_*2+c+1)*win]*L[b_*win:(b_+1)*win]
                acc=x if acc is None else acc+x
            tot=jnp.sum(acc,0,keepdims=True)
            if first: tot=tot+add[b,c:c+1]
            out[b,c:c+1]=tot
        return 0
    lax.fori_loop(0,nb,gather,0)

def recip(first, meta, other, kern, rows_dev, n1, n2):
    nb=meta.shape[0]; pb=meta.shape[2]
    win=layout(rows_dev)
    mats,tw=tables(n2)
    q=n1//RADIX
    tws=np.ascontiguousarray(np.broadcast_to(tw[:,:,:,None],(RADIX,2,q,n2//RADIX)))
    extra=win
    body=functools.partial(recip_kernel_body,first,nb,rows_dev,n1,n2,pb,win)
    ops=[meta,other]
    return pl.pallas_call(body,
        out_shape=jax.ShapeDtypeStruct((nb,2,pb),F32),
        in_specs=[pl.BlockSpec(memory_space=pltpu.VMEM)]*6,
        out_specs=pl.BlockSpec(memory_space=pltpu.VMEM),
        scratch_shapes=[pltpu.VMEM((n1+extra,2*n2),F32),pltpu.VMEM((2*RADIX,n1,n2//RADIX),F32),pltpu.VMEM((n1+extra,2*n2),F32),pltpu.VMEM((n1+extra,2*n2),F32)],
        compiler_params=pltpu.CompilerParams(vmem_limit_bytes=50*1024*1024),
        cost_estimate=pl.CostEstimate(flops=20_000_000_000,bytes_accessed=8_000_000,transcendentals=0),
        name="recip",
    )(meta,other,kern,jnp.asarray(mats),jnp.asarray(tw),jnp.asarray(tws))


def near_kernel(probes, phase, halo, blocks, source, out, acc):
    step = pl.program_id(0)
    x = halo[0]
    with_real = dot(x, blocks[0, 0])
    with_imag = dot(x, blocks[1, 0])
    real = with_real[:probes] - with_imag[probes:]
    imag = with_real[probes:] + with_imag[:probes]
    c = phase[2 * step]
    s = phase[2 * step + 1]

    @pl.when(step == 0)
    def _():
        acc[...] = 0.5 * source[...]

    acc[0] += real * c - imag * s
    acc[1] += real * s + imag * c

    @pl.when(step == pl.num_programs(0) - 1)
    def _():
        out[:, 0, :] = acc[0]
        out[:, 1, :] = acc[1]


def near_apply(halo, near_blocks, phase, source):
    _, probes, panels = source.shape
    count = near_blocks.shape[1]
    depth = near_blocks.shape[2]
    return pl.pallas_call(
        functools.partial(near_kernel, probes),
        grid=(count,),
        out_shape=jax.ShapeDtypeStruct((probes, 2, panels), F32),
        in_specs=[
            pl.BlockSpec(memory_space=pltpu.SMEM),
            pl.BlockSpec((1, 2 * probes, depth), lambda d: (d, 0, 0)),
            pl.BlockSpec((2, 1, depth, panels), lambda d: (0, d, 0, 0)),
            pl.BlockSpec(source.shape, lambda d: (0, 0, 0)),
        ],
        out_specs=pl.BlockSpec((probes, 2, panels), lambda d: (0, 0, 0)),
        scratch_shapes=[pltpu.VMEM(source.shape, F32)],
        compiler_params=pltpu.CompilerParams(vmem_limit_bytes=16 * 1024 * 1024),
        cost_estimate=pl.CostEstimate(
            flops=4 * count * 2 * probes * depth * panels,
            bytes_accessed=2 * near_blocks.size,
            transcendentals=0,
        ),
        name="near",
    )(phase, halo, near_blocks, source)


def shifted(array, axis, by):
    count = lax.axis_size(axis)
    return lax.ppermute(array, axis, [(i, (i + by) % count) for i in range(count)])


def neighbours(block):
    held = block[None]
    for axis in ("sect", "tile"):
        before = shifted(held, axis, 1)
        after = shifted(held, axis, -1)
        held = jnp.stack([before, held, after])
    return held.reshape((9,) + block.shape)


def phases(bloch_angle):
    tile_pos, tile_count = lax.axis_index("tile"), lax.axis_size("tile")
    sect_pos, sect_count = lax.axis_index("sect"), lax.axis_size("sect")
    offsets = jnp.arange(-1, 2, dtype=jnp.int32)
    leaves_tile = (tile_pos + offsets < 0) | (tile_pos + offsets >= tile_count)
    leaves_sect = (sect_pos + offsets < 0) | (sect_pos + offsets >= sect_count)
    angle_tile = jnp.where(leaves_tile, bloch_angle[0] * offsets, 0.0)
    angle_sect = jnp.where(leaves_sect, bloch_angle[1] * offsets, 0.0)
    angle = (angle_tile[:, None] + angle_sect[None, :]).reshape(9)
    return jnp.stack([jnp.cos(angle), jnp.sin(angle)], axis=1).reshape(18)


def gathered(block):
    for axis in ("sect", "tile"):
        count = lax.axis_size(axis)
        place = lax.axis_index(axis)
        reach = 1
        while reach < count:
            other = lax.ppermute(block, axis, [(i, i ^ reach) for i in range(count)])
            upper = (place // reach) % 2 == 1
            block = jnp.where(
                upper, jnp.concatenate([other, block]), jnp.concatenate([block, other])
            )
            reach *= 2
    return block


def exchange(parts):
    return lax.all_to_all(parts, AXES, 0, 0, tiled=True)


def local(source_probes, near_blocks, bloch_angle, grid_row, grid_col, stencil, recip_kernel):
    count = lax.axis_size("tile") * lax.axis_size("sect")
    n1 = recip_kernel.shape[0]
    n2 = recip_kernel.shape[1] * count
    rows_dev = n1 // count
    _, probes, panels = source_probes.shape
    repeat = count // probes

    def to_owners(rows):
        return jnp.repeat(rows, repeat, axis=0) if repeat > 1 else rows

    def to_panels(rows):
        return exchange(rows)[::repeat]

    rounded = source_probes.astype(BF)
    described = jnp.concatenate(
        [
            stencil.reshape(STENCIL * STENCIL, panels),
            (grid_row % rows_dev)[None].astype(BF),
            (grid_col // RADIX)[None].astype(BF),
            (grid_col % RADIX)[None].astype(BF),
            jnp.zeros((3, panels), BF),
        ]
    )
    sent = jnp.concatenate(
        [
            rounded.transpose(1, 0, 2),
            jnp.broadcast_to(described[None], (probes,) + described.shape),
        ],
        axis=1,
    )
    meta = exchange(to_owners(sent))
    kernel_rows = (recip_kernel * (1.0 / (n1 * n2))).T
    kern = gathered(kernel_rows).T
    phase = phases(bloch_angle)

    def near(source):
        flat = source.astype(BF).reshape(2 * probes, panels)
        return near_apply(neighbours(flat), near_blocks, phase, source)

    start = exchange(to_owners(near(source_probes)))
    first_owned = recip(True, meta, start, kern, rows_dev, n1, n2)
    first_image = to_panels(first_owned).transpose(1, 0, 2)
    second_owned = recip(False, meta, first_owned, kern, rows_dev, n1, n2)
    second_image = (near(first_image) + to_panels(second_owned)).transpose(1, 0, 2)
    return (first_image, second_image)


def solution(mesh):
    return jax.shard_map(
        local,
        mesh=mesh,
        in_specs=(
            P(None, "groups", AXES),
            P("groups", None, None, AXES),
            P("groups"),
            P(AXES),
            P(AXES),
            P(None, None, AXES),
            P("groups", AXES),
        ),
        out_specs=(P(None, "groups", AXES), P(None, "groups", AXES)),
        check_vma=False,
    )
```

time: 701 us -> 152 us (0.22)
  matrix products: 198 us -> 0 us
  local copies, waits for them, and re-layouts: 188 us -> 11.6 us
  waiting for transfers between devices: 161 us -> 39.1 us
  other arithmetic: 108 us -> 6.54 us
  Pallas kernels: 0 us -> 54.3 us
  blocking collectives: 0 us -> 11.1 us
    dot_general x48 -> x0, matrix products: 198 us -> none  [the longest x2 63.5 us: recip_term(): spread = jnp.dot(flat, matrix, preferred_element_type=jnp.float32)]
    all_to_all x4 -> x3, waiting for transfers between devices: 124 us -> 5.55 us  [exchange(): return lax.all_to_all(parts, AXES, 0, 0, tiled=True)]
    convert_element_type x5 -> x4, other arithmetic: 64.7 us -> 2.25 us  [the longest x1 0.85 us: local(): rounded = source_probes.astype(BF)]
    pallas_call x0 -> x4, Pallas kernels: none -> 54.3 us  [the longest x2 45.7 us: recip(): pl.pallas_call(body, out_shape=jax.ShapeDtypeStruct((nb, 2, pb), F32), in...]
    unnamed x106 -> x19, local copies, waits for them, and re-layouts: 61.7 us -> 9.85 us
    all_to_all x5 -> x0, local copies, waits for them, and re-layouts: 49.6 us -> none  [the longest x2 28.7 us: recip_term(): lax.all_to_all(spatial, ('tile', 'sect'), split_axis=0, concat_axis=2, ti...]
    reshape x7 -> x2, local copies, waits for them, and re-layouts: 48 us -> 0.09 us  [the longest x1 0.08 us: phases(): return jnp.stack([jnp.cos(angle), jnp.sin(angle)], axis=1).reshape(18)]
    all_to_all x4 -> x0, other arithmetic: 30.4 us -> none  [the longest x2 15.9 us: recip_term(): lax.all_to_all(spectrum, ('tile', 'sect'), split_axis=2, concat_axis=0, t...]
  transfers between devices with their start and end apart: 16 -> 15, of which waited for: 10 -> 5; matrix products, arithmetic and copies ran while one was open for 28% -> 6% of each run, Pallas kernels for 0% -> 21%
where the time goes in v1:
time: 152 us
  Pallas kernels  54.3 us (36%)
  waiting for transfers between devices  39.1 us (26%)
  starting transfers between devices  27.8 us (18%)
  local copies, waits for them, and re-layouts  11.6 us (8%)
  blocking collectives  11.1 us (7%)
  other arithmetic  6.54 us (4%)
    pallas_call x2, Pallas kernels, recip(): pl.pallas_call(body, out_shape=jax.ShapeDtypeStruct((nb, 2, pb), F32), in...  45.7 us
    ppermute x4, waiting for transfers between devices, gathered(): other = lax.ppermute(block, axis, [(i, i ^ reach) for i in range(count)])  31.7 us
    all_to_all x3, starting transfers between devices, exchange(): return lax.all_to_all(parts, AXES, 0, 0, tiled=True)  13.3 us
    ppermute x8, starting transfers between devices, shifted(): lax.ppermute(array, axis, [(i, (i + by) % count) for i in range(count)])  11.4 us
    all_to_all x1, blocking collectives, exchange(): return lax.all_to_all(parts, AXES, 0, 0, tiled=True)  11.1 us
    unnamed x19, local copies, waits for them, and re-layouts  9.85 us
    pallas_call x2, Pallas kernels, near_apply(): pl.pallas_call(functools.partial(near_kernel, probes), grid=(count,), out...  8.62 us
    all_to_all x3, waiting for transfers between devices, exchange(): return lax.all_to_all(parts, AXES, 0, 0, tiled=True)  5.55 us
  transfers between devices with their start and end apart: 15, of which 5 were waited for; matrix products, arithmetic and copies ran while one was open for 6% of the time, Pallas kernels for 21%

profile of v1, /device:TPU:0, one launch (start us, length us, event | category | flops | bytes accessed | tf_op | source)
XLA Modules:
  0.0 151.5 jit_solution(9395086362846435072)
XLA Ops:
  0.6 0.9 convert_element_type.48
  1.5 0.0 copy-start.6
  1.5 3.1 %collective-permute-start = (bf16[1,32,512]{2,1,0:T(8,128)(2,1)S(1)}, bf16[1,32,512]{2,1,0:T(8,128)(2,1)S(1)}, u32[]{:S(2)}, u32[]{:S(2)}) collective-permute-start(bf16[1,32,512]{2,1,0:T(8,128)(2,1)S(1)} %bitcast.38), channel_id=1, source_target_pairs={{0,1},{1,2},{2,3},{3,0},{4,5},{5,6},{6,7},{7,4},{8,9},{9,10},{10,1... | collective-permute-start | bytes 98312 | tf_op jit(solution)/shard_map/ppermute | solution.py:274
  4.6 2.1 %collective-permute-start.1 = (bf16[1,32,512]{2,1,0:T(8,128)(2,1)S(1)}, bf16[1,32,512]{2,1,0:T(8,128)(2,1)S(1)}, u32[]{:S(2)}, u32[]{:S(2)}) collective-permute-start(bf16[1,32,512]{2,1,0:T(8,128)(2,1)S(1)} %bitcast.39), channel_id=1, source_target_pairs={{0,3},{1,0},{2,1},{3,2},{4,7},{5,4},{6,5},{7,6},{8,11},{9,8},{10,9... | collective-permute-start | bytes 98312 | tf_op jit(solution)/shard_map/ppermute | solution.py:274
  6.7 1.0 copy.47
  7.7 0.1 collective-permute-start.4
  7.8 1.3 fusion.11
  9.1 0.7 fusion.4
  9.8 1.3 or_select_fusion
  11.1 0.1 add_cosine_fusion
  11.2 0.7 fusion.2
  11.9 0.1 cos.14
  12.0 0.1 sin.14
  12.0 3.5 %collective-permute-done.4 = f32[32,512]{0,1:T(8,128)S(1)} collective-permute-done((f32[32,512]{0,1:T(8,128)S(1)}, f32[32,512]{0,1:T(8,128)S(1)}, u32[]{:S(2)}, u32[]{:S(2)}) %collective-permute-start.4) | collective-permute-done | bytes 65568 | tf_op jit(solution)/shard_map/ppermute | solution.py:304
  15.5 0.2 maximum_select_fusion.2
  15.7 1.1 collective-permute-start.5
  16.8 0.1 copy.43
  16.9 0.1 reshape.80.phase
  17.0 0.1 collective-permute-start.3
  17.1 0.5 collective-permute-start.2
  17.6 11.6 %collective-permute-done.5 = f32[64,512]{0,1:T(8,128)S(1)} collective-permute-done((f32[64,512]{0,1:T(8,128)S(1)}, f32[64,512]{0,1:T(8,128)S(1)}, u32[]{:S(2)}, u32[]{:S(2)}) %collective-permute-start.5) | collective-permute-done | bytes 131104 | tf_op jit(solution)/shard_map/ppermute | solution.py:304
  29.2 0.2 maximum_select_fusion.3
  29.4 0.1 collective-permute-start.6
  29.5 0.0 copy-start
  29.5 3.7 %copy-done = bf16[2,9,512,512]{3,2,1,0:T(8,128)(2,1)S(1)} copy-done((bf16[2,9,512,512]{3,2,1,0:T(8,128)(2,1)S(1)}, bf16[2,9,512,512]{3,2,1,0:T(8,128)(2,1)}, u32[]{:S(2)}) %copy-start) | copy-done | bytes 9437208
  33.2 0.8 copy-done.2
  34.0 4.6 %near.2 = f32[16,2,512]{2,1,0:T(2,128)} custom-call(f32[18]{0:T(128)S(1)} %reshape.80.phase, bf16[9,32,512]{2,1,0:T(8,128)(2,1)S(1)} %bitcast.37, bf16[2,9,512,512]{3,2,1,0:T(8,128)(2,1)S(1)} %copy-done, f32[2,16,512]{2,1,0:T(8,128)S(1)} %copy-done.2), custom_call_target="tpu_custom_call" | custom-call | flops 301989888 | bytes 9437184 | tf_op jit(solution)/shard_map/near/pallas_call | solution.py:250
  38.7 4.4 %all-to-all-start.1 = ((f32[16,2,512]{2,1,0:T(2,128)}), f32[16,2,512]{2,1,0:T(2,128)S(1)}, u32[]{:S(2)}, u32[]{:S(2)}) async-start(f32[16,2,512]{2,1,0:T(2,128)} %near.2), calls=%async_computation.1 | async-start | bytes 131072 | tf_op jit(solution)/shard_map/all_to_all | solution.py:314
  43.3 0.9 pad_maximum_fusion
  44.2 5.5 %all-to-all-done.1.refs_1_ = f32[16,2,512]{2,1,0:T(2,128)S(1)} async-done(((f32[16,2,512]{2,1,0:T(2,128)}), f32[16,2,512]{2,1,0:T(2,128)S(1)}, u32[]{:S(2)}, u32[]{:S(2)}) %all-to-all-start.1) | async-done | bytes 65568 | tf_op jit(solution)/shard_map/all_to_all | solution.py:314
  49.7 3.6 %all-to-all-start = ((bf16[16,24,512]{2,1,0:T(8,128)(2,1)}), bf16[16,24,512]{2,1,0:T(8,128)(2,1)S(1)}, u32[]{:S(2)}, u32[]{:S(2)}) async-start(bf16[16,24,512]{2,1,0:T(8,128)(2,1)} %pad_maximum_fusion), calls=%async_computation | async-start | bytes 786432 | tf_op jit(solution)/shard_map/all_to_all | solution.py:314
  53.3 1.9 %collective-permute-start.7 = (f32[256,512]{0,1:T(8,128)S(1)}, f32[256,512]{0,1:T(8,128)}, u32[]{:S(2)}, u32[]{:S(2)}) collective-permute-start(f32[256,512]{0,1:T(8,128)S(1)} %maximum_select_fusion.1), channel_id=1, source_target_pairs={{0,8},{4,12},{8,0},{12,4},{1,9},{5,13},{9,1},{13,5},{2,10},{6,14},... | collective-permute-start | bytes 1572872 | tf_op jit(solution)/shard_map/ppermute | solution.py:304
  55.2 16.6 %collective-permute-done.7 = f32[256,512]{0,1:T(8,128)} collective-permute-done((f32[256,512]{0,1:T(8,128)S(1)}, f32[256,512]{0,1:T(8,128)}, u32[]{:S(2)}, u32[]{:S(2)}) %collective-permute-start.7) | collective-permute-done | bytes 524320 | tf_op jit(solution)/shard_map/ppermute | solution.py:304
  71.9 1.4 fusion.refs_2_
  73.3 22.6 %recip.2.refs_1_ = f32[16,2,512]{2,1,0:T(2,128)S(1)} custom-call(bf16[16,24,512]{2,1,0:T(8,128)(2,1)S(1)} %all-to-all-done.refs_0_, f32[16,2,512]{2,1,0:T(2,128)S(1)} %all-to-all-done.1.refs_1_, f32[512,512]{1,0:T(8,128)S(1)} %fusion.refs_2_, bf16[4,256,256]{2,1,0:T(8,128)(2,1)S(1)} %copy-done.4, f32[4,2,128]{2,1,0:T(2,128)S(1)} %copy-done.6, ...), custom_call_target="tpu_custom_call" | custom-call | flops 20000000000 | bytes 8000000 | tf_op jit(solution)/shard_map/recip/pallas_call | solution.py:212
  95.9 11.1 %all_to_all.20 = f32[16,2,512]{2,1,0:T(2,128)S(1)} all-to-all(f32[16,2,512]{2,1,0:T(2,128)S(1)} %recip.2.refs_1_), channel_id=1, replica_groups=mesh['groups'=2,'tile'=4,'sect'=4] {'tile','sect'}, dimensions={0} | all-to-all | bytes 131072 | tf_op jit(solution)/shard_map/all_to_all | solution.py:314
  107.0 0.0 copy-start.3
  107.0 0.4 collective-permute-start.8
  107.4 3.5 %collective-permute-start.9 = (bf16[1,32,512]{2,1,0:T(8,128)(2,1)S(1)}, bf16[1,32,512]{2,1,0:T(8,128)(2,1)S(1)}, u32[]{:S(2)}, u32[]{:S(2)}) collective-permute-start(bf16[1,32,512]{2,1,0:T(8,128)(2,1)S(1)} %bitcast.42), channel_id=1, source_target_pairs={{0,3},{1,0},{2,1},{3,2},{4,7},{5,4},{6,5},{7,6},{8,11},{9,8},{10,9... | collective-permute-start | bytes 98312 | tf_op jit(solution)/shard_map/ppermute | solution.py:274
  110.9 1.9 %collective-permute-done.8 = bf16[1,32,512]{2,1,0:T(8,128)(2,1)S(1)} collective-permute-done((bf16[1,32,512]{2,1,0:T(8,128)(2,1)S(1)}, bf16[1,32,512]{2,1,0:T(8,128)(2,1)S(1)}, u32[]{:S(2)}, u32[]{:S(2)}) %collective-permute-start.8) | collective-permute-done | bytes 32800 | tf_op jit(solution)/shard_map/ppermute | solution.py:274
  112.8 0.1 collective-permute-start.10
  112.9 1.7 %collective-permute-start.11 = (bf16[3,1,32,512]{3,2,1,0:T(8,128)(2,1)S(1)}, bf16[3,1,32,512]{3,2,1,0:T(8,128)(2,1)S(1)}, u32[]{:S(2)}, u32[]{:S(2)}) collective-permute-start(bf16[3,1,32,512]{3,2,1,0:T(8,128)(2,1)S(1)} %get-tuple-element.14), channel_id=1, source_target_pairs={{0,12},{4,0},{8,4},{12,8},{1,13},{5,1},{9,5},{13,9},{2,14},{6,2},{... | collective-permute-start | bytes 294920 | tf_op jit(solution)/shard_map/ppermute | solution.py:274
  114.6 23.1 %recip.3 = f32[16,2,512]{2,1,0:T(2,128)} custom-call(bf16[16,24,512]{2,1,0:T(8,128)(2,1)S(1)} %all-to-all-done.refs_0_, f32[16,2,512]{2,1,0:T(2,128)S(1)} %recip.2.refs_1_, f32[512,512]{1,0:T(8,128)S(1)} %fusion.refs_2_, bf16[4,256,256]{2,1,0:T(8,128)(2,1)S(1)} %copy-done.4, f32[4,2,128]{2,1,0:T(2,128)S(1)} %copy-done.6, f32[4,2,128,128]{3,2,1,0:T(8,128)S(1)} %copy-done.5), custom_call_target="tpu_custom_call" | custom-call | flops 20000000000 | bytes 8000000 | tf_op jit(solution)/shard_map/recip/pallas_call | solution.py:212
  137.7 5.4 %all-to-all-start.3 = ((f32[16,2,512]{2,1,0:T(2,128)}), f32[16,2,512]{2,1,0:T(2,128)S(1)}, u32[]{:S(2)}, u32[]{:S(2)}) async-start(f32[16,2,512]{2,1,0:T(2,128)} %recip.3), calls=%async_computation.3 | async-start | bytes 131072 | tf_op jit(solution)/shard_map/all_to_all | solution.py:314
  143.2 0.0 copy-start.1
  143.2 3.7 %copy-done.1 = bf16[2,9,512,512]{3,2,1,0:T(8,128)(2,1)S(1)} copy-done((bf16[2,9,512,512]{3,2,1,0:T(8,128)(2,1)S(1)}, bf16[2,9,512,512]{3,2,1,0:T(8,128)(2,1)}, u32[]{:S(2)}) %copy-start.1) | copy-done | bytes 9437208
  146.8 4.0 %near.3 = f32[16,2,512]{2,1,0:T(2,128)S(1)} custom-call(f32[18]{0:T(128)S(1)} %reshape.80.phase, bf16[9,32,512]{2,1,0:T(8,128)(2,1)S(1)} %bitcast.36, bf16[2,9,512,512]{3,2,1,0:T(8,128)(2,1)S(1)} %copy-done.1, f32[2,16,512]{2,1,0:T(8,128)S(1)} %get-tuple-element.11.source), custom_call_target="tpu_custom_call" | custom-call | flops 301989888 | bytes 9437184 | tf_op jit(solution)/shard_map/near/pallas_call | solution.py:250
  150.9 0.6 copy.51
  (36 shorter events, 0.4 us)
Async XLA Ops:
  0.6 42.5 %copy-start.7 = (bf16[4,4,512]{2,1,0:T(4,128)(2,1)S(1)}, bf16[4,4,512]{2,1,0:T(4,128)(2,1)}, u32[]{:S(2)}) copy-start(bf16[4,4,512]{2,1,0:T(4,128)(2,1)} %param.18) | copy-start | bytes 49156
  1.5 71.8 %copy-start.4 = (bf16[4,256,256]{2,1,0:T(8,128)(2,1)S(1)}, bf16[4,256,256]{2,1,0:T(8,128)(2,1)}, u32[]{:S(2)}) copy-start(bf16[4,256,256]{2,1,0:T(8,128)(2,1)} %constant.116.clone.refs_3_) | copy-start | bytes 1572868
  1.5 71.8 %copy-start.5 = (f32[4,2,128,128]{3,2,1,0:T(8,128)S(1)}, f32[4,2,128,128]{3,2,1,0:T(8,128)}, u32[]{:S(2)}) copy-start(f32[4,2,128,128]{3,2,1,0:T(8,128)} %constant.118.clone.refs_5_) | copy-start | bytes 1572868
  1.5 71.8 %copy-start.6 = (f32[4,2,128]{2,1,0:T(2,128)S(1)}, f32[4,2,128]{2,1,0:T(2,128)}, u32[]{:S(2)}) copy-start(f32[4,2,128]{2,1,0:T(2,128)} %constant.117.clone.refs_4_) | copy-start | bytes 12292
  1.5 15.5 %collective-permute-start = (bf16[1,32,512]{2,1,0:T(8,128)(2,1)S(1)}, bf16[1,32,512]{2,1,0:T(8,128)(2,1)S(1)}, u32[]{:S(2)}, u32[]{:S(2)}) collective-permute-start(bf16[1,32,512]{2,1,0:T(8,128)(2,1)S(1)} %bitcast.38), channel_id=1, source_target_pairs={{0,1},{1,2},{2,3},{3,0},{4,5},{5,6},{6,7},{7,4},{8,9},{9,10},{10,1... | collective-permute-start | bytes 98312 | tf_op jit(solution)/shard_map/ppermute | solution.py:274
  4.6 12.4 %collective-permute-start.1 = (bf16[1,32,512]{2,1,0:T(8,128)(2,1)S(1)}, bf16[1,32,512]{2,1,0:T(8,128)(2,1)S(1)}, u32[]{:S(2)}, u32[]{:S(2)}) collective-permute-start(bf16[1,32,512]{2,1,0:T(8,128)(2,1)S(1)} %bitcast.39), channel_id=1, source_target_pairs={{0,3},{1,0},{2,1},{3,2},{4,7},{5,4},{6,5},{7,6},{8,11},{9,8},{10,9... | collective-permute-start | bytes 98312 | tf_op jit(solution)/shard_map/ppermute | solution.py:274
  7.7 7.8 %collective-permute-start.4 = (f32[32,512]{0,1:T(8,128)S(1)}, f32[32,512]{0,1:T(8,128)S(1)}, u32[]{:S(2)}, u32[]{:S(2)}) collective-permute-start(f32[32,512]{0,1:T(8,128)S(1)} %multiply_bitcast_fusion), channel_id=1, source_target_pairs={{0,1},{1,0},{2,3},{3,2},{4,5},{5,4},{6,7},{7,6},{8,9},{9,8},{10,11... | collective-permute-start | bytes 196616 | tf_op jit(solution)/shard_map/ppermute | solution.py:304
  15.7 13.4 %collective-permute-start.5 = (f32[64,512]{0,1:T(8,128)S(1)}, f32[64,512]{0,1:T(8,128)S(1)}, u32[]{:S(2)}, u32[]{:S(2)}) collective-permute-start(f32[64,512]{0,1:T(8,128)S(1)} %maximum_select_fusion.2), channel_id=1, source_target_pairs={{0,2},{1,3},{2,0},{3,1},{4,6},{5,7},{6,4},{7,5},{8,10},{9,11},{10,... | collective-permute-start | bytes 393224 | tf_op jit(solution)/shard_map/ppermute | solution.py:304
  17.0 12.4 %collective-permute-start.3 = (bf16[3,1,32,512]{3,2,1,0:T(8,128)(2,1)S(1)}, bf16[3,1,32,512]{3,2,1,0:T(8,128)(2,1)S(1)}, u32[]{:S(2)}, u32[]{:S(2)}) collective-permute-start(bf16[3,1,32,512]{3,2,1,0:T(8,128)(2,1)S(1)} %get-tuple-element.17), channel_id=1, source_target_pairs={{0,12},{4,0},{8,4},{12,8},{1,13},{5,1},{9,5},{13,9},{2,14},{6,2},{... | collective-permute-start | bytes 294920 | tf_op jit(solution)/shard_map/ppermute | solution.py:274
  17.1 12.4 %collective-permute-start.2 = (bf16[3,1,32,512]{3,2,0,1:T(8,128)(2,1)S(1)}, bf16[3,1,32,512]{3,2,0,1:T(8,128)(2,1)S(1)}, u32[]{:S(2)}, u32[]{:S(2)}) collective-permute-start(bf16[3,1,32,512]{3,2,0,1:T(8,128)(2,1)S(1)} %get-tuple-element.15), channel_id=1, source_target_pairs={{0,4},{4,8},{8,12},{12,0},{1,5},{5,9},{9,13},{13,1},{2,6},{6,10},{... | collective-permute-start | bytes 294920 | tf_op jit(solution)/shard_map/ppermute | solution.py:274
  29.4 23.9 %collective-permute-start.6 = (f32[128,512]{0,1:T(8,128)S(1)}, f32[128,512]{0,1:T(8,128)S(1)}, u32[]{:S(2)}, u32[]{:S(2)}) collective-permute-start(f32[128,512]{0,1:T(8,128)S(1)} %maximum_select_fusion.3), channel_id=1, source_target_pairs={{0,4},{4,0},{8,12},{12,8},{1,5},{5,1},{9,13},{13,9},{2,6},{6,2},{1... | collective-permute-start | bytes 786440 | tf_op jit(solution)/shard_map/ppermute | solution.py:304
  29.5 3.7 %copy-start = (bf16[2,9,512,512]{3,2,1,0:T(8,128)(2,1)S(1)}, bf16[2,9,512,512]{3,2,1,0:T(8,128)(2,1)}, u32[]{:S(2)}) copy-start(bf16[2,9,512,512]{3,2,1,0:T(8,128)(2,1)} %blocks.3) | copy-start | bytes 28311556
  33.2 0.8 copy-start.2
  38.7 11.0 %all-to-all-start.1 = ((f32[16,2,512]{2,1,0:T(2,128)}), f32[16,2,512]{2,1,0:T(2,128)S(1)}, u32[]{:S(2)}, u32[]{:S(2)}) async-start(f32[16,2,512]{2,1,0:T(2,128)} %near.2), calls=%async_computation.1 | async-start | bytes 131072 | tf_op jit(solution)/shard_map/all_to_all | solution.py:314
  49.7 23.5 %all-to-all-start = ((bf16[16,24,512]{2,1,0:T(8,128)(2,1)}), bf16[16,24,512]{2,1,0:T(8,128)(2,1)S(1)}, u32[]{:S(2)}, u32[]{:S(2)}) async-start(bf16[16,24,512]{2,1,0:T(8,128)(2,1)} %pad_maximum_fusion), calls=%async_computation | async-start | bytes 786432 | tf_op jit(solution)/shard_map/all_to_all | solution.py:314
  53.3 18.6 %collective-permute-start.7 = (f32[256,512]{0,1:T(8,128)S(1)}, f32[256,512]{0,1:T(8,128)}, u32[]{:S(2)}, u32[]{:S(2)}) collective-permute-start(f32[256,512]{0,1:T(8,128)S(1)} %maximum_select_fusion.1), channel_id=1, source_target_pairs={{0,8},{4,12},{8,0},{12,4},{1,9},{5,13},{9,1},{13,5},{2,10},{6,14},... | collective-permute-start | bytes 1572872 | tf_op jit(solution)/shard_map/ppermute | solution.py:304
  107.0 36.1 %copy-start.3 = (f32[2,16,512]{2,1,0:T(8,128)}, f32[2,16,512]{2,1,0:T(8,128)S(1)}, u32[]{:S(2)}) copy-start(f32[2,16,512]{2,1,0:T(8,128)S(1)} %get-tuple-element.11.source) | copy-start | bytes 196612
  107.0 5.8 %collective-permute-start.8 = (bf16[1,32,512]{2,1,0:T(8,128)(2,1)S(1)}, bf16[1,32,512]{2,1,0:T(8,128)(2,1)S(1)}, u32[]{:S(2)}, u32[]{:S(2)}) collective-permute-start(bf16[1,32,512]{2,1,0:T(8,128)(2,1)S(1)} %bitcast.41), channel_id=1, source_target_pairs={{0,1},{1,2},{2,3},{3,0},{4,5},{5,6},{6,7},{7,4},{8,9},{9,10},{10,1... | collective-permute-start | bytes 98312 | tf_op jit(solution)/shard_map/ppermute | solution.py:274
  107.4 5.4 %collective-permute-start.9 = (bf16[1,32,512]{2,1,0:T(8,128)(2,1)S(1)}, bf16[1,32,512]{2,1,0:T(8,128)(2,1)S(1)}, u32[]{:S(2)}, u32[]{:S(2)}) collective-permute-start(bf16[1,32,512]{2,1,0:T(8,128)(2,1)S(1)} %bitcast.42), channel_id=1, source_target_pairs={{0,3},{1,0},{2,1},{3,2},{4,7},{5,4},{6,5},{7,6},{8,11},{9,8},{10,9... | collective-permute-start | bytes 98312 | tf_op jit(solution)/shard_map/ppermute | solution.py:274
  112.8 30.2 %collective-permute-start.10 = (bf16[3,1,32,512]{3,2,0,1:T(8,128)(2,1)S(1)}, bf16[3,1,32,512]{3,2,0,1:T(8,128)(2,1)S(1)}, u32[]{:S(2)}, u32[]{:S(2)}) collective-permute-start(bf16[3,1,32,512]{3,2,0,1:T(8,128)(2,1)S(1)} %get-tuple-element.12), channel_id=1, source_target_pairs={{0,4},{4,8},{8,12},{12,0},{1,5},{5,9},{9,13},{13,1},{2,6},{6,10},{... | collective-permute-start | bytes 294920 | tf_op jit(solution)/shard_map/ppermute | solution.py:274
  112.9 30.2 %collective-permute-start.11 = (bf16[3,1,32,512]{3,2,1,0:T(8,128)(2,1)S(1)}, bf16[3,1,32,512]{3,2,1,0:T(8,128)(2,1)S(1)}, u32[]{:S(2)}, u32[]{:S(2)}) collective-permute-start(bf16[3,1,32,512]{3,2,1,0:T(8,128)(2,1)S(1)} %get-tuple-element.14), channel_id=1, source_target_pairs={{0,12},{4,0},{8,4},{12,8},{1,13},{5,1},{9,5},{13,9},{2,14},{6,2},{... | collective-permute-start | bytes 294920 | tf_op jit(solution)/shard_map/ppermute | solution.py:274
  137.7 13.1 %all-to-all-start.3 = ((f32[16,2,512]{2,1,0:T(2,128)}), f32[16,2,512]{2,1,0:T(2,128)S(1)}, u32[]{:S(2)}, u32[]{:S(2)}) async-start(f32[16,2,512]{2,1,0:T(2,128)} %recip.3), calls=%async_computation.3 | async-start | bytes 131072 | tf_op jit(solution)/shard_map/all_to_all | solution.py:314
  143.2 3.7 %copy-start.1 = (bf16[2,9,512,512]{3,2,1,0:T(8,128)(2,1)S(1)}, bf16[2,9,512,512]{3,2,1,0:T(8,128)(2,1)}, u32[]{:S(2)}) copy-start(bf16[2,9,512,512]{3,2,1,0:T(8,128)(2,1)} %blocks.3) | copy-start | bytes 28311556

commit v2 on v0

v2 whole, which is shorter than its diff:
```python
import functools

import jax
import jax.numpy as jnp
import ml_dtypes
import numpy as np
from jax import lax
from jax.experimental import pallas as pl
from jax.experimental.pallas import tpu as pltpu
from jax.sharding import PartitionSpec as P

STENCIL = 4
RADIX = 4
UNROLL = 8
F32 = jnp.float32
BF = jnp.bfloat16
AXES = ("tile", "sect")


def split_host(x):
    hi = x.astype(ml_dtypes.bfloat16)
    lo = (x - hi.astype(np.float64)).astype(ml_dtypes.bfloat16)
    return np.stack([hi, lo])


def transform_tables(length):
    short = length // RADIX
    index = np.arange(short)
    tables = []
    for r in range(RADIX):
        angle = 2 * np.pi / length * (((RADIX * index[:, None] + r) * index[None, :]) % length)
        c, s = np.cos(angle), np.sin(angle)
        full = np.block([[c, -s], [s, c]])
        tables.append(np.stack([split_host(full), split_host(full.T)]))
    return np.stack(tables)


def dot(a, b):
    return jnp.dot(a, b, preferred_element_type=F32)


def dot_last(a, b):
    return lax.dot_general(a, b, (((1,), (1,)), ((), ())), preferred_element_type=F32)


def split(x):
    hi = x.astype(BF)
    return hi, (x - hi.astype(F32)).astype(BF)


def times_right(x, table):
    hi, lo = split(x)
    return dot(hi, table[0]) + dot(lo, table[0]) + dot(hi, table[1])


def times_left(table, x):
    hi, lo = split(x)
    return dot(table[0], hi) + dot(table[0], lo) + dot(table[1], hi)


def butterfly(parts, sign):
    (ar, ai), (br, bi), (cr, ci), (dr, di) = parts
    even_r, even_i, diff_r, diff_i = ar + cr, ai + ci, ar - cr, ai - ci
    odd_r, odd_i = br + dr, bi + di
    turn_r, turn_i = (di - bi, br - dr) if sign > 0 else (bi - di, dr - br)
    return [
        (even_r + odd_r, even_i + odd_i),
        (diff_r + turn_r, diff_i + turn_i),
        (even_r - odd_r, even_i - odd_i),
        (diff_r - turn_r, diff_i - turn_i),
    ]


def window_rows(rows_dev):
    lead = max((b * rows_dev) % 8 for b in range(8))
    return -(-(rows_dev + STENCIL - 1 + lead) // 8) * 8


def recip_kernel(rows_dev, n1, n2, meta, scale, tab1, tab2, *rest):
    *source, out, grid, freq, field, ahead = rest
    blocks, _, panels = meta.shape
    q1, q2 = n1 // RADIX, n2 // RADIX
    wide = 2 * q2
    win = window_rows(rows_dev)

    def describe(block):
        rows = meta[block].astype(F32)
        weights = rows[2 : 2 + STENCIL * STENCIL]
        start = (block * rows_dev) // 8 * 8
        first_row = rows[18:19] + (block * rows_dev - start).astype(F32)
        col_group, col_rest = rows[19:20], rows[20:21]
        lane = lax.broadcasted_iota(jnp.int32, (q2, panels), 0).astype(F32)
        hits = [
            jnp.where(lane == jnp.where(col_rest == float(r), col_group, -1.0), 1.0, 0.0)
            for r in range(RADIX)
        ]
        one_hot = jnp.concatenate(hits, 0).astype(BF)
        offset = lax.broadcasted_iota(jnp.int32, (win, panels), 0).astype(F32) - first_row
        at = [offset == float(a) for a in range(STENCIL)]
        spread = []
        for b in range(STENCIL):
            part = jnp.where(at[0], weights[b : b + 1], 0.0)
            for a in range(1, STENCIL):
                k = a * STENCIL + b
                part = jnp.where(at[a], weights[k : k + 1], part)
            spread.append(part)
        return rows, pl.multiple_of(start, 8), one_hot, spread

    grid[...] = jnp.zeros_like(grid)

    def scatter(block, carry):
        rows, start, one_hot, spread = describe(block)
        value = source[0][block].astype(BF).astype(F32) if source else rows[0:2]
        terms = []
        for b in range(STENCIL):
            for c in range(2):
                product = spread[b] * value[c : c + 1]
                hi = product.astype(BF).astype(F32)
                terms += [hi, product - hi]
        sums = dot_last(jnp.concatenate(terms, 0).astype(BF), one_hot)
        for r in range(RADIX):
            for c in range(2):
                total = None
                for b in range(STENCIL):
                    k = (b * 2 + c) * 2 * win
                    lanes = slice((r - b) % RADIX * q2, ((r - b) % RADIX + 1) * q2)
                    x = sums[k : k + win, lanes] + sums[k + win : k + 2 * win, lanes]
                    if r < b:
                        x = pltpu.roll(x, 1, 1)
                    total = x if total is None else total + x
                lanes = slice((r * 2 + c) * q2, (r * 2 + c + 1) * q2)
                grid[pl.ds(start, win), lanes] += total
        return carry

    lax.fori_loop(0, blocks, scatter, 0, unroll=UNROLL)
    grid[0:win, :] += grid[n1 : n1 + win, :]

    parts = []
    for r in range(RADIX):
        y = times_right(grid[0:n1, r * wide : (r + 1) * wide], tab2.at[r, 0])
        parts.append((y[:, :q2], y[:, q2:]))
    for m, (real, imag) in enumerate(butterfly(parts, -1)):
        freq[2 * m] = real
        freq[2 * m + 1] = imag

    for pair in range(0, RADIX, 2):
        parts = []
        for r in range(RADIX):
            rows = pl.ds(r, q1, stride=RADIX)
            both = [
                jnp.concatenate([freq[2 * pair + c, rows, :], freq[2 * pair + 2 + c, rows, :]], 1)
                for c in range(2)
            ]
            y = times_left(tab1.at[r, 1], jnp.concatenate(both, 0))
            parts.append((y[:q1], y[q1:]))
        scaled = []
        for m, (real, imag) in enumerate(butterfly(parts, -1)):
            k = scale[m * q1 : (m + 1) * q1, pair * q2 : (pair + 2) * q2]
            scaled.append((real * k, imag * k))
        for r, both in enumerate(butterfly(scaled, 1)):
            y = times_left(tab1.at[r, 0], jnp.concatenate(both, 0))
            rows = pl.ds(r, q1, stride=RADIX)
            for c in range(2):
                freq[2 * pair + c, rows, :] = y[c * q1 : (c + 1) * q1, :q2]
                freq[2 * pair + 2 + c, rows, :] = y[c * q1 : (c + 1) * q1, q2:]

    parts = [(freq[2 * m], freq[2 * m + 1]) for m in range(RADIX)]
    for r, both in enumerate(butterfly(parts, 1)):
        y = times_right(jnp.concatenate(both, 1), tab2.at[r, 1])
        field[0:n1, r * wide : (r + 1) * wide] = y
        if r < STENCIL - 1:
            for c in range(2):
                lanes = slice((r * 2 + c) * q2, (r * 2 + c + 1) * q2)
                ahead[0:n1, lanes] = pltpu.roll(y[:, c * q2 : (c + 1) * q2], q2 - 1, 1)
    field[n1 : n1 + win, :] = field[0:win, :]
    ahead[n1 : n1 + win, :] = ahead[0:win, :]

    def collect(block, carry):
        _, start, one_hot, spread = describe(block)
        pieces = []
        for b in range(STENCIL):
            for c in range(2):
                row = []
                for r in range(b, b + RADIX):
                    lanes = slice((r % RADIX * 2 + c) * q2, (r % RADIX * 2 + c + 1) * q2)
                    row.append((field if r < RADIX else ahead)[pl.ds(start, win), lanes])
                pieces.append(jnp.concatenate(row, 1))
        values = dot(jnp.concatenate(pieces, 0).astype(BF), one_hot)
        for c in range(2):
            total = None
            for b in range(STENCIL):
                k = (b * 2 + c) * win
                x = values[k : k + win] * spread[b]
                total = x if total is None else total + x
            out[block, c : c + 1] = jnp.sum(total, 0, keepdims=True)
        return carry

    lax.fori_loop(0, blocks, collect, 0, unroll=UNROLL)


def recip_apply(meta, scale, rows_dev, *source):
    blocks, _, panels = meta.shape
    n1, n2 = scale.shape
    reach = n1 + window_rows(rows_dev)
    tab1, tab2 = transform_tables(n1), transform_tables(n2)
    in_vmem = pl.BlockSpec(memory_space=pltpu.VMEM)
    return pl.pallas_call(
        functools.partial(recip_kernel, rows_dev, n1, n2),
        out_shape=jax.ShapeDtypeStruct((blocks, 2, panels), F32),
        in_specs=[in_vmem] * (4 + len(source)),
        out_specs=in_vmem,
        scratch_shapes=[
            pltpu.VMEM((reach, 2 * n2), F32),
            pltpu.VMEM((2 * RADIX, n1, n2 // RADIX), F32),
            pltpu.VMEM((reach, 2 * n2), F32),
            pltpu.VMEM((reach, 2 * n2 // RADIX * (STENCIL - 1)), F32),
        ],
        compiler_params=pltpu.CompilerParams(vmem_limit_bytes=28 * 1024 * 1024),
        cost_estimate=pl.CostEstimate(
            flops=10_000_000_000, bytes_accessed=8_000_000, transcendentals=0
        ),
        name="recip",
    )(meta, scale, jnp.asarray(tab1), jnp.asarray(tab2), *source)


def border_phases(bloch):
    lane = lax.broadcasted_iota(jnp.int32, (1, 128), 1)
    angle = jnp.zeros((1, 128), F32)
    for k, (axis, offset) in enumerate(zip(AXES, (lane // 3 - 1, lane % 3 - 1))):
        place = lax.axis_index(axis) + offset
        leaves = (place < 0) | (place >= lax.axis_size(axis))
        angle += jnp.where(leaves, bloch[k] * offset.astype(F32), 0.0)
    return jnp.cos(angle), jnp.sin(angle)


def near_kernel(probes_first, bloch, halo, source, blocks, out):
    count, twice, _ = halo.shape
    probes = twice // 2
    cosines, sines = border_phases(bloch)
    total_real = 0.5 * source[0]
    total_imag = 0.5 * source[1]
    for d in range(count):
        x = halo[d]
        with_real = dot(x, blocks[0, d])
        with_imag = dot(x, blocks[1, d])
        real = with_real[:probes] - with_imag[probes:]
        imag = with_real[probes:] + with_imag[:probes]
        c = cosines[:, d : d + 1]
        s = sines[:, d : d + 1]
        total_real += real * c - imag * s
        total_imag += real * s + imag * c
    for c, total in enumerate((total_real, total_imag)):
        if probes_first:
            out[:, c, :] = total
        else:
            out[c] = total


def near_apply(halo, near_blocks, bloch_angle, source, probes_first):
    _, probes, panels = source.shape
    _, count, depth, _ = near_blocks.shape
    in_vmem = pl.BlockSpec(memory_space=pltpu.VMEM)
    shape = (probes, 2, panels) if probes_first else (2, probes, panels)
    return pl.pallas_call(
        functools.partial(near_kernel, probes_first),
        out_shape=jax.ShapeDtypeStruct(shape, F32),
        in_specs=[pl.BlockSpec(memory_space=pltpu.SMEM), in_vmem, in_vmem, in_vmem],
        out_specs=in_vmem,
        compiler_params=pltpu.CompilerParams(vmem_limit_bytes=8 * 1024 * 1024),
        cost_estimate=pl.CostEstimate(
            flops=4 * count * 2 * probes * depth * panels,
            bytes_accessed=2 * near_blocks.size,
            transcendentals=0,
        ),
        name="near",
    )(bloch_angle, halo, source, near_blocks)


def neighbour_kernel(tiles, sects, part, start, image, sent):
    image[...] = part[...] + start[...]

    def lay(block, carry):
        tile, sect = block // sects, block % sects
        rows = []
        for d in (-1, 0, 1):
            for e in (-1, 0, 1):
                near = (tile + d + tiles) % tiles * sects + (sect + e + sects) % sects
                rows.append(image[near])
        mine = image[block]
        hi = mine.astype(BF).astype(F32)
        mid = (mine - hi).astype(BF).astype(F32)
        rows += [mid, mine - hi - mid, jnp.zeros_like(mine)]
        sent[block] = jnp.concatenate(rows, 0).astype(BF)
        return carry

    lax.fori_loop(0, image.shape[0], lay, 0, unroll=4)


def neighbour_rows(part, start):
    blocks, _, panels = part.shape
    in_vmem = pl.BlockSpec(memory_space=pltpu.VMEM)
    return pl.pallas_call(
        functools.partial(neighbour_kernel, lax.axis_size("tile"), lax.axis_size("sect")),
        out_shape=(
            jax.ShapeDtypeStruct(part.shape, F32),
            jax.ShapeDtypeStruct((blocks, 24, panels), BF),
        ),
        in_specs=[in_vmem] * 2,
        out_specs=(in_vmem, in_vmem),
        compiler_params=pltpu.CompilerParams(vmem_limit_bytes=24 * 1024 * 1024),
        name="neighbour_rows",
    )(part, start)


def pack_kernel(rows_dev, source, stencil, first_row, first_col, sent, low):
    probes, panels = source.shape[1:]
    row, col = first_row[...], first_col[...]
    numbers = [row % rows_dev, col // RADIX, col % RADIX]
    rows = [stencil[a].astype(F32) for a in range(STENCIL)] + [x.astype(F32) for x in numbers]
    rows.append(jnp.zeros((3, panels), F32))
    described = jnp.concatenate(rows, 0)
    for p in range(probes):
        value = [source[c, p : p + 1, :] for c in range(2)]
        sent[p] = jnp.concatenate(value + [described], 0).astype(BF)
    for c in range(2):
        low[c * probes : (c + 1) * probes] = source[c].astype(BF)


def pack(rows_dev, source, stencil, grid_row, grid_col):
    _, probes, panels = source.shape
    rows = 2 + STENCIL * STENCIL + 6
    in_vmem = pl.BlockSpec(memory_space=pltpu.VMEM)
    return pl.pallas_call(
        functools.partial(pack_kernel, rows_dev),
        out_shape=(
            jax.ShapeDtypeStruct((probes, rows, panels), BF),
            jax.ShapeDtypeStruct((2 * probes, panels), BF),
        ),
        in_specs=[in_vmem] * 4,
        out_specs=(in_vmem, in_vmem),
        compiler_params=pltpu.CompilerParams(vmem_limit_bytes=16 * 1024 * 1024),
        name="pack",
    )(source, stencil, grid_row[None], grid_col[None])


def shifted(array, axis, by):
    count = lax.axis_size(axis)
    return lax.ppermute(array, axis, [(i, (i + by) % count) for i in range(count)])


def beside(block, axis):
    return jnp.stack([shifted(block, axis, 1), block, shifted(block, axis, -1)])


def doubling_steps():
    far = [(axis, 2**p) for axis in AXES[::-1] for p in range(1, 12) if 2**p < lax.axis_size(axis)]
    return far[::-1] + [(axis, 1) for axis in AXES[::-1] if lax.axis_size(axis) > 1]


def doubled(block, step):
    axis, reach = step
    other = lax.ppermute(block, axis, [(i, i ^ reach) for i in range(lax.axis_size(axis))])
    upper = (lax.axis_index(axis) // reach) % 2 == 1
    return jnp.where(upper, jnp.stack([other, block]), jnp.stack([block, other]))


def in_columns(block, steps):
    held = steps[::-1]
    order = sorted(range(len(held)), key=lambda k: (AXES.index(held[k][0]), -held[k][1]))
    *_, columns, length = block.shape
    dims = len(held)
    whole = block.transpose([dims + 1] + order + [dims])
    return whole.reshape(length, columns * 2**dims)


def exchange(parts):
    return lax.all_to_all(parts, AXES, 0, 0, tiled=True)


def local(source_probes, near_blocks, bloch_angle, grid_row, grid_col, stencil, recip_kernel):
    count = lax.axis_size("tile") * lax.axis_size("sect")
    n1 = recip_kernel.shape[0]
    n2 = recip_kernel.shape[1] * count
    rows_dev = n1 // count
    _, probes, panels = source_probes.shape
    repeat = count // probes

    def to_owners(rows):
        return jnp.repeat(rows, repeat, axis=0) if repeat > 1 else rows

    def to_panels(rows):
        return exchange(rows)[::repeat]

    sent, low = pack(rows_dev, source_probes, stencil, grid_row, grid_col)
    meta = exchange(to_owners(sent))
    steps = doubling_steps()
    kernel_rows = doubled((recip_kernel * (1.0 / (n1 * n2))).T, steps[0])
    kernel_rows, low = lax.optimization_barrier((kernel_rows, low))
    halo = beside(beside(low, "sect"), "tile").reshape(9, 2 * probes, panels)
    for step in steps[1:-1]:
        kernel_rows = doubled(kernel_rows, step)
    first_near = near_apply(halo, near_blocks, bloch_angle, source_probes, True)
    kernel_rows, first_near = lax.optimization_barrier((kernel_rows, first_near))
    scale = in_columns(doubled(kernel_rows, steps[-1]), steps)
    start = exchange(to_owners(first_near))
    first_owned, spread = neighbour_rows(recip_apply(meta, scale, rows_dev), start)
    second_owned = recip_apply(meta, scale, rows_dev, first_owned)
    rows, second_owned = lax.optimization_barrier((to_panels(spread), second_owned))
    rows = rows.transpose(1, 0, 2)
    halo = rows[:18].reshape(9, 2 * probes, panels)
    first_image = rows[8:10].astype(F32) + rows[18:20].astype(F32) + rows[20:22].astype(F32)
    second_near = near_apply(halo, near_blocks, bloch_angle, first_image, False)
    second_image = second_near + to_panels(second_owned).transpose(1, 0, 2)
    return (first_image, second_image)


def solution(mesh):
    return jax.shard_map(
        local,
        mesh=mesh,
        in_specs=(
            P(None, "groups", AXES),
            P("groups", None, None, AXES),
            P("groups"),
            P(AXES),
            P(AXES),
            P(None, None, AXES),
            P("groups", AXES),
        ),
        out_specs=(P(None, "groups", AXES), P(None, "groups", AXES)),
        check_vma=False,
    )
```

time: 701 us -> 97.2 us (0.14)
  matrix products: 198 us -> 0 us
  local copies, waits for them, and re-layouts: 188 us -> 15.4 us
  waiting for transfers between devices: 161 us -> 9.06 us
  other arithmetic: 108 us -> 1.78 us
  Pallas kernels: 0 us -> 37.2 us
    dot_general x48 -> x0, matrix products: 198 us -> none  [the longest x2 63.5 us: recip_term(): spread = jnp.dot(flat, matrix, preferred_element_type=jnp.float32)]
    all_to_all x4, waiting for transfers between devices: 124 us -> 0.61 us  [exchange(): return lax.all_to_all(parts, AXES, 0, 0, tiled=True)]
    convert_element_type x5 -> x0, other arithmetic: 64.7 us -> none  [the longest x1 62.7 us: spread_matrix(): return matrix.astype(jnp.bfloat16)]
    all_to_all x5 -> x0, local copies, waits for them, and re-layouts: 49.6 us -> none  [the longest x2 28.7 us: recip_term(): lax.all_to_all(spatial, ('tile', 'sect'), split_axis=0, concat_axis=2, ti...]
    reshape x7 -> x1, local copies, waits for them, and re-layouts: 48 us -> 0.33 us  [in_columns(): return whole.reshape(length, columns * 2 ** dims)]
    unnamed x106 -> x24, local copies, waits for them, and re-layouts: 61.7 us -> 14.9 us
    pallas_call x0 -> x6, Pallas kernels: none -> 37.2 us  [the longest x2 30 us: recip_apply(): pl.pallas_call(functools.partial(recip_kernel, rows_dev, n1, n2), out_sha...]
    all_to_all x4 -> x0, other arithmetic: 30.4 us -> none  [the longest x2 15.9 us: recip_term(): lax.all_to_all(spectrum, ('tile', 'sect'), split_axis=2, concat_axis=0, t...]
  transfers between devices with their start and end apart: 16 -> 12, of which waited for: 10 -> 6; matrix products, arithmetic and copies ran while one was open for 28% -> 1% of each run, Pallas kernels for 0% -> 37%
where the time goes in v2:
time: 97.2 us; the launch traced here: 96.3 us
  Pallas kernels  37.2 us (38%)
  starting transfers between devices  31.9 us (33%)
  local copies, waits for them, and re-layouts  15.4 us (16%)
  waiting for transfers between devices  9.06 us (9%)
  other arithmetic  1.78 us (2%)
    pallas_call x2, Pallas kernels, recip_apply(): pl.pallas_call(functools.partial(recip_kernel, rows_dev, n1, n2), out_sha...  30 us
    all_to_all x4, starting transfers between devices, exchange(): return lax.all_to_all(parts, AXES, 0, 0, tiled=True)  22.4 us
    unnamed x24, local copies, waits for them, and re-layouts  14.9 us
    ppermute x4, starting transfers between devices, shifted(): lax.ppermute(array, axis, [(i, (i + by) % count) for i in range(count)])  5.32 us
    pallas_call x2, Pallas kernels, near_apply(): pl.pallas_call(functools.partial(near_kernel, probes_first), out_shape=ja...  5.17 us
    ppermute x4, waiting for transfers between devices, shifted(): lax.ppermute(array, axis, [(i, (i + by) % count) for i in range(count)])  5.01 us
    ppermute x4, starting transfers between devices, doubled(): lax.ppermute(block, axis, [(i, i ^ reach) for i in range(lax.axis_size(ax...  4.19 us
    ppermute x4, waiting for transfers between devices, doubled(): lax.ppermute(block, axis, [(i, i ^ reach) for i in range(lax.axis_size(ax...  3.44 us
  transfers between devices with their start and end apart: 12, of which 6 were waited for; matrix products, arithmetic and copies ran while one was open for 1% of the time, Pallas kernels for 37%

profile of v2, /device:TPU:0, one launch (start us, length us, event | category | flops | bytes accessed | tf_op | source)
XLA Modules:
  0.0 96.3 jit_solution(6319770744812038548)
XLA Ops:
  0.6 0.9 multiply_bitcast_fusion.1
  1.5 3.0 %collective-permute-start = (f32[32,512]{1,0:T(8,128)S(1)}, f32[32,512]{1,0:T(8,128)S(1)}, u32[]{:S(2)}, u32[]{:S(2)}) collective-permute-start(f32[32,512]{1,0:T(8,128)S(1)} %get-tuple-element.24), channel_id=1, source_target_pairs={{0,8},{4,12},{8,0},{12,4},{1,9},{5,13},{9,1},{13,5},{2,10},{6,14},... | collective-permute-start | bytes 196616 | tf_op jit(solution)/shard_map/ppermute | solution.py:362
  4.5 0.8 copy-done.2
  5.4 0.7 copy-done.5
  6.1 0.7 copy-done.8
  6.8 0.7 copy-done.9
  7.4 0.8 pack.1
  8.3 3.7 %collective-permute-start.4 = (bf16[32,512]{1,0:T(8,128)(2,1)S(1)}, bf16[32,512]{1,0:T(8,128)(2,1)S(1)}, u32[]{:S(2)}, u32[]{:S(2)}) collective-permute-start(bf16[32,512]{1,0:T(8,128)(2,1)S(1)} %get-tuple-element.15), channel_id=1, source_target_pairs={{0,3},{1,0},{2,1},{3,2},{4,7},{5,4},{6,5},{7,6},{8,11},{9,8},{10,9... | collective-permute-start | bytes 98312 | tf_op jit(solution)/shard_map/ppermute | solution.py:348
  11.9 0.0 collective-permute-start.3
  11.9 1.0 %collective-permute-start.1 = (f32[2,32,512]{2,1,0:T(8,128)S(1)}, f32[2,32,512]{2,1,0:T(8,128)S(1)}, u32[]{:S(2)}, u32[]{:S(2)}) collective-permute-start(f32[2,32,512]{2,1,0:T(8,128)S(1)} %maximum_select_fusion.4), channel_id=1, source_target_pairs={{0,2},{1,3},{2,0},{3,1},{4,6},{5,7},{6,4},{7,5},{8,10},{9,11},{10,... | collective-permute-start | bytes 393224 | tf_op jit(solution)/shard_map/ppermute | solution.py:362
  12.9 4.8 %all-to-all-start = ((bf16[16,24,512]{2,1,0:T(8,128)(2,1)}), bf16[16,24,512]{2,1,0:T(8,128)(2,1)S(1)}, u32[]{:S(2)}, u32[]{:S(2)}) async-start(bf16[16,24,512]{2,1,0:T(8,128)(2,1)} %get-tuple-element.12), calls=%async_computation | async-start | bytes 786432 | tf_op jit(solution)/shard_map/all_to_all | solution.py:377
  17.7 0.0 collective-permute-done.4
  17.7 0.1 collective-permute-done.3
  17.8 1.7 %collective-permute-start.6 = (bf16[3,32,512]{2,1,0:T(8,128)(2,1)S(1)}, bf16[3,32,512]{2,1,0:T(8,128)(2,1)S(1)}, u32[]{:S(2)}, u32[]{:S(2)}) collective-permute-start(bf16[3,32,512]{2,1,0:T(8,128)(2,1)S(1)} %get-tuple-element.23), channel_id=1, source_target_pairs={{0,12},{4,0},{8,4},{12,8},{1,13},{5,1},{9,5},{13,9},{2,14},{6,2},{... | collective-permute-start | bytes 294920 | tf_op jit(solution)/shard_map/ppermute | solution.py:348
  19.5 1.5 %collective-permute-done.1 = f32[2,32,512]{2,1,0:T(8,128)S(1)} collective-permute-done((f32[2,32,512]{2,1,0:T(8,128)S(1)}, f32[2,32,512]{2,1,0:T(8,128)S(1)}, u32[]{:S(2)}, u32[]{:S(2)}) %collective-permute-start.1) | collective-permute-done | bytes 131104 | tf_op jit(solution)/shard_map/ppermute | solution.py:362
  21.0 0.1 collective-permute-start.2
  21.1 2.9 %collective-permute-done.6 = bf16[3,32,512]{2,1,0:T(8,128)(2,1)S(1)} collective-permute-done((bf16[3,32,512]{2,1,0:T(8,128)(2,1)S(1)}, bf16[3,32,512]{2,1,0:T(8,128)(2,1)S(1)}, u32[]{:S(2)}, u32[]{:S(2)}) %collective-permute-start.6) | collective-permute-done | bytes 98336 | tf_op jit(solution)/shard_map/ppermute | solution.py:348
  24.1 2.0 %collective-permute-done.5 = bf16[3,32,512]{2,1,0:T(8,128)(2,1)S(1)} collective-permute-done((bf16[3,32,512]{2,1,0:T(8,128)(2,1)S(1)}, bf16[3,32,512]{2,1,0:T(8,128)(2,1)S(1)}, u32[]{:S(2)}, u32[]{:S(2)}) %collective-permute-start.5) | collective-permute-done | bytes 98336 | tf_op jit(solution)/shard_map/ppermute | solution.py:348
  26.1 0.0 copy-start
  26.1 3.7 %copy-done = bf16[2,9,512,512]{3,2,1,0:T(8,128)(2,1)S(1)} copy-done((bf16[2,9,512,512]{3,2,1,0:T(8,128)(2,1)S(1)}, bf16[2,9,512,512]{3,2,1,0:T(8,128)(2,1)}, u32[]{:S(2)}) %copy-start) | copy-done | bytes 9437208
  29.8 0.8 copy-done.3
  30.6 0.7 copy-done.6
  31.3 2.9 %near.2 = f32[16,2,512]{2,1,0:T(2,128)} custom-call(f32[2]{0:T(128)S(1)} %copy-done.6, bf16[9,32,512]{2,1,0:T(8,128)(2,1)S(1)} %bitcast.34, f32[2,16,512]{2,1,0:T(8,128)S(1)} %copy-done.3, bf16[2,9,512,512]{3,2,1,0:T(8,128)(2,1)S(1)} %copy-done), custom_call_target="tpu_custom_call" | custom-call | flops 301989888 | bytes 9437184 | tf_op jit(solution)/shard_map/near/pallas_call | solution.py:264
  34.2 0.0 collective-permute-done.2
  34.3 0.1 collective-permute-start.7
  34.4 1.9 %collective-permute-done.7 = f32[2,2,2,32,512]{4,3,0,1,2:T(8,128)S(1)} collective-permute-done((f32[2,2,2,32,512]{4,3,0,1,2:T(8,128)S(1)}, f32[2,2,2,32,512]{4,3,0,1,2:T(8,128)S(1)}, u32[]{:S(2)}, u32[]{:S(2)}) %collective-permute-start.7) | collective-permute-done | bytes 524320 | tf_op jit(solution)/shard_map/ppermute | solution.py:362
  36.3 0.1 maximum_select_fusion
  36.4 0.3 copy.22.scale
  36.8 0.0 all-to-all-done.meta
  36.8 5.7 %all-to-all-start.1 = ((f32[16,2,512]{2,1,0:T(2,128)}), f32[16,2,512]{2,1,0:T(2,128)S(1)}, u32[]{:S(2)}, u32[]{:S(2)}) async-start(f32[16,2,512]{2,1,0:T(2,128)} %near.2), calls=%async_computation.1 | async-start | bytes 131072 | tf_op jit(solution)/shard_map/all_to_all | solution.py:377
  42.4 0.0 copy-start.10
  42.5 1.6 %copy-done.10 = bf16[4,2,2,256,256]{4,3,2,1,0:T(8,128)(2,1)S(1)} copy-done((bf16[4,2,2,256,256]{4,3,2,1,0:T(8,128)(2,1)S(1)}, bf16[4,2,2,256,256]{4,3,2,1,0:T(8,128)(2,1)}, u32[]{:S(2)}) %copy-start.10) | copy-done | bytes 2097176
  44.0 14.7 %recip.2.part = f32[16,2,512]{2,1,0:T(2,128)S(1)} custom-call(bf16[16,24,512]{2,1,0:T(8,128)(2,1)S(1)} %all-to-all-done.meta, f32[512,512]{1,0:T(8,128)S(1)} %copy.22.scale, bf16[4,2,2,256,256]{4,3,2,1,0:T(8,128)(2,1)S(1)} %copy-done.10, bf16[4,2,2,256,256]{4,3,2,1,0:T(8,128)(2,1)S(1)} %copy-done.10), custom_call_target="tpu_custom_call" | custom-call | flops 10000000000 | bytes 8000000 | tf_op jit(solution)/shard_map/recip/pallas_call | solution.py:207
  58.7 0.0 all-to-all-done.1.start
  58.8 1.2 %neighbour_rows.1 = (f32[16,2,512]{2,1,0:T(2,128)S(1)}, bf16[16,24,512]{2,1,0:T(8,128)(2,1)}) custom-call(f32[16,2,512]{2,1,0:T(2,128)S(1)} %recip.2.part, f32[16,2,512]{2,1,0:T(2,128)S(1)} %all-to-all-done.1.start), custom_call_target="tpu_custom_call" | custom-call | tf_op jit(solution)/shard_map/neighbour_rows/pallas_call | solution.py:302
  60.0 6.0 %all-to-all-start.2 = ((bf16[16,24,512]{2,1,0:T(8,128)(2,1)}), bf16[16,24,512]{2,1,0:T(8,128)(2,1)S(1)}, u32[]{:S(2)}, u32[]{:S(2)}) async-start(bf16[16,24,512]{2,1,0:T(8,128)(2,1)} %get-tuple-element.18), calls=%async_computation.2 | async-start | bytes 786432 | tf_op jit(solution)/shard_map/all_to_all | solution.py:377
  66.0 0.0 copy-start.11
  66.0 1.6 %copy-done.11 = bf16[4,2,2,256,256]{4,3,2,1,0:T(8,128)(2,1)S(1)} copy-done((bf16[4,2,2,256,256]{4,3,2,1,0:T(8,128)(2,1)S(1)}, bf16[4,2,2,256,256]{4,3,2,1,0:T(8,128)(2,1)}, u32[]{:S(2)}) %copy-start.11) | copy-done | bytes 2097176
  67.6 15.3 %recip.3 = f32[16,2,512]{2,1,0:T(2,128)} custom-call(bf16[16,24,512]{2,1,0:T(8,128)(2,1)S(1)} %all-to-all-done.meta, f32[512,512]{1,0:T(8,128)S(1)} %copy.22.scale, bf16[4,2,2,256,256]{4,3,2,1,0:T(8,128)(2,1)S(1)} %copy-done.11, bf16[4,2,2,256,256]{4,3,2,1,0:T(8,128)(2,1)S(1)} %copy-done.11, f32[16,2,512]{2,1,0:T(2,128)S(1)} %get-tuple-element.19.rest_0_), custom_call_target="tpu_custom_call" | custom-call | flops 10000000000 | bytes 8000000 | tf_op jit(solution)/shard_map/recip/pallas_call | solution.py:207
  82.9 0.0 all-to-all-done.2
  82.9 0.1 copy.29
  83.1 6.0 %all-to-all-start.3 = ((f32[16,2,512]{2,1,0:T(2,128)}), f32[16,2,512]{2,1,0:T(2,128)S(1)}, u32[]{:S(2)}, u32[]{:S(2)}) async-start(f32[16,2,512]{2,1,0:T(2,128)} %recip.3), calls=%async_computation.3 | async-start | bytes 131072 | tf_op jit(solution)/shard_map/all_to_all | solution.py:377
  89.1 0.0 copy-start.4
  89.1 0.0 copy-start.1
  89.1 3.7 %copy-done.1 = bf16[2,9,512,512]{3,2,1,0:T(8,128)(2,1)S(1)} copy-done((bf16[2,9,512,512]{3,2,1,0:T(8,128)(2,1)S(1)}, bf16[2,9,512,512]{3,2,1,0:T(8,128)(2,1)}, u32[]{:S(2)}) %copy-start.1) | copy-done | bytes 9437208
  92.8 2.3 %near.3 = f32[2,16,512]{2,1,0:T(8,128)S(1)} custom-call(f32[2]{0:T(128)S(1)} %copy-done.7, bf16[9,32,512]{2,1,0:T(8,128)(2,1)S(1)} %bitcast.35, f32[2,16,512]{2,1,0:T(8,128)S(1)} %convert_add_fusion.source, bf16[2,9,512,512]{3,2,1,0:T(8,128)(2,1)S(1)} %copy-done.1), custom_call_target="tpu_custom_call" | custom-call | flops 301989888 | bytes 9437184 | tf_op jit(solution)/shard_map/near/pallas_call | solution.py:264
  95.1 0.6 all-to-all-done.3
  95.7 0.6 bitcast_add_fusion
  (20 shorter events, 0.2 us)
Async XLA Ops:
  1.5 6.8 %collective-permute-start = (f32[32,512]{1,0:T(8,128)S(1)}, f32[32,512]{1,0:T(8,128)S(1)}, u32[]{:S(2)}, u32[]{:S(2)}) collective-permute-start(f32[32,512]{1,0:T(8,128)S(1)} %get-tuple-element.24), channel_id=1, source_target_pairs={{0,8},{4,12},{8,0},{12,4},{1,9},{5,13},{9,1},{13,5},{2,10},{6,14},... | collective-permute-start | bytes 196616 | tf_op jit(solution)/shard_map/ppermute | solution.py:362
  4.5 0.8 copy-start.2
  5.4 0.7 copy-start.5
  6.1 0.7 copy-start.8
  6.8 0.7 copy-start.9
  8.3 9.5 %collective-permute-start.4 = (bf16[32,512]{1,0:T(8,128)(2,1)S(1)}, bf16[32,512]{1,0:T(8,128)(2,1)S(1)}, u32[]{:S(2)}, u32[]{:S(2)}) collective-permute-start(bf16[32,512]{1,0:T(8,128)(2,1)S(1)} %get-tuple-element.15), channel_id=1, source_target_pairs={{0,3},{1,0},{2,1},{3,2},{4,7},{5,4},{6,5},{7,6},{8,11},{9,8},{10,9... | collective-permute-start | bytes 98312 | tf_op jit(solution)/shard_map/ppermute | solution.py:348
  11.9 5.9 %collective-permute-start.3 = (bf16[32,512]{1,0:T(8,128)(2,1)S(1)}, bf16[32,512]{1,0:T(8,128)(2,1)S(1)}, u32[]{:S(2)}, u32[]{:S(2)}) collective-permute-start(bf16[32,512]{1,0:T(8,128)(2,1)S(1)} %get-tuple-element.15), channel_id=1, source_target_pairs={{0,1},{1,2},{2,3},{3,0},{4,5},{5,6},{6,7},{7,4},{8,9},{9,10},{10,1... | collective-permute-start | bytes 98312 | tf_op jit(solution)/shard_map/ppermute | solution.py:348
  11.9 9.1 %collective-permute-start.1 = (f32[2,32,512]{2,1,0:T(8,128)S(1)}, f32[2,32,512]{2,1,0:T(8,128)S(1)}, u32[]{:S(2)}, u32[]{:S(2)}) collective-permute-start(f32[2,32,512]{2,1,0:T(8,128)S(1)} %maximum_select_fusion.4), channel_id=1, source_target_pairs={{0,2},{1,3},{2,0},{3,1},{4,6},{5,7},{6,4},{7,5},{8,10},{9,11},{10,... | collective-permute-start | bytes 393224 | tf_op jit(solution)/shard_map/ppermute | solution.py:362
  12.9 23.8 %all-to-all-start = ((bf16[16,24,512]{2,1,0:T(8,128)(2,1)}), bf16[16,24,512]{2,1,0:T(8,128)(2,1)S(1)}, u32[]{:S(2)}, u32[]{:S(2)}) async-start(bf16[16,24,512]{2,1,0:T(8,128)(2,1)} %get-tuple-element.12), calls=%async_computation | async-start | bytes 786432 | tf_op jit(solution)/shard_map/all_to_all | solution.py:377
  17.8 6.3 %collective-permute-start.6 = (bf16[3,32,512]{2,1,0:T(8,128)(2,1)S(1)}, bf16[3,32,512]{2,1,0:T(8,128)(2,1)S(1)}, u32[]{:S(2)}, u32[]{:S(2)}) collective-permute-start(bf16[3,32,512]{2,1,0:T(8,128)(2,1)S(1)} %get-tuple-element.23), channel_id=1, source_target_pairs={{0,12},{4,0},{8,4},{12,8},{1,13},{5,1},{9,5},{13,9},{2,14},{6,2},{... | collective-permute-start | bytes 294920 | tf_op jit(solution)/shard_map/ppermute | solution.py:348
  19.5 6.6 %collective-permute-start.5 = (bf16[3,32,512]{2,1,0:T(8,128)(2,1)S(1)}, bf16[3,32,512]{2,1,0:T(8,128)(2,1)S(1)}, u32[]{:S(2)}, u32[]{:S(2)}) collective-permute-start(bf16[3,32,512]{2,1,0:T(8,128)(2,1)S(1)} %get-tuple-element.23), channel_id=1, source_target_pairs={{0,4},{4,8},{8,12},{12,0},{1,5},{5,9},{9,13},{13,1},{2,6},{6,10},{... | collective-permute-start | bytes 294920 | tf_op jit(solution)/shard_map/ppermute | solution.py:348
  21.0 13.2 %collective-permute-start.2 = (f32[2,2,32,512]{3,2,1,0:T(8,128)S(1)}, f32[2,2,32,512]{3,2,1,0:T(8,128)S(1)}, u32[]{:S(2)}, u32[]{:S(2)}) collective-permute-start(f32[2,2,32,512]{3,2,1,0:T(8,128)S(1)} %maximum_select_fusion.2), channel_id=1, source_target_pairs={{0,1},{1,0},{2,3},{3,2},{4,5},{5,4},{6,7},{7,6},{8,9},{9,8},{10,11... | collective-permute-start | bytes 786440 | tf_op jit(solution)/shard_map/ppermute | solution.py:362
  26.1 3.7 %copy-start = (bf16[2,9,512,512]{3,2,1,0:T(8,128)(2,1)S(1)}, bf16[2,9,512,512]{3,2,1,0:T(8,128)(2,1)}, u32[]{:S(2)}) copy-start(bf16[2,9,512,512]{3,2,1,0:T(8,128)(2,1)} %blocks.3) | copy-start | bytes 28311556
  29.8 0.8 copy-start.3
  30.6 0.7 copy-start.6
  34.3 2.0 %collective-permute-start.7 = (f32[2,2,2,32,512]{4,3,0,1,2:T(8,128)S(1)}, f32[2,2,2,32,512]{4,3,0,1,2:T(8,128)S(1)}, u32[]{:S(2)}, u32[]{:S(2)}) collective-permute-start(f32[2,2,2,32,512]{4,3,0,1,2:T(8,128)S(1)} %maximum_select_fusion.1), channel_id=1, source_target_pairs={{0,4},{4,0},{8,12},{12,8},{1,5},{5,1},{9,13},{13,9},{2,6},{6,2},{1... | collective-permute-start | bytes 1572872 | tf_op jit(solution)/shard_map/ppermute | solution.py:362
  36.8 22.0 %all-to-all-start.1 = ((f32[16,2,512]{2,1,0:T(2,128)}), f32[16,2,512]{2,1,0:T(2,128)S(1)}, u32[]{:S(2)}, u32[]{:S(2)}) async-start(f32[16,2,512]{2,1,0:T(2,128)} %near.2), calls=%async_computation.1 | async-start | bytes 131072 | tf_op jit(solution)/shard_map/all_to_all | solution.py:377
  42.4 1.6 %copy-start.10 = (bf16[4,2,2,256,256]{4,3,2,1,0:T(8,128)(2,1)S(1)}, bf16[4,2,2,256,256]{4,3,2,1,0:T(8,128)(2,1)}, u32[]{:S(2)}) copy-start(bf16[4,2,2,256,256]{4,3,2,1,0:T(8,128)(2,1)} %constant.70.clone.tab1.tab2) | copy-start | bytes 6291460
  60.0 22.9 %all-to-all-start.2 = ((bf16[16,24,512]{2,1,0:T(8,128)(2,1)}), bf16[16,24,512]{2,1,0:T(8,128)(2,1)S(1)}, u32[]{:S(2)}, u32[]{:S(2)}) async-start(bf16[16,24,512]{2,1,0:T(8,128)(2,1)} %get-tuple-element.18), calls=%async_computation.2 | async-start | bytes 786432 | tf_op jit(solution)/shard_map/all_to_all | solution.py:377
  66.0 1.6 %copy-start.11 = (bf16[4,2,2,256,256]{4,3,2,1,0:T(8,128)(2,1)S(1)}, bf16[4,2,2,256,256]{4,3,2,1,0:T(8,128)(2,1)}, u32[]{:S(2)}) copy-start(bf16[4,2,2,256,256]{4,3,2,1,0:T(8,128)(2,1)} %constant.70.clone.tab1.tab2) | copy-start | bytes 6291460
  67.6 21.5 %copy-start.7 = (f32[2]{0:T(128)S(1)}, f32[2]{0:T(128)}, u32[]{:S(2)}) copy-start(f32[2]{0:T(128)} %bloch.3) | copy-start | bytes 28
  83.1 12.6 %all-to-all-start.3 = ((f32[16,2,512]{2,1,0:T(2,128)}), f32[16,2,512]{2,1,0:T(2,128)S(1)}, u32[]{:S(2)}, u32[]{:S(2)}) async-start(f32[16,2,512]{2,1,0:T(2,128)} %recip.3), calls=%async_computation.3 | async-start | bytes 131072 | tf_op jit(solution)/shard_map/all_to_all | solution.py:377
  89.1 7.3 %copy-start.4 = (f32[2,16,512]{2,1,0:T(8,128)}, f32[2,16,512]{2,1,0:T(8,128)S(1)}, u32[]{:S(2)}) copy-start(f32[2,16,512]{2,1,0:T(8,128)S(1)} %convert_add_fusion.source) | copy-start | bytes 196612
  89.1 3.7 %copy-start.1 = (bf16[2,9,512,512]{3,2,1,0:T(8,128)(2,1)S(1)}, bf16[2,9,512,512]{3,2,1,0:T(8,128)(2,1)}, u32[]{:S(2)}) copy-start(bf16[2,9,512,512]{3,2,1,0:T(8,128)(2,1)} %blocks.3) | copy-start | bytes 28311556

commit v3 on v2

--- a/solution.py
+++ b/solution.py
@@ -11,7 +11,8 @@
 
 STENCIL = 4
 RADIX = 4
-UNROLL = 8
+UNROLL = 16
+MOST_HELD = 20 * 1024 * 1024
 F32 = jnp.float32
 BF = jnp.bfloat16
 AXES = ("tile", "sect")
@@ -50,12 +51,16 @@
 
 def times_right(x, table):
     hi, lo = split(x)
-    return dot(hi, table[0]) + dot(lo, table[0]) + dot(hi, table[1])
+    rows = x.shape[0]
+    y = dot(jnp.concatenate([hi, lo], 0), table[0])
+    return y[:rows] + y[rows:] + dot(hi, table[1])
 
 
 def times_left(table, x):
     hi, lo = split(x)
-    return dot(table[0], hi) + dot(table[0], lo) + dot(table[1], hi)
+    rows = x.shape[0]
+    y = dot(table[...].reshape(2 * rows, rows), hi)
+    return y[:rows] + y[rows:] + dot(table[0], lo)
 
 
 def butterfly(parts, sign):
@@ -76,60 +81,52 @@
     return -(-(rows_dev + STENCIL - 1 + lead) // 8) * 8
 
 
+def held_bytes(shape, rows_dev, n2):
+    blocks, _, panels = shape
+    return blocks * panels * RADIX * (2 * (n2 // RADIX) + 4 * window_rows(rows_dev))
+
+
 def recip_kernel(rows_dev, n1, n2, meta, scale, tab1, tab2, *rest):
-    *source, out, grid, freq, field, ahead = rest
+    keep = held_bytes(meta.shape, rows_dev, n2) <= MOST_HELD
+    *source, out, grid, freq = rest[: len(rest) - 2 * keep]
+    hot, weight = rest[len(rest) - 2 :]
     blocks, _, panels = meta.shape
     q1, q2 = n1 // RADIX, n2 // RADIX
     wide = 2 * q2
     win = window_rows(rows_dev)
 
+    def start_of(block):
+        return pl.multiple_of((block * rows_dev) // 8 * 8, 8)
+
+    grid[...] = jnp.zeros_like(grid)
+
     def describe(block):
         rows = meta[block].astype(F32)
-        weights = rows[2 : 2 + STENCIL * STENCIL]
-        start = (block * rows_dev) // 8 * 8
-        first_row = rows[18:19] + (block * rows_dev - start).astype(F32)
-        col_group, col_rest = rows[19:20], rows[20:21]
+        offset = lax.broadcasted_iota(jnp.int32, (win, panels), 0).astype(F32)
+        offset = offset - (rows[18:19] + (block * rows_dev - start_of(block)).astype(F32))
+        at = [offset == float(a) for a in range(STENCIL)]
         lane = lax.broadcasted_iota(jnp.int32, (q2, panels), 0).astype(F32)
-        hits = [
-            jnp.where(lane == jnp.where(col_rest == float(r), col_group, -1.0), 1.0, 0.0)
-            for r in range(RADIX)
-        ]
-        one_hot = jnp.concatenate(hits, 0).astype(BF)
-        offset = lax.broadcasted_iota(jnp.int32, (win, panels), 0).astype(F32) - first_row
-        at = [offset == float(a) for a in range(STENCIL)]
-        spread = []
-        for b in range(STENCIL):
-            part = jnp.where(at[0], weights[b : b + 1], 0.0)
-            for a in range(1, STENCIL):
-                k = a * STENCIL + b
-                part = jnp.where(at[a], weights[k : k + 1], part)
-            spread.append(part)
-        return rows, pl.multiple_of(start, 8), one_hot, spread
-
-    grid[...] = jnp.zeros_like(grid)
+        for r in range(RADIX):
+            spread = jnp.zeros((win, panels), F32)
+            for a in range(STENCIL):
+                k = 2 + a * RADIX + r
+                spread = jnp.where(at[a], rows[k : k + 1], spread)
+            one_hot = jnp.where(lane == rows[19 + r : 20 + r], 1.0, 0.0).astype(BF)
+            yield r, spread, one_hot
 
     def scatter(block, carry):
-        rows, start, one_hot, spread = describe(block)
-        value = source[0][block].astype(BF).astype(F32) if source else rows[0:2]
-        terms = []
-        for b in range(STENCIL):
+        value = source[0][block].astype(BF).astype(F32) if source else meta[block].astype(F32)[0:2]
+        start = start_of(block)
+        for r, spread, one_hot in describe(block):
+            if keep:
+                weight[block, r] = spread
+                hot[block, r] = one_hot
+            both = jnp.concatenate([spread * value[c : c + 1] for c in range(2)], 0)
+            sums = dot_last(jnp.concatenate(split(both), 0), one_hot)
+            sums = sums[: 2 * win] + sums[2 * win :]
             for c in range(2):
-                product = spread[b] * value[c : c + 1]
-                hi = product.astype(BF).astype(F32)
-                terms += [hi, product - hi]
-        sums = dot_last(jnp.concatenate(terms, 0).astype(BF), one_hot)
-        for r in range(RADIX):
-            for c in range(2):
-                total = None
-                for b in range(STENCIL):
-                    k = (b * 2 + c) * 2 * win
-                    lanes = slice((r - b) % RADIX * q2, ((r - b) % RADIX + 1) * q2)
-                    x = sums[k : k + win, lanes] + sums[k + win : k + 2 * win, lanes]
-                    if r < b:
-                        x = pltpu.roll(x, 1, 1)
-                    total = x if total is None else total + x
                 lanes = slice((r * 2 + c) * q2, (r * 2 + c + 1) * q2)
-                grid[pl.ds(start, win), lanes] += total
+                grid[pl.ds(start, win), lanes] += sums[c * win : (c + 1) * win]
         return carry
 
     lax.fori_loop(0, blocks, scatter, 0, unroll=UNROLL)
@@ -166,33 +163,23 @@
 
     parts = [(freq[2 * m], freq[2 * m + 1]) for m in range(RADIX)]
     for r, both in enumerate(butterfly(parts, 1)):
-        y = times_right(jnp.concatenate(both, 1), tab2.at[r, 1])
-        field[0:n1, r * wide : (r + 1) * wide] = y
-        if r < STENCIL - 1:
+        grid[0:n1, r * wide : (r + 1) * wide] = times_right(jnp.concatenate(both, 1), tab2.at[r, 1])
+    grid[n1 : n1 + win, :] = grid[0:win, :]
+
+    def held(block):
+        for r in range(RADIX):
+            yield r, weight[block, r], hot[block, r]
+
+    def collect(block, carry):
+        start = start_of(block)
+        totals = [jnp.zeros((win, panels), F32)] * 2
+        for r, spread, one_hot in held(block) if keep else describe(block):
+            near = [grid[pl.ds(start, win), (r * 2 + c) * q2 : (r * 2 + c + 1) * q2] for c in range(2)]
+            values = dot(jnp.concatenate(near, 0).astype(BF), one_hot)
             for c in range(2):
-                lanes = slice((r * 2 + c) * q2, (r * 2 + c + 1) * q2)
-                ahead[0:n1, lanes] = pltpu.roll(y[:, c * q2 : (c + 1) * q2], q2 - 1, 1)
-    field[n1 : n1 + win, :] = field[0:win, :]
-    ahead[n1 : n1 + win, :] = ahead[0:win, :]
-
-    def collect(block, carry):
-        _, start, one_hot, spread = describe(block)
-        pieces = []
-        for b in range(STENCIL):
-            for c in range(2):
-                row = []
-                for r in range(b, b + RADIX):
-                    lanes = slice((r % RADIX * 2 + c) * q2, (r % RADIX * 2 + c + 1) * q2)
-                    row.append((field if r < RADIX else ahead)[pl.ds(start, win), lanes])
-                pieces.append(jnp.concatenate(row, 1))
-        values = dot(jnp.concatenate(pieces, 0).astype(BF), one_hot)
+                totals[c] = totals[c] + values[c * win : (c + 1) * win] * spread
         for c in range(2):
-            total = None
-            for b in range(STENCIL):
-                k = (b * 2 + c) * win
-                x = values[k : k + win] * spread[b]
-                total = x if total is None else total + x
-            out[block, c : c + 1] = jnp.sum(total, 0, keepdims=True)
+            out[block, c : c + 1] = jnp.sum(totals[c], 0, keepdims=True)
         return carry
 
     lax.fori_loop(0, blocks, collect, 0, unroll=UNROLL)
@@ -202,6 +189,12 @@
     blocks, _, panels = meta.shape
     n1, n2 = scale.shape
     reach = n1 + window_rows(rows_dev)
+    kept = [
+        pltpu.VMEM((blocks, RADIX, n2 // RADIX, panels), BF),
+        pltpu.VMEM((blocks, RADIX, window_rows(rows_dev), panels), F32),
+    ]
+    if held_bytes(meta.shape, rows_dev, n2) > MOST_HELD:
+        kept = []
     tab1, tab2 = transform_tables(n1), transform_tables(n2)
     in_vmem = pl.BlockSpec(memory_space=pltpu.VMEM)
     return pl.pallas_call(
@@ -212,10 +205,9 @@
         scratch_shapes=[
             pltpu.VMEM((reach, 2 * n2), F32),
             pltpu.VMEM((2 * RADIX, n1, n2 // RADIX), F32),
-            pltpu.VMEM((reach, 2 * n2), F32),
-            pltpu.VMEM((reach, 2 * n2 // RADIX * (STENCIL - 1)), F32),
-        ],
-        compiler_params=pltpu.CompilerParams(vmem_limit_bytes=28 * 1024 * 1024),
+        ]
+        + kept,
+        compiler_params=pltpu.CompilerParams(vmem_limit_bytes=40 * 1024 * 1024),
         cost_estimate=pl.CostEstimate(
             flops=10_000_000_000, bytes_accessed=8_000_000, transcendentals=0
         ),
@@ -312,12 +304,31 @@
     )(part, start)
 
 
-def pack_kernel(rows_dev, source, stencil, first_row, first_col, sent, low):
+def pack_kernel(rows_dev, groups, *refs):
+    given, (sent, low), held, sems = refs[:4], refs[4:6], refs[6:10], refs[10]
+    copies = [pltpu.make_async_copy(given[k], held[k], sems.at[k]) for k in range(4)]
+    for copy in copies:
+        copy.start()
+    for copy in copies:
+        copy.wait()
+    source, stencil, first_row, first_col = held
     probes, panels = source.shape[1:]
     row, col = first_row[...], first_col[...]
-    numbers = [row % rows_dev, col // RADIX, col % RADIX]
-    rows = [stencil[a].astype(F32) for a in range(STENCIL)] + [x.astype(F32) for x in numbers]
-    rows.append(jnp.zeros((3, panels), F32))
+    rest = col % RADIX
+    given = [stencil[a].astype(F32) for a in range(STENCIL)]
+    rows = []
+    for a in range(STENCIL):
+        for r in range(RADIX):
+            taken = given[a][r : r + 1]
+            for k in range(1, RADIX):
+                b = (r - k) % RADIX
+                taken = jnp.where(rest == k, given[a][b : b + 1], taken)
+            rows.append(taken)
+    rows.append((row % rows_dev).astype(F32))
+    for r in range(RADIX):
+        group = col // RADIX + jnp.where(rest > r, 1, 0)
+        rows.append(jnp.where(group == groups, 0, group).astype(F32))
+    rows.append(jnp.zeros((1, panels), F32))
     described = jnp.concatenate(rows, 0)
     for p in range(probes):
         value = [source[c, p : p + 1, :] for c in range(2)]
@@ -326,21 +337,23 @@
         low[c * probes : (c + 1) * probes] = source[c].astype(BF)
 
 
-def pack(rows_dev, source, stencil, grid_row, grid_col):
+def pack(rows_dev, n2, source, stencil, grid_row, grid_col):
     _, probes, panels = source.shape
-    rows = 2 + STENCIL * STENCIL + 6
+    rows = 2 + STENCIL * RADIX + 6
     in_vmem = pl.BlockSpec(memory_space=pltpu.VMEM)
+    given = (source, stencil, grid_row[None], grid_col[None])
     return pl.pallas_call(
-        functools.partial(pack_kernel, rows_dev),
+        functools.partial(pack_kernel, rows_dev, n2 // RADIX),
         out_shape=(
             jax.ShapeDtypeStruct((probes, rows, panels), BF),
             jax.ShapeDtypeStruct((2 * probes, panels), BF),
         ),
-        in_specs=[in_vmem] * 4,
+        in_specs=[pl.BlockSpec(memory_space=pl.ANY)] * 4,
         out_specs=(in_vmem, in_vmem),
-        compiler_params=pltpu.CompilerParams(vmem_limit_bytes=16 * 1024 * 1024),
+        scratch_shapes=[pltpu.VMEM(x.shape, x.dtype) for x in given] + [pltpu.SemaphoreType.DMA((4,))],
+        compiler_params=pltpu.CompilerParams(vmem_limit_bytes=60 * 1024 * 1024),
         name="pack",
-    )(source, stencil, grid_row[None], grid_col[None])
+    )(*given)
 
 
 def shifted(array, axis, by):
@@ -391,7 +404,7 @@
     def to_panels(rows):
         return exchange(rows)[::repeat]
 
-    sent, low = pack(rows_dev, source_probes, stencil, grid_row, grid_col)
+    sent, low = pack(rows_dev, n2, source_probes, stencil, grid_row, grid_col)
     meta = exchange(to_owners(sent))
     steps = doubling_steps()
     kernel_rows = doubled((recip_kernel * (1.0 / (n1 * n2))).T, steps[0])
@@ -399,9 +412,9 @@
     halo = beside(beside(low, "sect"), "tile").reshape(9, 2 * probes, panels)
     for step in steps[1:-1]:
         kernel_rows = doubled(kernel_rows, step)
+    kernel_rows, halo = lax.optimization_barrier((kernel_rows, halo))
+    scale = in_columns(doubled(kernel_rows, steps[-1]), steps)
     first_near = near_apply(halo, near_blocks, bloch_angle, source_probes, True)
-    kernel_rows, first_near = lax.optimization_barrier((kernel_rows, first_near))
-    scale = in_columns(doubled(kernel_rows, steps[-1]), steps)
     start = exchange(to_owners(first_near))
     first_owned, spread = neighbour_rows(recip_apply(meta, scale, rows_dev), start)
     second_owned = recip_apply(meta, scale, rows_dev, first_owned)

time: 97.2 us -> 91.3 us (0.939)
  Pallas kernels: 37.2 us -> 29.4 us
  waiting for transfers between devices: 9.06 us -> 15.2 us
  local copies, waits for them, and re-layouts: 15.4 us -> 12.5 us
  starting transfers between devices: 31.9 us -> 30 us
    pallas_call x2, Pallas kernels: 30 us -> 21.3 us  [recip_apply(): pl.pallas_call(functools.partial(recip_kernel, rows_dev, n1, n2), out_sha...]
    ppermute x4, waiting for transfers between devices: 5.01 us -> 13.7 us  [shifted(): lax.ppermute(array, axis, [(i, (i + by) % count) for i in range(count)])]
    all_to_all x4, starting transfers between devices: 22.4 us -> 19.2 us  [exchange(): return lax.all_to_all(parts, AXES, 0, 0, tiled=True)]
    unnamed x24 -> x16, local copies, waits for them, and re-layouts: 14.9 us -> 12 us
    ppermute x4, waiting for transfers between devices: 3.44 us -> 0.55 us  [doubled(): lax.ppermute(block, axis, [(i, i ^ reach) for i in range(lax.axis_size(ax...]
    ppermute x4, starting transfers between devices: 4.19 us -> 6.55 us  [doubled(): lax.ppermute(block, axis, [(i, i ^ reach) for i in range(lax.axis_size(ax...]
    ppermute x4, starting transfers between devices: 5.32 us -> 4.25 us  [shifted(): lax.ppermute(array, axis, [(i, (i + by) % count) for i in range(count)])]
  transfers between devices with their start and end apart: 12 -> 12, of which waited for: 6 -> 7; matrix products, arithmetic and copies ran while one was open for 1% -> 2% of each run, Pallas kernels for 37% -> 31%
where the time goes in v3:
time: 91.3 us; the launch traced here: 90.5 us
  starting transfers between devices  30 us (33%)
  Pallas kernels  29.4 us (32%)
  waiting for transfers between devices  15.2 us (17%)
  local copies, waits for them, and re-layouts  12.5 us (14%)
  other arithmetic  2.53 us (3%)
    pallas_call x2, Pallas kernels, recip_apply(): pl.pallas_call(functools.partial(recip_kernel, rows_dev, n1, n2), out_sha...  21.3 us
    all_to_all x4, starting transfers between devices, exchange(): return lax.all_to_all(parts, AXES, 0, 0, tiled=True)  19.2 us
    ppermute x4, waiting for transfers between devices, shifted(): lax.ppermute(array, axis, [(i, (i + by) % count) for i in range(count)])  13.7 us
    unnamed x16, local copies, waits for them, and re-layouts  12 us
    ppermute x4, starting transfers between devices, doubled(): lax.ppermute(block, axis, [(i, i ^ reach) for i in range(lax.axis_size(ax...  6.55 us
    pallas_call x2, Pallas kernels, near_apply(): pl.pallas_call(functools.partial(near_kernel, probes_first), out_shape=ja...  5.17 us
    ppermute x4, starting transfers between devices, shifted(): lax.ppermute(array, axis, [(i, (i + by) % count) for i in range(count)])  4.25 us
  transfers between devices with their start and end apart: 12, of which 7 were waited for; matrix products, arithmetic and copies ran while one was open for 2% of the time, Pallas kernels for 31%

profile of v3, /device:TPU:0, one launch (start us, length us, event | category | flops | bytes accessed | tf_op | source)
XLA Modules:
  0.0 90.5 jit_solution(7968248422729309103)
XLA Ops:
  0.6 0.9 multiply_bitcast_fusion.1
  1.5 3.0 %collective-permute-start = (f32[32,512]{1,0:T(8,128)S(1)}, f32[32,512]{1,0:T(8,128)S(1)}, u32[]{:S(2)}, u32[]{:S(2)}) collective-permute-start(f32[32,512]{1,0:T(8,128)S(1)} %get-tuple-element.24), channel_id=1, source_target_pairs={{0,8},{4,12},{8,0},{12,4},{1,9},{5,13},{9,1},{13,5},{2,10},{6,14},... | collective-permute-start | bytes 196616 | tf_op jit(solution)/shard_map/ppermute | solution.py:375
  4.5 1.7 %pack.1 = (bf16[16,24,512]{2,1,0:T(8,128)(2,1)}, bf16[32,512]{1,0:T(8,128)(2,1)}) custom-call(f32[2,16,512]{2,1,0:T(8,128)} %source.1, bf16[4,4,512]{2,1,0:T(4,128)(2,1)} %refs_1_.1, s32[1,512]{1,0:T(1,128)} %bitcast.52, s32[1,512]{1,0:T(1,128)} %bitcast.53), custom_call_target="tpu_custom_call" | custom-call | tf_op jit(solution)/shard_map/pack/pallas_call | solution.py:345
  6.2 0.5 collective-permute-done
  6.8 3.2 %collective-permute-start.1 = (f32[2,32,512]{2,1,0:T(8,128)S(1)}, f32[2,32,512]{2,1,0:T(8,128)S(1)}, u32[]{:S(2)}, u32[]{:S(2)}) collective-permute-start(f32[2,32,512]{2,1,0:T(8,128)S(1)} %maximum_select_fusion.4), channel_id=1, source_target_pairs={{0,2},{1,3},{2,0},{3,1},{4,6},{5,7},{6,4},{7,5},{8,10},{9,11},{10,... | collective-permute-start | bytes 393224 | tf_op jit(solution)/shard_map/ppermute | solution.py:375
  9.9 3.9 %all-to-all-start = ((bf16[16,24,512]{2,1,0:T(8,128)(2,1)}), bf16[16,24,512]{2,1,0:T(8,128)(2,1)S(1)}, u32[]{:S(2)}, u32[]{:S(2)}) async-start(bf16[16,24,512]{2,1,0:T(8,128)(2,1)} %get-tuple-element.12), calls=%async_computation | async-start | bytes 786432 | tf_op jit(solution)/shard_map/all_to_all | solution.py:390
  13.9 3.7 %collective-permute-start.4 = (bf16[32,512]{1,0:T(8,128)(2,1)}, bf16[32,512]{1,0:T(8,128)(2,1)S(1)}, u32[]{:S(2)}, u32[]{:S(2)}) collective-permute-start(bf16[32,512]{1,0:T(8,128)(2,1)} %get-tuple-element.15), channel_id=1, source_target_pairs={{0,3},{1,0},{2,1},{3,2},{4,7},{5,4},{6,5},{7,6},{8,11},{9,8},{10,9... | collective-permute-start | bytes 98312 | tf_op jit(solution)/shard_map/ppermute | solution.py:361
  17.6 0.0 collective-permute-start.3
  17.6 0.0 collective-permute-done.1
  17.6 0.3 collective-permute-start.2
  17.9 5.8 %collective-permute-done.4 = bf16[32,512]{1,0:T(8,128)(2,1)S(1)} collective-permute-done((bf16[32,512]{1,0:T(8,128)(2,1)}, bf16[32,512]{1,0:T(8,128)(2,1)S(1)}, u32[]{:S(2)}, u32[]{:S(2)}) %collective-permute-start.4) | collective-permute-done | bytes 32800 | tf_op jit(solution)/shard_map/ppermute | solution.py:361
  23.7 3.3 %collective-permute-done.3 = bf16[32,512]{1,0:T(8,128)(2,1)S(1)} collective-permute-done((bf16[32,512]{1,0:T(8,128)(2,1)}, bf16[32,512]{1,0:T(8,128)(2,1)S(1)}, u32[]{:S(2)}, u32[]{:S(2)}) %collective-permute-start.3) | collective-permute-done | bytes 32800 | tf_op jit(solution)/shard_map/ppermute | solution.py:361
  27.0 0.8 fusion
  27.8 0.3 collective-permute-start.6
  28.1 0.3 collective-permute-start.5
  28.4 2.2 %collective-permute-done.6 = bf16[3,32,512]{2,1,0:T(8,128)(2,1)S(1)} collective-permute-done((bf16[3,32,512]{2,1,0:T(8,128)(2,1)S(1)}, bf16[3,32,512]{2,1,0:T(8,128)(2,1)S(1)}, u32[]{:S(2)}, u32[]{:S(2)}) %collective-permute-start.6) | collective-permute-done | bytes 98336 | tf_op jit(solution)/shard_map/ppermute | solution.py:361
  30.6 2.4 %collective-permute-done.5 = bf16[3,32,512]{2,1,0:T(8,128)(2,1)S(1)} collective-permute-done((bf16[3,32,512]{2,1,0:T(8,128)(2,1)S(1)}, bf16[3,32,512]{2,1,0:T(8,128)(2,1)S(1)}, u32[]{:S(2)}, u32[]{:S(2)}) %collective-permute-start.5) | collective-permute-done | bytes 98336 | tf_op jit(solution)/shard_map/ppermute | solution.py:361
  33.0 0.0 collective-permute-done.2
  33.1 0.1 collective-permute-start.7
  33.2 0.0 copy-start
  33.2 3.7 %copy-done = bf16[2,9,512,512]{3,2,1,0:T(8,128)(2,1)S(1)} copy-done((bf16[2,9,512,512]{3,2,1,0:T(8,128)(2,1)S(1)}, bf16[2,9,512,512]{3,2,1,0:T(8,128)(2,1)}, u32[]{:S(2)}) %copy-start) | copy-done | bytes 9437208
  36.9 0.8 copy-done.2
  37.7 0.7 copy-done.4
  38.4 2.9 %near.2 = f32[16,2,512]{2,1,0:T(2,128)} custom-call(f32[2]{0:T(128)S(1)} %copy-done.4, bf16[9,32,512]{2,1,0:T(8,128)(2,1)S(1)} %bitcast.34, f32[2,16,512]{2,1,0:T(8,128)S(1)} %copy-done.2, bf16[2,9,512,512]{3,2,1,0:T(8,128)(2,1)S(1)} %copy-done), custom_call_target="tpu_custom_call" | custom-call | flops 301989888 | bytes 9437184 | tf_op jit(solution)/shard_map/near/pallas_call | solution.py:256
  41.3 0.0 collective-permute-done.7
  41.3 0.1 maximum_select_fusion
  41.4 0.3 copy.22.scale
  41.7 0.0 all-to-all-done.meta
  41.7 3.7 %all-to-all-start.1 = ((f32[16,2,512]{2,1,0:T(2,128)}), f32[16,2,512]{2,1,0:T(2,128)S(1)}, u32[]{:S(2)}, u32[]{:S(2)}) async-start(f32[16,2,512]{2,1,0:T(2,128)} %near.2), calls=%async_computation.1 | async-start | bytes 131072 | tf_op jit(solution)/shard_map/all_to_all | solution.py:390
  45.5 0.0 copy-start.6
  45.5 1.6 %copy-done.6 = bf16[4,2,2,256,256]{4,3,2,1,0:T(8,128)(2,1)S(1)} copy-done((bf16[4,2,2,256,256]{4,3,2,1,0:T(8,128)(2,1)S(1)}, bf16[4,2,2,256,256]{4,3,2,1,0:T(8,128)(2,1)}, u32[]{:S(2)}) %copy-start.6) | copy-done | bytes 2097176
  47.1 10.3 %recip.2.part = f32[16,2,512]{2,1,0:T(2,128)S(1)} custom-call(bf16[16,24,512]{2,1,0:T(8,128)(2,1)S(1)} %all-to-all-done.meta, f32[512,512]{1,0:T(8,128)S(1)} %copy.22.scale, bf16[4,2,2,256,256]{4,3,2,1,0:T(8,128)(2,1)S(1)} %copy-done.6, bf16[4,2,2,256,256]{4,3,2,1,0:T(8,128)(2,1)S(1)} %copy-done.6), custom_call_target="tpu_custom_call" | custom-call | flops 10000000000 | bytes 8000000 | tf_op jit(solution)/shard_map/recip/pallas_call | solution.py:200
  57.4 0.0 all-to-all-done.1.start
  57.4 1.2 %neighbour_rows.1 = (f32[16,2,512]{2,1,0:T(2,128)S(1)}, bf16[16,24,512]{2,1,0:T(8,128)(2,1)}) custom-call(f32[16,2,512]{2,1,0:T(2,128)S(1)} %recip.2.part, f32[16,2,512]{2,1,0:T(2,128)S(1)} %all-to-all-done.1.start), custom_call_target="tpu_custom_call" | custom-call | tf_op jit(solution)/shard_map/neighbour_rows/pallas_call | solution.py:294
  58.6 5.9 %all-to-all-start.2 = ((bf16[16,24,512]{2,1,0:T(8,128)(2,1)}), bf16[16,24,512]{2,1,0:T(8,128)(2,1)S(1)}, u32[]{:S(2)}, u32[]{:S(2)}) async-start(bf16[16,24,512]{2,1,0:T(8,128)(2,1)} %get-tuple-element.18), calls=%async_computation.2 | async-start | bytes 786432 | tf_op jit(solution)/shard_map/all_to_all | solution.py:390
  64.5 0.0 copy-start.7
  64.5 1.6 %copy-done.7 = bf16[4,2,2,256,256]{4,3,2,1,0:T(8,128)(2,1)S(1)} copy-done((bf16[4,2,2,256,256]{4,3,2,1,0:T(8,128)(2,1)S(1)}, bf16[4,2,2,256,256]{4,3,2,1,0:T(8,128)(2,1)}, u32[]{:S(2)}) %copy-start.7) | copy-done | bytes 2097176
  66.1 10.9 %recip.3 = f32[16,2,512]{2,1,0:T(2,128)} custom-call(bf16[16,24,512]{2,1,0:T(8,128)(2,1)S(1)} %all-to-all-done.meta, f32[512,512]{1,0:T(8,128)S(1)} %copy.22.scale, bf16[4,2,2,256,256]{4,3,2,1,0:T(8,128)(2,1)S(1)} %copy-done.7, bf16[4,2,2,256,256]{4,3,2,1,0:T(8,128)(2,1)S(1)} %copy-done.7, f32[16,2,512]{2,1,0:T(2,128)S(1)} %get-tuple-element.19.rest_0_), custom_call_target="tpu_custom_call" | custom-call | flops 10000000000 | bytes 8000000 | tf_op jit(solution)/shard_map/recip/pallas_call | solution.py:200
  77.0 0.3 all-to-all-done.2
  77.4 0.1 copy.29
  77.5 5.7 %all-to-all-start.3 = ((f32[16,2,512]{2,1,0:T(2,128)}), f32[16,2,512]{2,1,0:T(2,128)S(1)}, u32[]{:S(2)}, u32[]{:S(2)}) async-start(f32[16,2,512]{2,1,0:T(2,128)} %recip.3), calls=%async_computation.3 | async-start | bytes 131072 | tf_op jit(solution)/shard_map/all_to_all | solution.py:390
  83.2 0.0 copy-start.3
  83.2 0.0 copy-done.5
  83.3 0.0 copy-start.1
  83.3 3.7 %copy-done.1 = bf16[2,9,512,512]{3,2,1,0:T(8,128)(2,1)S(1)} copy-done((bf16[2,9,512,512]{3,2,1,0:T(8,128)(2,1)S(1)}, bf16[2,9,512,512]{3,2,1,0:T(8,128)(2,1)}, u32[]{:S(2)}) %copy-start.1) | copy-done | bytes 9437208
  86.9 2.3 %near.3 = f32[2,16,512]{2,1,0:T(8,128)S(1)} custom-call(f32[2]{0:T(128)S(1)} %copy-done.5, bf16[9,32,512]{2,1,0:T(8,128)(2,1)S(1)} %bitcast.35, f32[2,16,512]{2,1,0:T(8,128)S(1)} %convert_add_fusion.source, bf16[2,9,512,512]{3,2,1,0:T(8,128)(2,1)S(1)} %copy-done.1), custom_call_target="tpu_custom_call" | custom-call | flops 301989888 | bytes 9437184 | tf_op jit(solution)/shard_map/near/pallas_call | solution.py:256
  89.2 0.6 all-to-all-done.3
  89.8 0.6 bitcast_add_fusion
  (12 shorter events, 0.2 us)
Async XLA Ops:
  1.5 5.3 %collective-permute-start = (f32[32,512]{1,0:T(8,128)S(1)}, f32[32,512]{1,0:T(8,128)S(1)}, u32[]{:S(2)}, u32[]{:S(2)}) collective-permute-start(f32[32,512]{1,0:T(8,128)S(1)} %get-tuple-element.24), channel_id=1, source_target_pairs={{0,8},{4,12},{8,0},{12,4},{1,9},{5,13},{9,1},{13,5},{2,10},{6,14},... | collective-permute-start | bytes 196616 | tf_op jit(solution)/shard_map/ppermute | solution.py:375
  6.8 10.8 %collective-permute-start.1 = (f32[2,32,512]{2,1,0:T(8,128)S(1)}, f32[2,32,512]{2,1,0:T(8,128)S(1)}, u32[]{:S(2)}, u32[]{:S(2)}) collective-permute-start(f32[2,32,512]{2,1,0:T(8,128)S(1)} %maximum_select_fusion.4), channel_id=1, source_target_pairs={{0,2},{1,3},{2,0},{3,1},{4,6},{5,7},{6,4},{7,5},{8,10},{9,11},{10,... | collective-permute-start | bytes 393224 | tf_op jit(solution)/shard_map/ppermute | solution.py:375
  9.9 31.8 %all-to-all-start = ((bf16[16,24,512]{2,1,0:T(8,128)(2,1)}), bf16[16,24,512]{2,1,0:T(8,128)(2,1)S(1)}, u32[]{:S(2)}, u32[]{:S(2)}) async-start(bf16[16,24,512]{2,1,0:T(8,128)(2,1)} %get-tuple-element.12), calls=%async_computation | async-start | bytes 786432 | tf_op jit(solution)/shard_map/all_to_all | solution.py:390
  13.9 9.8 %collective-permute-start.4 = (bf16[32,512]{1,0:T(8,128)(2,1)}, bf16[32,512]{1,0:T(8,128)(2,1)S(1)}, u32[]{:S(2)}, u32[]{:S(2)}) collective-permute-start(bf16[32,512]{1,0:T(8,128)(2,1)} %get-tuple-element.15), channel_id=1, source_target_pairs={{0,3},{1,0},{2,1},{3,2},{4,7},{5,4},{6,5},{7,6},{8,11},{9,8},{10,9... | collective-permute-start | bytes 98312 | tf_op jit(solution)/shard_map/ppermute | solution.py:361
  17.6 9.4 %collective-permute-start.3 = (bf16[32,512]{1,0:T(8,128)(2,1)}, bf16[32,512]{1,0:T(8,128)(2,1)S(1)}, u32[]{:S(2)}, u32[]{:S(2)}) collective-permute-start(bf16[32,512]{1,0:T(8,128)(2,1)} %get-tuple-element.15), channel_id=1, source_target_pairs={{0,1},{1,2},{2,3},{3,0},{4,5},{5,6},{6,7},{7,4},{8,9},{9,10},{10,1... | collective-permute-start | bytes 98312 | tf_op jit(solution)/shard_map/ppermute | solution.py:361
  17.6 15.4 %collective-permute-start.2 = (f32[2,2,32,512]{3,2,1,0:T(8,128)S(1)}, f32[2,2,32,512]{3,2,1,0:T(8,128)S(1)}, u32[]{:S(2)}, u32[]{:S(2)}) collective-permute-start(f32[2,2,32,512]{3,2,1,0:T(8,128)S(1)} %maximum_select_fusion.2), channel_id=1, source_target_pairs={{0,1},{1,0},{2,3},{3,2},{4,5},{5,4},{6,7},{7,6},{8,9},{9,8},{10,11... | collective-permute-start | bytes 786440 | tf_op jit(solution)/shard_map/ppermute | solution.py:375
  27.8 2.8 %collective-permute-start.6 = (bf16[3,32,512]{2,1,0:T(8,128)(2,1)S(1)}, bf16[3,32,512]{2,1,0:T(8,128)(2,1)S(1)}, u32[]{:S(2)}, u32[]{:S(2)}) collective-permute-start(bf16[3,32,512]{2,1,0:T(8,128)(2,1)S(1)} %get-tuple-element.23), channel_id=1, source_target_pairs={{0,12},{4,0},{8,4},{12,8},{1,13},{5,1},{9,5},{13,9},{2,14},{6,2},{... | collective-permute-start | bytes 294920 | tf_op jit(solution)/shard_map/ppermute | solution.py:361
  28.1 4.9 %collective-permute-start.5 = (bf16[3,32,512]{2,1,0:T(8,128)(2,1)S(1)}, bf16[3,32,512]{2,1,0:T(8,128)(2,1)S(1)}, u32[]{:S(2)}, u32[]{:S(2)}) collective-permute-start(bf16[3,32,512]{2,1,0:T(8,128)(2,1)S(1)} %get-tuple-element.23), channel_id=1, source_target_pairs={{0,4},{4,8},{8,12},{12,0},{1,5},{5,9},{9,13},{13,1},{2,6},{6,10},{... | collective-permute-start | bytes 294920 | tf_op jit(solution)/shard_map/ppermute | solution.py:361
  33.1 8.2 %collective-permute-start.7 = (f32[2,2,2,32,512]{4,3,0,1,2:T(8,128)S(1)}, f32[2,2,2,32,512]{4,3,0,1,2:T(8,128)S(1)}, u32[]{:S(2)}, u32[]{:S(2)}) collective-permute-start(f32[2,2,2,32,512]{4,3,0,1,2:T(8,128)S(1)} %maximum_select_fusion.1), channel_id=1, source_target_pairs={{0,4},{4,0},{8,12},{12,8},{1,5},{5,1},{9,13},{13,9},{2,6},{6,2},{1... | collective-permute-start | bytes 1572872 | tf_op jit(solution)/shard_map/ppermute | solution.py:375
  33.2 3.7 %copy-start = (bf16[2,9,512,512]{3,2,1,0:T(8,128)(2,1)S(1)}, bf16[2,9,512,512]{3,2,1,0:T(8,128)(2,1)}, u32[]{:S(2)}) copy-start(bf16[2,9,512,512]{3,2,1,0:T(8,128)(2,1)} %blocks.3) | copy-start | bytes 28311556
  36.9 0.8 copy-start.2
  37.7 0.7 copy-start.4
  41.7 15.7 %all-to-all-start.1 = ((f32[16,2,512]{2,1,0:T(2,128)}), f32[16,2,512]{2,1,0:T(2,128)S(1)}, u32[]{:S(2)}, u32[]{:S(2)}) async-start(f32[16,2,512]{2,1,0:T(2,128)} %near.2), calls=%async_computation.1 | async-start | bytes 131072 | tf_op jit(solution)/shard_map/all_to_all | solution.py:390
  45.5 1.6 %copy-start.6 = (bf16[4,2,2,256,256]{4,3,2,1,0:T(8,128)(2,1)S(1)}, bf16[4,2,2,256,256]{4,3,2,1,0:T(8,128)(2,1)}, u32[]{:S(2)}) copy-start(bf16[4,2,2,256,256]{4,3,2,1,0:T(8,128)(2,1)} %constant.70.clone.tab1.tab2) | copy-start | bytes 6291460
  58.6 18.8 %all-to-all-start.2 = ((bf16[16,24,512]{2,1,0:T(8,128)(2,1)}), bf16[16,24,512]{2,1,0:T(8,128)(2,1)S(1)}, u32[]{:S(2)}, u32[]{:S(2)}) async-start(bf16[16,24,512]{2,1,0:T(8,128)(2,1)} %get-tuple-element.18), calls=%async_computation.2 | async-start | bytes 786432 | tf_op jit(solution)/shard_map/all_to_all | solution.py:390
  64.5 1.6 %copy-start.7 = (bf16[4,2,2,256,256]{4,3,2,1,0:T(8,128)(2,1)S(1)}, bf16[4,2,2,256,256]{4,3,2,1,0:T(8,128)(2,1)}, u32[]{:S(2)}) copy-start(bf16[4,2,2,256,256]{4,3,2,1,0:T(8,128)(2,1)} %constant.70.clone.tab1.tab2) | copy-start | bytes 6291460
  66.1 17.1 %copy-start.5 = (f32[2]{0:T(128)S(1)}, f32[2]{0:T(128)}, u32[]{:S(2)}) copy-start(f32[2]{0:T(128)} %bloch.3) | copy-start | bytes 28
  77.5 12.3 %all-to-all-start.3 = ((f32[16,2,512]{2,1,0:T(2,128)}), f32[16,2,512]{2,1,0:T(2,128)S(1)}, u32[]{:S(2)}, u32[]{:S(2)}) async-start(f32[16,2,512]{2,1,0:T(2,128)} %recip.3), calls=%async_computation.3 | async-start | bytes 131072 | tf_op jit(solution)/shard_map/all_to_all | solution.py:390
  83.2 7.3 %copy-start.3 = (f32[2,16,512]{2,1,0:T(8,128)}, f32[2,16,512]{2,1,0:T(8,128)S(1)}, u32[]{:S(2)}) copy-start(f32[2,16,512]{2,1,0:T(8,128)S(1)} %convert_add_fusion.source) | copy-start | bytes 196612
  83.3 3.7 %copy-start.1 = (bf16[2,9,512,512]{3,2,1,0:T(8,128)(2,1)S(1)}, bf16[2,9,512,512]{3,2,1,0:T(8,128)(2,1)}, u32[]{:S(2)}) copy-start(bf16[2,9,512,512]{3,2,1,0:T(8,128)(2,1)} %blocks.3) | copy-start | bytes 28311556

commit v4 on v3

--- a/solution.py
+++ b/solution.py
@@ -366,8 +366,7 @@
 
 
 def doubling_steps():
-    far = [(axis, 2**p) for axis in AXES[::-1] for p in range(1, 12) if 2**p < lax.axis_size(axis)]
-    return far[::-1] + [(axis, 1) for axis in AXES[::-1] if lax.axis_size(axis) > 1]
+    return [(axis, 2**p) for axis in AXES[::-1] for p in range(11, -1, -1) if 2**p < lax.axis_size(axis)]
 
 
 def doubled(block, step):
@@ -405,16 +404,17 @@
         return exchange(rows)[::repeat]
 
     sent, low = pack(rows_dev, n2, source_probes, stencil, grid_row, grid_col)
+    side = beside(low, "sect")
+    steps = doubling_steps()
+    kernel_rows = doubled(recip_kernel.astype(jnp.float16).T, steps[0])
+    kernel_rows, side, sent = lax.optimization_barrier((kernel_rows, side, sent))
     meta = exchange(to_owners(sent))
-    steps = doubling_steps()
-    kernel_rows = doubled((recip_kernel * (1.0 / (n1 * n2))).T, steps[0])
-    kernel_rows, low = lax.optimization_barrier((kernel_rows, low))
-    halo = beside(beside(low, "sect"), "tile").reshape(9, 2 * probes, panels)
+    halo = beside(side, "tile").reshape(9, 2 * probes, panels)
     for step in steps[1:-1]:
         kernel_rows = doubled(kernel_rows, step)
-    kernel_rows, halo = lax.optimization_barrier((kernel_rows, halo))
-    scale = in_columns(doubled(kernel_rows, steps[-1]), steps)
     first_near = near_apply(halo, near_blocks, bloch_angle, source_probes, True)
+    kernel_rows, first_near = lax.optimization_barrier((kernel_rows, first_near))
+    scale = in_columns(doubled(kernel_rows, steps[-1]), steps).astype(F32) * (1.0 / (n1 * n2))
     start = exchange(to_owners(first_near))
     first_owned, spread = neighbour_rows(recip_apply(meta, scale, rows_dev), start)
     second_owned = recip_apply(meta, scale, rows_dev, first_owned)

time: 91.3 us -> 83.4 us (0.913)
  waiting for transfers between devices: 15.2 us -> 8.01 us
    ppermute x4, waiting for transfers between devices: 13.7 us -> 5.21 us  [shifted(): lax.ppermute(array, axis, [(i, (i + by) % count) for i in range(count)])]
    ppermute x4, starting transfers between devices: 4.25 us -> 2.63 us  [shifted(): lax.ppermute(array, axis, [(i, (i + by) % count) for i in range(count)])]
    all_to_all x4, starting transfers between devices: 19.2 us -> 20.3 us  [exchange(): return lax.all_to_all(parts, AXES, 0, 0, tiled=True)]
    ppermute x4, waiting for transfers between devices: 0.55 us -> 1.52 us  [doubled(): lax.ppermute(block, axis, [(i, i ^ reach) for i in range(lax.axis_size(ax...]
  transfers between devices with their start and end apart: 12 -> 12, of which waited for: 7 -> 6; matrix products, arithmetic and copies ran while one was open for 2% -> 1% of each run, Pallas kernels for 31% -> 34%
where the time goes in v4:
time: 83.4 us; the launch traced here: 82.6 us
  Pallas kernels  29.4 us (35%)
  starting transfers between devices  29.1 us (35%)
  local copies, waits for them, and re-layouts  12.5 us (15%)
  waiting for transfers between devices  8.01 us (10%)
  other arithmetic  2.73 us (3%)
  between operations  0.93 us (1%)
    pallas_call x2, Pallas kernels, recip_apply(): pl.pallas_call(functools.partial(recip_kernel, rows_dev, n1, n2), out_sha...  21.3 us
    all_to_all x4, starting transfers between devices, exchange(): return lax.all_to_all(parts, AXES, 0, 0, tiled=True)  20.3 us
    unnamed x16, local copies, waits for them, and re-layouts  12 us
    ppermute x4, starting transfers between devices, doubled(): lax.ppermute(block, axis, [(i, i ^ reach) for i in range(lax.axis_size(ax...  6.17 us
    ppermute x4, waiting for transfers between devices, shifted(): lax.ppermute(array, axis, [(i, (i + by) % count) for i in range(count)])  5.21 us
    pallas_call x2, Pallas kernels, near_apply(): pl.pallas_call(functools.partial(near_kernel, probes_first), out_shape=ja...  5.17 us
    ppermute x4, starting transfers between devices, shifted(): lax.ppermute(array, axis, [(i, (i + by) % count) for i in range(count)])  2.63 us
    pallas_call x1, Pallas kernels, pack(): pl.pallas_call(functools.partial(pack_kernel, rows_dev, n2 // RADIX), out...  1.7 us
  transfers between devices with their start and end apart: 12, of which 6 were waited for; matrix products, arithmetic and copies ran while one was open for 1% of the time, Pallas kernels for 34%

profile of v4, /device:TPU:0, one launch (start us, length us, event | category | flops | bytes accessed | tf_op | source)
XLA Modules:
  0.0 82.6 jit_solution(7618956554618215783)
XLA Ops:
  0.6 0.8 %convert_bitcast_fusion.1 = (f16[32,512]{1,0:T(8,128)(2,1)S(1)}, f16[1,32,512]{2,1,0:T(8,128)(2,1)S(1)}) fusion(f32[512,32]{0,1:T(8,128)} %param.17), kind=kLoop, calls=%fused_computation.13 | loop fusion | flops 16384 | bytes 131072 | tf_op jit(solution)/shard_map/transpose | solution.py:409
  1.5 4.0 %collective-permute-start = (f16[32,512]{1,0:T(8,128)(2,1)S(1)}, f16[32,512]{1,0:T(8,128)(2,1)S(1)}, u32[]{:S(2)}, u32[]{:S(2)}) collective-permute-start(f16[32,512]{1,0:T(8,128)(2,1)S(1)} %get-tuple-element.24), channel_id=1, source_target_pairs={{0,2},{1,3},{2,0},{3,1},{4,6},{5,7},{6,4},{7,5},{8,10},{9,11},{10,... | collective-permute-start | bytes 98312 | tf_op jit(solution)/shard_map/ppermute | solution.py:374
  5.5 1.7 %pack.1 = (bf16[16,24,512]{2,1,0:T(8,128)(2,1)}, bf16[32,512]{1,0:T(8,128)(2,1)}) custom-call(f32[2,16,512]{2,1,0:T(8,128)} %source.1, bf16[4,4,512]{2,1,0:T(4,128)(2,1)} %refs_1_.1, s32[1,512]{1,0:T(1,128)} %bitcast.52, s32[1,512]{1,0:T(1,128)} %bitcast.53), custom_call_target="tpu_custom_call" | custom-call | tf_op jit(solution)/shard_map/pack/pallas_call | solution.py:345
  7.2 1.4 %collective-permute-start.2 = (bf16[32,512]{1,0:T(8,128)(2,1)}, bf16[32,512]{1,0:T(8,128)(2,1)S(1)}, u32[]{:S(2)}, u32[]{:S(2)}) collective-permute-start(bf16[32,512]{1,0:T(8,128)(2,1)} %get-tuple-element.13), channel_id=1, source_target_pairs={{0,3},{1,0},{2,1},{3,2},{4,7},{5,4},{6,5},{7,6},{8,11},{9,8},{10,9... | collective-permute-start | bytes 98312 | tf_op jit(solution)/shard_map/ppermute | solution.py:361
  8.6 0.7 collective-permute-start.1
  9.3 0.0 collective-permute-done
  9.3 2.1 %collective-permute-done.2 = bf16[32,512]{1,0:T(8,128)(2,1)S(1)} collective-permute-done((bf16[32,512]{1,0:T(8,128)(2,1)}, bf16[32,512]{1,0:T(8,128)(2,1)S(1)}, u32[]{:S(2)}, u32[]{:S(2)}) %collective-permute-start.2) | collective-permute-done | bytes 32800 | tf_op jit(solution)/shard_map/ppermute | solution.py:361
  11.4 3.1 %collective-permute-done.1 = bf16[32,512]{1,0:T(8,128)(2,1)S(1)} collective-permute-done((bf16[32,512]{1,0:T(8,128)(2,1)}, bf16[32,512]{1,0:T(8,128)(2,1)S(1)}, u32[]{:S(2)}, u32[]{:S(2)}) %collective-permute-start.1) | collective-permute-done | bytes 32800 | tf_op jit(solution)/shard_map/ppermute | solution.py:361
  14.5 0.8 pad_maximum_fusion.1
  15.3 0.1 collective-permute-start.3
  15.4 0.1 collective-permute-start.6
  15.5 0.5 collective-permute-start.5
  16.0 4.3 %all-to-all-start = ((bf16[16,24,512]{2,1,0:T(8,128)(2,1)}), bf16[16,24,512]{2,1,0:T(8,128)(2,1)S(1)}, u32[]{:S(2)}, u32[]{:S(2)}) async-start(bf16[16,24,512]{2,1,0:T(8,128)(2,1)} %get-tuple-element.15), calls=%async_computation | async-start | bytes 786432 | tf_op jit(solution)/shard_map/all_to_all | solution.py:389
  20.3 0.0 collective-permute-done.3
  20.3 0.1 maximum_select_fusion.2
  20.3 2.0 %collective-permute-start.4 = (f16[2,2,32,512]{3,2,1,0:T(8,128)(2,1)S(1)}, f16[2,2,32,512]{3,2,1,0:T(8,128)(2,1)S(1)}, u32[]{:S(2)}, u32[]{:S(2)}) collective-permute-start(f16[2,2,32,512]{3,2,1,0:T(8,128)(2,1)S(1)} %maximum_select_fusion.2), channel_id=1, source_target_pairs={{0,8},{4,12},{8,0},{12,4},{1,9},{5,13},{9,1},{13,5},{2,10},{6,14},... | collective-permute-start | bytes 393224 | tf_op jit(solution)/shard_map/ppermute | solution.py:374
  22.3 0.1 maximum_select_fusion.3
  22.4 0.0 collective-permute-done.6
  22.5 0.0 copy-start
  22.5 3.7 %copy-done = bf16[2,9,512,512]{3,2,1,0:T(8,128)(2,1)S(1)} copy-done((bf16[2,9,512,512]{3,2,1,0:T(8,128)(2,1)S(1)}, bf16[2,9,512,512]{3,2,1,0:T(8,128)(2,1)}, u32[]{:S(2)}) %copy-start) | copy-done | bytes 9437208
  26.1 0.8 %copy-done.2 = f32[2,16,512]{2,1,0:T(8,128)S(1)} copy-done((f32[2,16,512]{2,1,0:T(8,128)S(1)}, f32[2,16,512]{2,1,0:T(8,128)}, u32[]{:S(2)}) %copy-start.2) | copy-done | bytes 65560
  27.0 0.7 copy-done.4
  27.6 2.9 %near.2 = f32[16,2,512]{2,1,0:T(2,128)} custom-call(f32[2]{0:T(128)S(1)} %copy-done.4, bf16[9,32,512]{2,1,0:T(8,128)(2,1)S(1)} %bitcast.33, f32[2,16,512]{2,1,0:T(8,128)S(1)} %copy-done.2, bf16[2,9,512,512]{3,2,1,0:T(8,128)(2,1)S(1)} %copy-done), custom_call_target="tpu_custom_call" | custom-call | flops 301989888 | bytes 9437184 | tf_op jit(solution)/shard_map/near/pallas_call | solution.py:256
  30.6 0.1 maximum_select_fusion.1
  30.7 0.1 collective-permute-start.7
  30.8 1.5 %collective-permute-done.7 = f16[2,2,2,32,512]{4,3,1,2,0:T(8,128)(2,1)S(1)} collective-permute-done((f16[2,2,2,32,512]{4,3,1,2,0:T(8,128)(2,1)S(1)}, f16[2,2,2,32,512]{4,3,1,2,0:T(8,128)(2,1)S(1)}, u32[]{:S(2)}, u32[]{:S(2)}) %collective-permute-start.7) | collective-permute-done | bytes 262176 | tf_op jit(solution)/shard_map/ppermute | solution.py:374
  32.3 0.2 convert_multiply_fusion
  32.5 0.3 copy.22.scale
  32.8 0.3 all-to-all-done.meta
  33.1 4.3 %all-to-all-start.1 = ((f32[16,2,512]{2,1,0:T(2,128)}), f32[16,2,512]{2,1,0:T(2,128)S(1)}, u32[]{:S(2)}, u32[]{:S(2)}) async-start(f32[16,2,512]{2,1,0:T(2,128)} %near.2), calls=%async_computation.1 | async-start | bytes 131072 | tf_op jit(solution)/shard_map/all_to_all | solution.py:389
  37.5 0.0 copy-start.6
  37.5 1.6 %copy-done.6 = bf16[4,2,2,256,256]{4,3,2,1,0:T(8,128)(2,1)S(1)} copy-done((bf16[4,2,2,256,256]{4,3,2,1,0:T(8,128)(2,1)S(1)}, bf16[4,2,2,256,256]{4,3,2,1,0:T(8,128)(2,1)}, u32[]{:S(2)}) %copy-start.6) | copy-done | bytes 2097176
  39.1 10.3 %recip.2.part = f32[16,2,512]{2,1,0:T(2,128)S(1)} custom-call(bf16[16,24,512]{2,1,0:T(8,128)(2,1)S(1)} %all-to-all-done.meta, f32[512,512]{1,0:T(8,128)S(1)} %copy.22.scale, bf16[4,2,2,256,256]{4,3,2,1,0:T(8,128)(2,1)S(1)} %copy-done.6, bf16[4,2,2,256,256]{4,3,2,1,0:T(8,128)(2,1)S(1)} %copy-done.6), custom_call_target="tpu_custom_call" | custom-call | flops 10000000000 | bytes 8000000 | tf_op jit(solution)/shard_map/recip/pallas_call | solution.py:200
  49.4 0.0 all-to-all-done.1.start
  49.4 1.2 %neighbour_rows.1 = (f32[16,2,512]{2,1,0:T(2,128)S(1)}, bf16[16,24,512]{2,1,0:T(8,128)(2,1)}) custom-call(f32[16,2,512]{2,1,0:T(2,128)S(1)} %recip.2.part, f32[16,2,512]{2,1,0:T(2,128)S(1)} %all-to-all-done.1.start), custom_call_target="tpu_custom_call" | custom-call | tf_op jit(solution)/shard_map/neighbour_rows/pallas_call | solution.py:294
  50.7 6.0 %all-to-all-start.2 = ((bf16[16,24,512]{2,1,0:T(8,128)(2,1)}), bf16[16,24,512]{2,1,0:T(8,128)(2,1)S(1)}, u32[]{:S(2)}, u32[]{:S(2)}) async-start(bf16[16,24,512]{2,1,0:T(8,128)(2,1)} %get-tuple-element.20), calls=%async_computation.2 | async-start | bytes 786432 | tf_op jit(solution)/shard_map/all_to_all | solution.py:389
  56.7 0.0 copy-start.7
  56.7 1.6 %copy-done.7 = bf16[4,2,2,256,256]{4,3,2,1,0:T(8,128)(2,1)S(1)} copy-done((bf16[4,2,2,256,256]{4,3,2,1,0:T(8,128)(2,1)S(1)}, bf16[4,2,2,256,256]{4,3,2,1,0:T(8,128)(2,1)}, u32[]{:S(2)}) %copy-start.7) | copy-done | bytes 2097176
  58.3 10.9 %recip.3 = f32[16,2,512]{2,1,0:T(2,128)} custom-call(bf16[16,24,512]{2,1,0:T(8,128)(2,1)S(1)} %all-to-all-done.meta, f32[512,512]{1,0:T(8,128)S(1)} %copy.22.scale, bf16[4,2,2,256,256]{4,3,2,1,0:T(8,128)(2,1)S(1)} %copy-done.7, bf16[4,2,2,256,256]{4,3,2,1,0:T(8,128)(2,1)S(1)} %copy-done.7, f32[16,2,512]{2,1,0:T(2,128)S(1)} %get-tuple-element.21.rest_0_), custom_call_target="tpu_custom_call" | custom-call | flops 10000000000 | bytes 8000000 | tf_op jit(solution)/shard_map/recip/pallas_call | solution.py:200
  69.2 0.3 all-to-all-done.2
  69.5 0.1 copy.29
  69.7 5.7 %all-to-all-start.3 = ((f32[16,2,512]{2,1,0:T(2,128)}), f32[16,2,512]{2,1,0:T(2,128)S(1)}, u32[]{:S(2)}, u32[]{:S(2)}) async-start(f32[16,2,512]{2,1,0:T(2,128)} %recip.3), calls=%async_computation.3 | async-start | bytes 131072 | tf_op jit(solution)/shard_map/all_to_all | solution.py:389
  75.4 0.0 copy-start.3
  75.4 0.0 copy-start.1
  75.4 3.7 %copy-done.1 = bf16[2,9,512,512]{3,2,1,0:T(8,128)(2,1)S(1)} copy-done((bf16[2,9,512,512]{3,2,1,0:T(8,128)(2,1)S(1)}, bf16[2,9,512,512]{3,2,1,0:T(8,128)(2,1)}, u32[]{:S(2)}) %copy-start.1) | copy-done | bytes 9437208
  79.1 2.3 %near.3 = f32[2,16,512]{2,1,0:T(8,128)S(1)} custom-call(f32[2]{0:T(128)S(1)} %copy-done.5, bf16[9,32,512]{2,1,0:T(8,128)(2,1)S(1)} %bitcast.34, f32[2,16,512]{2,1,0:T(8,128)S(1)} %convert_add_fusion.source, bf16[2,9,512,512]{3,2,1,0:T(8,128)(2,1)S(1)} %copy-done.1), custom_call_target="tpu_custom_call" | custom-call | flops 301989888 | bytes 9437184 | tf_op jit(solution)/shard_map/near/pallas_call | solution.py:256
  81.4 0.6 all-to-all-done.3
  82.0 0.6 bitcast_add_fusion
  (12 shorter events, 0.1 us)
Async XLA Ops:
  1.5 7.8 %collective-permute-start = (f16[32,512]{1,0:T(8,128)(2,1)S(1)}, f16[32,512]{1,0:T(8,128)(2,1)S(1)}, u32[]{:S(2)}, u32[]{:S(2)}) collective-permute-start(f16[32,512]{1,0:T(8,128)(2,1)S(1)} %get-tuple-element.24), channel_id=1, source_target_pairs={{0,2},{1,3},{2,0},{3,1},{4,6},{5,7},{6,4},{7,5},{8,10},{9,11},{10,... | collective-permute-start | bytes 98312 | tf_op jit(solution)/shard_map/ppermute | solution.py:374
  7.2 4.2 %collective-permute-start.2 = (bf16[32,512]{1,0:T(8,128)(2,1)}, bf16[32,512]{1,0:T(8,128)(2,1)S(1)}, u32[]{:S(2)}, u32[]{:S(2)}) collective-permute-start(bf16[32,512]{1,0:T(8,128)(2,1)} %get-tuple-element.13), channel_id=1, source_target_pairs={{0,3},{1,0},{2,1},{3,2},{4,7},{5,4},{6,5},{7,6},{8,11},{9,8},{10,9... | collective-permute-start | bytes 98312 | tf_op jit(solution)/shard_map/ppermute | solution.py:361
  8.6 5.9 %collective-permute-start.1 = (bf16[32,512]{1,0:T(8,128)(2,1)}, bf16[32,512]{1,0:T(8,128)(2,1)S(1)}, u32[]{:S(2)}, u32[]{:S(2)}) collective-permute-start(bf16[32,512]{1,0:T(8,128)(2,1)} %get-tuple-element.13), channel_id=1, source_target_pairs={{0,1},{1,2},{2,3},{3,0},{4,5},{5,6},{6,7},{7,4},{8,9},{9,10},{10,1... | collective-permute-start | bytes 98312 | tf_op jit(solution)/shard_map/ppermute | solution.py:361
  15.3 4.9 %collective-permute-start.3 = (f16[2,32,512]{2,1,0:T(8,128)(2,1)S(1)}, f16[2,32,512]{2,1,0:T(8,128)(2,1)S(1)}, u32[]{:S(2)}, u32[]{:S(2)}) collective-permute-start(f16[2,32,512]{2,1,0:T(8,128)(2,1)S(1)} %maximum_select_fusion.4), channel_id=1, source_target_pairs={{0,1},{1,0},{2,3},{3,2},{4,5},{5,4},{6,7},{7,6},{8,9},{9,8},{10,11... | collective-permute-start | bytes 196616 | tf_op jit(solution)/shard_map/ppermute | solution.py:374
  15.4 6.9 %collective-permute-start.6 = (bf16[3,32,512]{2,1,0:T(8,128)(2,1)S(1)}, bf16[3,32,512]{2,1,0:T(8,128)(2,1)S(1)}, u32[]{:S(2)}, u32[]{:S(2)}) collective-permute-start(bf16[3,32,512]{2,1,0:T(8,128)(2,1)S(1)} %pad_maximum_fusion.1), channel_id=1, source_target_pairs={{0,12},{4,0},{8,4},{12,8},{1,13},{5,1},{9,5},{13,9},{2,14},{6,2},{... | collective-permute-start | bytes 294920 | tf_op jit(solution)/shard_map/ppermute | solution.py:361
  15.5 6.9 %collective-permute-start.5 = (bf16[3,32,512]{2,1,0:T(8,128)(2,1)S(1)}, bf16[3,32,512]{2,1,0:T(8,128)(2,1)S(1)}, u32[]{:S(2)}, u32[]{:S(2)}) collective-permute-start(bf16[3,32,512]{2,1,0:T(8,128)(2,1)S(1)} %pad_maximum_fusion.1), channel_id=1, source_target_pairs={{0,4},{4,8},{8,12},{12,0},{1,5},{5,9},{9,13},{13,1},{2,6},{6,10},{... | collective-permute-start | bytes 294920 | tf_op jit(solution)/shard_map/ppermute | solution.py:361
  16.0 17.1 %all-to-all-start = ((bf16[16,24,512]{2,1,0:T(8,128)(2,1)}), bf16[16,24,512]{2,1,0:T(8,128)(2,1)S(1)}, u32[]{:S(2)}, u32[]{:S(2)}) async-start(bf16[16,24,512]{2,1,0:T(8,128)(2,1)} %get-tuple-element.15), calls=%async_computation | async-start | bytes 786432 | tf_op jit(solution)/shard_map/all_to_all | solution.py:389
  20.3 10.2 %collective-permute-start.4 = (f16[2,2,32,512]{3,2,1,0:T(8,128)(2,1)S(1)}, f16[2,2,32,512]{3,2,1,0:T(8,128)(2,1)S(1)}, u32[]{:S(2)}, u32[]{:S(2)}) collective-permute-start(f16[2,2,32,512]{3,2,1,0:T(8,128)(2,1)S(1)} %maximum_select_fusion.2), channel_id=1, source_target_pairs={{0,8},{4,12},{8,0},{12,4},{1,9},{5,13},{9,1},{13,5},{2,10},{6,14},... | collective-permute-start | bytes 393224 | tf_op jit(solution)/shard_map/ppermute | solution.py:374
  22.5 3.7 %copy-start = (bf16[2,9,512,512]{3,2,1,0:T(8,128)(2,1)S(1)}, bf16[2,9,512,512]{3,2,1,0:T(8,128)(2,1)}, u32[]{:S(2)}) copy-start(bf16[2,9,512,512]{3,2,1,0:T(8,128)(2,1)} %blocks.3) | copy-start | bytes 28311556
  26.1 0.8 %copy-start.2 = (f32[2,16,512]{2,1,0:T(8,128)S(1)}, f32[2,16,512]{2,1,0:T(8,128)}, u32[]{:S(2)}) copy-start(f32[2,16,512]{2,1,0:T(8,128)} %source.1) | copy-start | bytes 196612
  27.0 0.7 copy-start.4
  30.7 1.6 %collective-permute-start.7 = (f16[2,2,2,32,512]{4,3,1,2,0:T(8,128)(2,1)S(1)}, f16[2,2,2,32,512]{4,3,1,2,0:T(8,128)(2,1)S(1)}, u32[]{:S(2)}, u32[]{:S(2)}) collective-permute-start(f16[2,2,2,32,512]{4,3,1,2,0:T(8,128)(2,1)S(1)} %maximum_select_fusion.1), channel_id=1, source_target_pairs={{0,4},{4,0},{8,12},{12,8},{1,5},{5,1},{9,13},{13,9},{2,6},{6,2},{1... | collective-permute-start | bytes 786440 | tf_op jit(solution)/shard_map/ppermute | solution.py:374
  33.1 16.3 %all-to-all-start.1 = ((f32[16,2,512]{2,1,0:T(2,128)}), f32[16,2,512]{2,1,0:T(2,128)S(1)}, u32[]{:S(2)}, u32[]{:S(2)}) async-start(f32[16,2,512]{2,1,0:T(2,128)} %near.2), calls=%async_computation.1 | async-start | bytes 131072 | tf_op jit(solution)/shard_map/all_to_all | solution.py:389
  37.5 1.6 %copy-start.6 = (bf16[4,2,2,256,256]{4,3,2,1,0:T(8,128)(2,1)S(1)}, bf16[4,2,2,256,256]{4,3,2,1,0:T(8,128)(2,1)}, u32[]{:S(2)}) copy-start(bf16[4,2,2,256,256]{4,3,2,1,0:T(8,128)(2,1)} %constant.70.clone.tab1.tab2) | copy-start | bytes 6291460
  50.7 18.9 %all-to-all-start.2 = ((bf16[16,24,512]{2,1,0:T(8,128)(2,1)}), bf16[16,24,512]{2,1,0:T(8,128)(2,1)S(1)}, u32[]{:S(2)}, u32[]{:S(2)}) async-start(bf16[16,24,512]{2,1,0:T(8,128)(2,1)} %get-tuple-element.20), calls=%async_computation.2 | async-start | bytes 786432 | tf_op jit(solution)/shard_map/all_to_all | solution.py:389
  56.7 1.6 %copy-start.7 = (bf16[4,2,2,256,256]{4,3,2,1,0:T(8,128)(2,1)S(1)}, bf16[4,2,2,256,256]{4,3,2,1,0:T(8,128)(2,1)}, u32[]{:S(2)}) copy-start(bf16[4,2,2,256,256]{4,3,2,1,0:T(8,128)(2,1)} %constant.70.clone.tab1.tab2) | copy-start | bytes 6291460
  58.3 17.1 %copy-start.5 = (f32[2]{0:T(128)S(1)}, f32[2]{0:T(128)}, u32[]{:S(2)}) copy-start(f32[2]{0:T(128)} %bloch.3) | copy-start | bytes 28
  69.7 12.3 %all-to-all-start.3 = ((f32[16,2,512]{2,1,0:T(2,128)}), f32[16,2,512]{2,1,0:T(2,128)S(1)}, u32[]{:S(2)}, u32[]{:S(2)}) async-start(f32[16,2,512]{2,1,0:T(2,128)} %recip.3), calls=%async_computation.3 | async-start | bytes 131072 | tf_op jit(solution)/shard_map/all_to_all | solution.py:389
  75.4 7.3 %copy-start.3 = (f32[2,16,512]{2,1,0:T(8,128)}, f32[2,16,512]{2,1,0:T(8,128)S(1)}, u32[]{:S(2)}) copy-start(f32[2,16,512]{2,1,0:T(8,128)S(1)} %convert_add_fusion.source) | copy-start | bytes 196612
  75.4 3.7 %copy-start.1 = (bf16[2,9,512,512]{3,2,1,0:T(8,128)(2,1)S(1)}, bf16[2,9,512,512]{3,2,1,0:T(8,128)(2,1)}, u32[]{:S(2)}) copy-start(bf16[2,9,512,512]{3,2,1,0:T(8,128)(2,1)} %blocks.3) | copy-start | bytes 28311556

commit v5 on v4

--- a/solution.py
+++ b/solution.py
@@ -30,10 +30,20 @@
     tables = []
     for r in range(RADIX):
         angle = 2 * np.pi / length * (((RADIX * index[:, None] + r) * index[None, :]) % length)
-        c, s = np.cos(angle), np.sin(angle)
-        full = np.block([[c, -s], [s, c]])
-        tables.append(np.stack([split_host(full), split_host(full.T)]))
+        both = [np.cos(angle), np.sin(angle)]
+        tables.append(
+            np.stack([np.stack([split_host(x) for x in both]), np.stack([split_host(x.T) for x in both])])
+        )
     return np.stack(tables)
+
+
+def full_table(table, transposed):
+    full = []
+    for part in range(2):
+        c, s = table[transposed, 0, part], table[transposed, 1, part]
+        up, down = (s, -s) if transposed else (-s, s)
+        full.append(jnp.concatenate([jnp.concatenate([c, up], 1), jnp.concatenate([down, c], 1)], 0))
+    return full
 
 
 def dot(a, b):
@@ -59,7 +69,7 @@
 def times_left(table, x):
     hi, lo = split(x)
     rows = x.shape[0]
-    y = dot(table[...].reshape(2 * rows, rows), hi)
+    y = dot(jnp.concatenate(table, 0), hi)
     return y[:rows] + y[rows:] + dot(table[0], lo)
 
 
@@ -134,7 +144,7 @@
 
     parts = []
     for r in range(RADIX):
-        y = times_right(grid[0:n1, r * wide : (r + 1) * wide], tab2.at[r, 0])
+        y = times_right(grid[0:n1, r * wide : (r + 1) * wide], full_table(tab2.at[r], 0))
         parts.append((y[:, :q2], y[:, q2:]))
     for m, (real, imag) in enumerate(butterfly(parts, -1)):
         freq[2 * m] = real
@@ -148,14 +158,14 @@
                 jnp.concatenate([freq[2 * pair + c, rows, :], freq[2 * pair + 2 + c, rows, :]], 1)
                 for c in range(2)
             ]
-            y = times_left(tab1.at[r, 1], jnp.concatenate(both, 0))
+            y = times_left(full_table(tab1.at[r], 1), jnp.concatenate(both, 0))
             parts.append((y[:q1], y[q1:]))
         scaled = []
         for m, (real, imag) in enumerate(butterfly(parts, -1)):
             k = scale[m * q1 : (m + 1) * q1, pair * q2 : (pair + 2) * q2]
             scaled.append((real * k, imag * k))
         for r, both in enumerate(butterfly(scaled, 1)):
-            y = times_left(tab1.at[r, 0], jnp.concatenate(both, 0))
+            y = times_left(full_table(tab1.at[r], 0), jnp.concatenate(both, 0))
             rows = pl.ds(r, q1, stride=RADIX)
             for c in range(2):
                 freq[2 * pair + c, rows, :] = y[c * q1 : (c + 1) * q1, :q2]
@@ -163,7 +173,7 @@
 
     parts = [(freq[2 * m], freq[2 * m + 1]) for m in range(RADIX)]
     for r, both in enumerate(butterfly(parts, 1)):
-        grid[0:n1, r * wide : (r + 1) * wide] = times_right(jnp.concatenate(both, 1), tab2.at[r, 1])
+        grid[0:n1, r * wide : (r + 1) * wide] = times_right(jnp.concatenate(both, 1), full_table(tab2.at[r], 1))
     grid[n1 : n1 + win, :] = grid[0:win, :]
 
     def held(block):
@@ -404,10 +414,10 @@
         return exchange(rows)[::repeat]
 
     sent, low = pack(rows_dev, n2, source_probes, stencil, grid_row, grid_col)
-    side = beside(low, "sect")
     steps = doubling_steps()
     kernel_rows = doubled(recip_kernel.astype(jnp.float16).T, steps[0])
-    kernel_rows, side, sent = lax.optimization_barrier((kernel_rows, side, sent))
+    kernel_rows, sent = lax.optimization_barrier((kernel_rows, sent))
+    side = beside(low, "sect")
     meta = exchange(to_owners(sent))
     halo = beside(side, "tile").reshape(9, 2 * probes, panels)
     for step in steps[1:-1]:

time: 83.4 us -> 79.7 us (0.956)
  local copies, waits for them, and re-layouts: 12.5 us -> 9.36 us
    unnamed x16 -> x14, local copies, waits for them, and re-layouts: 12 us -> 8.86 us
    all_to_all x4, starting transfers between devices: 20.3 us -> 18.1 us  [exchange(): return lax.all_to_all(parts, AXES, 0, 0, tiled=True)]
    ppermute x4, waiting for transfers between devices: 5.21 us -> 3.57 us  [shifted(): lax.ppermute(array, axis, [(i, (i + by) % count) for i in range(count)])]
    ppermute x4, starting transfers between devices: 6.17 us -> 7.66 us  [doubled(): lax.ppermute(block, axis, [(i, i ^ reach) for i in range(lax.axis_size(ax...]
    all_to_all x4, waiting for transfers between devices: 1.27 us -> 2.76 us  [exchange(): return lax.all_to_all(parts, AXES, 0, 0, tiled=True)]
  transfers between devices with their start and end apart: 12 -> 12, of which waited for: 6 -> 6; matrix products, arithmetic and copies ran while one was open for 1% -> 2% of each run, Pallas kernels for 34% -> 36%
where the time goes in v5:
time: 79.7 us; the launch traced here: 78.9 us
  Pallas kernels  29.6 us (37%)
  starting transfers between devices  28.4 us (36%)
  local copies, waits for them, and re-layouts  9.36 us (12%)
  waiting for transfers between devices  7.85 us (10%)
  other arithmetic  2.82 us (4%)
  between operations  0.88 us (1%)
    pallas_call x2, Pallas kernels, recip_apply(): pl.pallas_call(functools.partial(recip_kernel, rows_dev, n1, n2), out_sha...  21.5 us
    all_to_all x4, starting transfers between devices, exchange(): return lax.all_to_all(parts, AXES, 0, 0, tiled=True)  18.1 us
    unnamed x14, local copies, waits for them, and re-layouts  8.86 us
    ppermute x4, starting transfers between devices, doubled(): lax.ppermute(block, axis, [(i, i ^ reach) for i in range(lax.axis_size(ax...  7.66 us
    pallas_call x2, Pallas kernels, near_apply(): pl.pallas_call(functools.partial(near_kernel, probes_first), out_shape=ja...  5.17 us
    ppermute x4, waiting for transfers between devices, shifted(): lax.ppermute(array, axis, [(i, (i + by) % count) for i in range(count)])  3.57 us
    all_to_all x4, waiting for transfers between devices, exchange(): return lax.all_to_all(parts, AXES, 0, 0, tiled=True)  2.76 us
    ppermute x4, starting transfers between devices, shifted(): lax.ppermute(array, axis, [(i, (i + by) % count) for i in range(count)])  2.63 us
  transfers between devices with their start and end apart: 12, of which 6 were waited for; matrix products, arithmetic and copies ran while one was open for 2% of the time, Pallas kernels for 36%

profile of v5, /device:TPU:0, one launch (start us, length us, event | category | flops | bytes accessed | tf_op | source)
XLA Modules:
  0.0 78.9 jit_solution(15690288230483788276)
XLA Ops:
  0.6 0.0 copy-start.6
  0.6 0.9 %convert_bitcast_fusion.1 = (f16[32,512]{1,0:T(8,128)(2,1)S(1)}, f16[1,32,512]{2,1,0:T(8,128)(2,1)S(1)}) fusion(f32[512,32]{0,1:T(8,128)} %param.17), kind=kLoop, calls=%fused_computation.13 | loop fusion | flops 16384 | bytes 131072 | tf_op jit(solution)/shard_map/transpose | solution.py:418
  1.6 4.0 %collective-permute-start = (f16[32,512]{1,0:T(8,128)(2,1)S(1)}, f16[32,512]{1,0:T(8,128)(2,1)S(1)}, u32[]{:S(2)}, u32[]{:S(2)}) collective-permute-start(f16[32,512]{1,0:T(8,128)(2,1)S(1)} %get-tuple-element.24), channel_id=1, source_target_pairs={{0,2},{1,3},{2,0},{3,1},{4,6},{5,7},{6,4},{7,5},{8,10},{9,11},{10,... | collective-permute-start | bytes 98312 | tf_op jit(solution)/shard_map/ppermute | solution.py:384
  5.6 1.7 %pack.1 = (bf16[16,24,512]{2,1,0:T(8,128)(2,1)}, bf16[32,512]{1,0:T(8,128)(2,1)}) custom-call(f32[2,16,512]{2,1,0:T(8,128)} %source.1, bf16[4,4,512]{2,1,0:T(4,128)(2,1)} %refs_1_.1, s32[1,512]{1,0:T(1,128)} %bitcast.52, s32[1,512]{1,0:T(1,128)} %bitcast.53), custom_call_target="tpu_custom_call" | custom-call | tf_op jit(solution)/shard_map/pack/pallas_call | solution.py:355
  7.3 1.4 %collective-permute-start.4 = (bf16[32,512]{1,0:T(8,128)(2,1)}, bf16[32,512]{1,0:T(8,128)(2,1)S(1)}, u32[]{:S(2)}, u32[]{:S(2)}) collective-permute-start(bf16[32,512]{1,0:T(8,128)(2,1)} %get-tuple-element.15), channel_id=1, source_target_pairs={{0,3},{1,0},{2,1},{3,2},{4,7},{5,4},{6,5},{7,6},{8,11},{9,8},{10,9... | collective-permute-start | bytes 98312 | tf_op jit(solution)/shard_map/ppermute | solution.py:371
  8.7 0.7 collective-permute-start.3
  9.4 0.0 collective-permute-done
  9.4 1.6 %collective-permute-start.1 = (f16[2,32,512]{2,1,0:T(8,128)(2,1)S(1)}, f16[2,32,512]{2,1,0:T(8,128)(2,1)S(1)}, u32[]{:S(2)}, u32[]{:S(2)}) collective-permute-start(f16[2,32,512]{2,1,0:T(8,128)(2,1)S(1)} %maximum_select_fusion.4), channel_id=1, source_target_pairs={{0,1},{1,0},{2,3},{3,2},{4,5},{5,4},{6,7},{7,6},{8,9},{9,8},{10,11... | collective-permute-start | bytes 196616 | tf_op jit(solution)/shard_map/ppermute | solution.py:384
  11.1 0.8 collective-permute-done.4
  11.9 2.8 %collective-permute-done.3 = bf16[32,512]{1,0:T(8,128)(2,1)S(1)} collective-permute-done((bf16[32,512]{1,0:T(8,128)(2,1)}, bf16[32,512]{1,0:T(8,128)(2,1)S(1)}, u32[]{:S(2)}, u32[]{:S(2)}) %collective-permute-start.3) | collective-permute-done | bytes 32800 | tf_op jit(solution)/shard_map/ppermute | solution.py:371
  14.6 0.8 fusion
  15.4 0.1 collective-permute-start.6
  15.5 0.5 collective-permute-start.5
  16.0 3.6 %all-to-all-start = ((bf16[16,24,512]{2,1,0:T(8,128)(2,1)}), bf16[16,24,512]{2,1,0:T(8,128)(2,1)S(1)}, u32[]{:S(2)}, u32[]{:S(2)}) async-start(bf16[16,24,512]{2,1,0:T(8,128)(2,1)} %get-tuple-element.13), calls=%async_computation | async-start | bytes 786432 | tf_op jit(solution)/shard_map/all_to_all | solution.py:399
  19.5 0.0 collective-permute-done.1
  19.6 0.1 maximum_select_fusion.2
  19.6 1.9 %collective-permute-start.2 = (f16[2,2,32,512]{3,2,1,0:T(8,128)(2,1)S(1)}, f16[2,2,32,512]{3,2,1,0:T(8,128)(2,1)S(1)}, u32[]{:S(2)}, u32[]{:S(2)}) collective-permute-start(f16[2,2,32,512]{3,2,1,0:T(8,128)(2,1)S(1)} %maximum_select_fusion.2), channel_id=1, source_target_pairs={{0,8},{4,12},{8,0},{12,4},{1,9},{5,13},{9,1},{13,5},{2,10},{6,14},... | collective-permute-start | bytes 393224 | tf_op jit(solution)/shard_map/ppermute | solution.py:384
  21.5 0.1 maximum_select_fusion.3
  21.6 0.0 collective-permute-done.6
  21.6 0.0 collective-permute-done.5
  21.7 0.0 copy-start
  21.7 3.7 %copy-done = bf16[2,9,512,512]{3,2,1,0:T(8,128)(2,1)S(1)} copy-done((bf16[2,9,512,512]{3,2,1,0:T(8,128)(2,1)S(1)}, bf16[2,9,512,512]{3,2,1,0:T(8,128)(2,1)}, u32[]{:S(2)}) %copy-start) | copy-done | bytes 9437208
  25.3 0.8 %copy-done.2 = f32[2,16,512]{2,1,0:T(8,128)S(1)} copy-done((f32[2,16,512]{2,1,0:T(8,128)S(1)}, f32[2,16,512]{2,1,0:T(8,128)}, u32[]{:S(2)}) %copy-start.2) | copy-done | bytes 65560
  26.2 0.7 copy-done.4
  26.8 2.9 %near.2 = f32[16,2,512]{2,1,0:T(2,128)} custom-call(f32[2]{0:T(128)S(1)} %copy-done.4, bf16[9,32,512]{2,1,0:T(8,128)(2,1)S(1)} %bitcast.34, f32[2,16,512]{2,1,0:T(8,128)S(1)} %copy-done.2, bf16[2,9,512,512]{3,2,1,0:T(8,128)(2,1)S(1)} %copy-done), custom_call_target="tpu_custom_call" | custom-call | flops 301989888 | bytes 9437184 | tf_op jit(solution)/shard_map/near/pallas_call | solution.py:266
  29.7 0.0 collective-permute-done.2
  29.8 0.1 maximum_select_fusion.1
  29.9 0.1 collective-permute-start.7
  30.0 1.5 %collective-permute-done.7 = f16[2,2,2,32,512]{4,3,1,2,0:T(8,128)(2,1)S(1)} collective-permute-done((f16[2,2,2,32,512]{4,3,1,2,0:T(8,128)(2,1)S(1)}, f16[2,2,2,32,512]{4,3,1,2,0:T(8,128)(2,1)S(1)}, u32[]{:S(2)}, u32[]{:S(2)}) %collective-permute-start.7) | collective-permute-done | bytes 262176 | tf_op jit(solution)/shard_map/ppermute | solution.py:384
  31.5 0.2 convert_multiply_fusion
  31.7 0.3 copy.22.scale
  32.0 0.4 all-to-all-done.meta
  32.4 4.3 %all-to-all-start.1 = ((f32[16,2,512]{2,1,0:T(2,128)}), f32[16,2,512]{2,1,0:T(2,128)S(1)}, u32[]{:S(2)}, u32[]{:S(2)}) async-start(f32[16,2,512]{2,1,0:T(2,128)} %near.2), calls=%async_computation.1 | async-start | bytes 131072 | tf_op jit(solution)/shard_map/all_to_all | solution.py:399
  36.7 10.5 %recip.2.part = f32[16,2,512]{2,1,0:T(2,128)S(1)} custom-call(bf16[16,24,512]{2,1,0:T(8,128)(2,1)S(1)} %all-to-all-done.meta, f32[512,512]{1,0:T(8,128)S(1)} %copy.22.scale, bf16[4,2,2,2,128,128]{5,4,3,2,1,0:T(8,128)(2,1)S(1)} %copy-done.6, bf16[4,2,2,2,128,128]{5,4,3,2,1,0:T(8,128)(2,1)S(1)} %copy-done.6), custom_call_target="tpu_custom_call" | custom-call | flops 10000000000 | bytes 8000000 | tf_op jit(solution)/shard_map/recip/pallas_call | solution.py:210
  47.2 0.0 all-to-all-done.1.start
  47.2 1.2 %neighbour_rows.1 = (f32[16,2,512]{2,1,0:T(2,128)S(1)}, bf16[16,24,512]{2,1,0:T(8,128)(2,1)}) custom-call(f32[16,2,512]{2,1,0:T(2,128)S(1)} %recip.2.part, f32[16,2,512]{2,1,0:T(2,128)S(1)} %all-to-all-done.1.start), custom_call_target="tpu_custom_call" | custom-call | tf_op jit(solution)/shard_map/neighbour_rows/pallas_call | solution.py:304
  48.4 6.0 %all-to-all-start.2 = ((bf16[16,24,512]{2,1,0:T(8,128)(2,1)}), bf16[16,24,512]{2,1,0:T(8,128)(2,1)S(1)}, u32[]{:S(2)}, u32[]{:S(2)}) async-start(bf16[16,24,512]{2,1,0:T(8,128)(2,1)} %get-tuple-element.18), calls=%async_computation.2 | async-start | bytes 786432 | tf_op jit(solution)/shard_map/all_to_all | solution.py:399
  54.4 0.0 copy-start.5
  54.4 11.1 %recip.3 = f32[16,2,512]{2,1,0:T(2,128)} custom-call(bf16[16,24,512]{2,1,0:T(8,128)(2,1)S(1)} %all-to-all-done.meta, f32[512,512]{1,0:T(8,128)S(1)} %copy.22.scale, bf16[4,2,2,2,128,128]{5,4,3,2,1,0:T(8,128)(2,1)S(1)} %copy-done.6, bf16[4,2,2,2,128,128]{5,4,3,2,1,0:T(8,128)(2,1)S(1)} %copy-done.6, f32[16,2,512]{2,1,0:T(2,128)S(1)} %get-tuple-element.19.rest_0_), custom_call_target="tpu_custom_call" | custom-call | flops 10000000000 | bytes 8000000 | tf_op jit(solution)/shard_map/recip/pallas_call | solution.py:210
  65.5 1.8 %all-to-all-done.2 = bf16[16,24,512]{2,1,0:T(8,128)(2,1)S(1)} async-done(((bf16[16,24,512]{2,1,0:T(8,128)(2,1)}), bf16[16,24,512]{2,1,0:T(8,128)(2,1)S(1)}, u32[]{:S(2)}, u32[]{:S(2)}) %all-to-all-start.2) | async-done | bytes 393248 | tf_op jit(solution)/shard_map/all_to_all | solution.py:399
  67.3 0.1 copy.29
  67.4 4.2 %all-to-all-start.3 = ((f32[16,2,512]{2,1,0:T(2,128)}), f32[16,2,512]{2,1,0:T(2,128)S(1)}, u32[]{:S(2)}, u32[]{:S(2)}) async-start(f32[16,2,512]{2,1,0:T(2,128)} %recip.3), calls=%async_computation.3 | async-start | bytes 131072 | tf_op jit(solution)/shard_map/all_to_all | solution.py:399
  71.7 0.0 copy-start.3
  71.7 0.0 copy-start.1
  71.7 3.7 %copy-done.1 = bf16[2,9,512,512]{3,2,1,0:T(8,128)(2,1)S(1)} copy-done((bf16[2,9,512,512]{3,2,1,0:T(8,128)(2,1)S(1)}, bf16[2,9,512,512]{3,2,1,0:T(8,128)(2,1)}, u32[]{:S(2)}) %copy-start.1) | copy-done | bytes 9437208
  75.4 2.3 %near.3 = f32[2,16,512]{2,1,0:T(8,128)S(1)} custom-call(f32[2]{0:T(128)S(1)} %copy-done.5, bf16[9,32,512]{2,1,0:T(8,128)(2,1)S(1)} %bitcast.35, f32[2,16,512]{2,1,0:T(8,128)S(1)} %convert_add_fusion.source, bf16[2,9,512,512]{3,2,1,0:T(8,128)(2,1)S(1)} %copy-done.1), custom_call_target="tpu_custom_call" | custom-call | flops 301989888 | bytes 9437184 | tf_op jit(solution)/shard_map/near/pallas_call | solution.py:266
  77.7 0.6 all-to-all-done.3
  78.3 0.6 bitcast_add_fusion
  (10 shorter events, 0.1 us)
Async XLA Ops:
  0.6 36.1 %copy-start.6 = (bf16[4,2,2,2,128,128]{5,4,3,2,1,0:T(8,128)(2,1)S(1)}, bf16[4,2,2,2,128,128]{5,4,3,2,1,0:T(8,128)(2,1)}, u32[]{:S(2)}) copy-start(bf16[4,2,2,2,128,128]{5,4,3,2,1,0:T(8,128)(2,1)} %constant.70.clone.tab1.tab2) | copy-start | bytes 3145732
  1.6 7.8 %collective-permute-start = (f16[32,512]{1,0:T(8,128)(2,1)S(1)}, f16[32,512]{1,0:T(8,128)(2,1)S(1)}, u32[]{:S(2)}, u32[]{:S(2)}) collective-permute-start(f16[32,512]{1,0:T(8,128)(2,1)S(1)} %get-tuple-element.24), channel_id=1, source_target_pairs={{0,2},{1,3},{2,0},{3,1},{4,6},{5,7},{6,4},{7,5},{8,10},{9,11},{10,... | collective-permute-start | bytes 98312 | tf_op jit(solution)/shard_map/ppermute | solution.py:384
  7.3 4.5 %collective-permute-start.4 = (bf16[32,512]{1,0:T(8,128)(2,1)}, bf16[32,512]{1,0:T(8,128)(2,1)S(1)}, u32[]{:S(2)}, u32[]{:S(2)}) collective-permute-start(bf16[32,512]{1,0:T(8,128)(2,1)} %get-tuple-element.15), channel_id=1, source_target_pairs={{0,3},{1,0},{2,1},{3,2},{4,7},{5,4},{6,5},{7,6},{8,11},{9,8},{10,9... | collective-permute-start | bytes 98312 | tf_op jit(solution)/shard_map/ppermute | solution.py:371
  8.7 5.9 %collective-permute-start.3 = (bf16[32,512]{1,0:T(8,128)(2,1)}, bf16[32,512]{1,0:T(8,128)(2,1)S(1)}, u32[]{:S(2)}, u32[]{:S(2)}) collective-permute-start(bf16[32,512]{1,0:T(8,128)(2,1)} %get-tuple-element.15), channel_id=1, source_target_pairs={{0,1},{1,2},{2,3},{3,0},{4,5},{5,6},{6,7},{7,4},{8,9},{9,10},{10,1... | collective-permute-start | bytes 98312 | tf_op jit(solution)/shard_map/ppermute | solution.py:371
  9.4 10.1 %collective-permute-start.1 = (f16[2,32,512]{2,1,0:T(8,128)(2,1)S(1)}, f16[2,32,512]{2,1,0:T(8,128)(2,1)S(1)}, u32[]{:S(2)}, u32[]{:S(2)}) collective-permute-start(f16[2,32,512]{2,1,0:T(8,128)(2,1)S(1)} %maximum_select_fusion.4), channel_id=1, source_target_pairs={{0,1},{1,0},{2,3},{3,2},{4,5},{5,4},{6,7},{7,6},{8,9},{9,8},{10,11... | collective-permute-start | bytes 196616 | tf_op jit(solution)/shard_map/ppermute | solution.py:384
  15.4 6.2 %collective-permute-start.6 = (bf16[3,32,512]{2,1,0:T(8,128)(2,1)S(1)}, bf16[3,32,512]{2,1,0:T(8,128)(2,1)S(1)}, u32[]{:S(2)}, u32[]{:S(2)}) collective-permute-start(bf16[3,32,512]{2,1,0:T(8,128)(2,1)S(1)} %get-tuple-element.23), channel_id=1, source_target_pairs={{0,12},{4,0},{8,4},{12,8},{1,13},{5,1},{9,5},{13,9},{2,14},{6,2},{... | collective-permute-start | bytes 294920 | tf_op jit(solution)/shard_map/ppermute | solution.py:371
  15.5 6.1 %collective-permute-start.5 = (bf16[3,32,512]{2,1,0:T(8,128)(2,1)S(1)}, bf16[3,32,512]{2,1,0:T(8,128)(2,1)S(1)}, u32[]{:S(2)}, u32[]{:S(2)}) collective-permute-start(bf16[3,32,512]{2,1,0:T(8,128)(2,1)S(1)} %get-tuple-element.23), channel_id=1, source_target_pairs={{0,4},{4,8},{8,12},{12,0},{1,5},{5,9},{9,13},{13,1},{2,6},{6,10},{... | collective-permute-start | bytes 294920 | tf_op jit(solution)/shard_map/ppermute | solution.py:371
  16.0 16.4 %all-to-all-start = ((bf16[16,24,512]{2,1,0:T(8,128)(2,1)}), bf16[16,24,512]{2,1,0:T(8,128)(2,1)S(1)}, u32[]{:S(2)}, u32[]{:S(2)}) async-start(bf16[16,24,512]{2,1,0:T(8,128)(2,1)} %get-tuple-element.13), calls=%async_computation | async-start | bytes 786432 | tf_op jit(solution)/shard_map/all_to_all | solution.py:399
  19.6 10.1 %collective-permute-start.2 = (f16[2,2,32,512]{3,2,1,0:T(8,128)(2,1)S(1)}, f16[2,2,32,512]{3,2,1,0:T(8,128)(2,1)S(1)}, u32[]{:S(2)}, u32[]{:S(2)}) collective-permute-start(f16[2,2,32,512]{3,2,1,0:T(8,128)(2,1)S(1)} %maximum_select_fusion.2), channel_id=1, source_target_pairs={{0,8},{4,12},{8,0},{12,4},{1,9},{5,13},{9,1},{13,5},{2,10},{6,14},... | collective-permute-start | bytes 393224 | tf_op jit(solution)/shard_map/ppermute | solution.py:384
  21.7 3.7 %copy-start = (bf16[2,9,512,512]{3,2,1,0:T(8,128)(2,1)S(1)}, bf16[2,9,512,512]{3,2,1,0:T(8,128)(2,1)}, u32[]{:S(2)}) copy-start(bf16[2,9,512,512]{3,2,1,0:T(8,128)(2,1)} %blocks.3) | copy-start | bytes 28311556
  25.3 0.8 %copy-start.2 = (f32[2,16,512]{2,1,0:T(8,128)S(1)}, f32[2,16,512]{2,1,0:T(8,128)}, u32[]{:S(2)}) copy-start(f32[2,16,512]{2,1,0:T(8,128)} %source.1) | copy-start | bytes 196612
  26.2 0.7 copy-start.4
  29.9 1.6 %collective-permute-start.7 = (f16[2,2,2,32,512]{4,3,1,2,0:T(8,128)(2,1)S(1)}, f16[2,2,2,32,512]{4,3,1,2,0:T(8,128)(2,1)S(1)}, u32[]{:S(2)}, u32[]{:S(2)}) collective-permute-start(f16[2,2,2,32,512]{4,3,1,2,0:T(8,128)(2,1)S(1)} %maximum_select_fusion.1), channel_id=1, source_target_pairs={{0,4},{4,0},{8,12},{12,8},{1,5},{5,1},{9,13},{13,9},{2,6},{6,2},{1... | collective-permute-start | bytes 786440 | tf_op jit(solution)/shard_map/ppermute | solution.py:384
  32.4 14.8 %all-to-all-start.1 = ((f32[16,2,512]{2,1,0:T(2,128)}), f32[16,2,512]{2,1,0:T(2,128)S(1)}, u32[]{:S(2)}, u32[]{:S(2)}) async-start(f32[16,2,512]{2,1,0:T(2,128)} %near.2), calls=%async_computation.1 | async-start | bytes 131072 | tf_op jit(solution)/shard_map/all_to_all | solution.py:399
  48.4 18.9 %all-to-all-start.2 = ((bf16[16,24,512]{2,1,0:T(8,128)(2,1)}), bf16[16,24,512]{2,1,0:T(8,128)(2,1)S(1)}, u32[]{:S(2)}, u32[]{:S(2)}) async-start(bf16[16,24,512]{2,1,0:T(8,128)(2,1)} %get-tuple-element.18), calls=%async_computation.2 | async-start | bytes 786432 | tf_op jit(solution)/shard_map/all_to_all | solution.py:399
  54.4 17.3 %copy-start.5 = (f32[2]{0:T(128)S(1)}, f32[2]{0:T(128)}, u32[]{:S(2)}) copy-start(f32[2]{0:T(128)} %bloch.3) | copy-start | bytes 28
  67.4 10.9 %all-to-all-start.3 = ((f32[16,2,512]{2,1,0:T(2,128)}), f32[16,2,512]{2,1,0:T(2,128)S(1)}, u32[]{:S(2)}, u32[]{:S(2)}) async-start(f32[16,2,512]{2,1,0:T(2,128)} %recip.3), calls=%async_computation.3 | async-start | bytes 131072 | tf_op jit(solution)/shard_map/all_to_all | solution.py:399
  71.7 7.3 %copy-start.3 = (f32[2,16,512]{2,1,0:T(8,128)}, f32[2,16,512]{2,1,0:T(8,128)S(1)}, u32[]{:S(2)}) copy-start(f32[2,16,512]{2,1,0:T(8,128)S(1)} %convert_add_fusion.source) | copy-start | bytes 196612
  71.7 3.7 %copy-start.1 = (bf16[2,9,512,512]{3,2,1,0:T(8,128)(2,1)S(1)}, bf16[2,9,512,512]{3,2,1,0:T(8,128)(2,1)}, u32[]{:S(2)}) copy-start(bf16[2,9,512,512]{3,2,1,0:T(8,128)(2,1)} %blocks.3) | copy-start | bytes 28311556

commit v6 on v5

--- a/solution.py
+++ b/solution.py
@@ -12,6 +12,7 @@
 STENCIL = 4
 RADIX = 4
 UNROLL = 16
+GROUP = 4
 MOST_HELD = 20 * 1024 * 1024
 F32 = jnp.float32
 BF = jnp.bfloat16
@@ -150,26 +151,24 @@
         freq[2 * m] = real
         freq[2 * m + 1] = imag
 
-    for pair in range(0, RADIX, 2):
+    for first in range(0, RADIX, GROUP):
+        group = range(first, first + GROUP)
         parts = []
         for r in range(RADIX):
             rows = pl.ds(r, q1, stride=RADIX)
-            both = [
-                jnp.concatenate([freq[2 * pair + c, rows, :], freq[2 * pair + 2 + c, rows, :]], 1)
-                for c in range(2)
-            ]
+            both = [jnp.concatenate([freq[2 * g + c, rows, :] for g in group], 1) for c in range(2)]
             y = times_left(full_table(tab1.at[r], 1), jnp.concatenate(both, 0))
             parts.append((y[:q1], y[q1:]))
         scaled = []
         for m, (real, imag) in enumerate(butterfly(parts, -1)):
-            k = scale[m * q1 : (m + 1) * q1, pair * q2 : (pair + 2) * q2]
+            k = scale[m * q1 : (m + 1) * q1, first * q2 : (first + GROUP) * q2]
             scaled.append((real * k, imag * k))
         for r, both in enumerate(butterfly(scaled, 1)):
             y = times_left(full_table(tab1.at[r], 0), jnp.concatenate(both, 0))
             rows = pl.ds(r, q1, stride=RADIX)
-            for c in range(2):
-                freq[2 * pair + c, rows, :] = y[c * q1 : (c + 1) * q1, :q2]
-                freq[2 * pair + 2 + c, rows, :] = y[c * q1 : (c + 1) * q1, q2:]
+            for k, g in enumerate(group):
+                for c in range(2):
+                    freq[2 * g + c, rows, :] = y[c * q1 : (c + 1) * q1, k * q2 : (k + 1) * q2]
 
     parts = [(freq[2 * m], freq[2 * m + 1]) for m in range(RADIX)]
     for r, both in enumerate(butterfly(parts, 1)):

time: 79.7 us -> 79.9 us (level)
  no operation moved by 1% of the time
where the time goes in v6:
time: 79.9 us; the launch traced here: 79.2 us
  Pallas kernels  29.9 us (37%)
  starting transfers between devices  28.5 us (36%)
  local copies, waits for them, and re-layouts  9.36 us (12%)
  waiting for transfers between devices  7.71 us (10%)
  other arithmetic  2.82 us (4%)
  between operations  0.88 us (1%)
    pallas_call x2, Pallas kernels, recip_apply(): pl.pallas_call(functools.partial(recip_kernel, rows_dev, n1, n2), out_sha...  21.8 us
    all_to_all x4, starting transfers between devices, exchange(): return lax.all_to_all(parts, AXES, 0, 0, tiled=True)  18.2 us
    unnamed x14, local copies, waits for them, and re-layouts  8.86 us
    ppermute x4, starting transfers between devices, doubled(): lax.ppermute(block, axis, [(i, i ^ reach) for i in range(lax.axis_size(ax...  7.66 us
    pallas_call x2, Pallas kernels, near_apply(): pl.pallas_call(functools.partial(near_kernel, probes_first), out_shape=ja...  5.17 us
    ppermute x4, waiting for transfers between devices, shifted(): lax.ppermute(array, axis, [(i, (i + by) % count) for i in range(count)])  3.57 us
    ppermute x4, starting transfers between devices, shifted(): lax.ppermute(array, axis, [(i, (i + by) % count) for i in range(count)])  2.63 us
    all_to_all x4, waiting for transfers between devices, exchange(): return lax.all_to_all(parts, AXES, 0, 0, tiled=True)  2.62 us
  transfers between devices with their start and end apart: 12, of which 6 were waited for; matrix products, arithmetic and copies ran while one was open for 2% of the time, Pallas kernels for 36%

profile of v6, /device:TPU:0, one launch (start us, length us, event | category | flops | bytes accessed | tf_op | source)
XLA Modules:
  0.0 79.2 jit_solution(7100464477319661485)
XLA Ops:
  0.6 0.0 copy-start.6
  0.6 0.9 %convert_bitcast_fusion.1 = (f16[32,512]{1,0:T(8,128)(2,1)S(1)}, f16[1,32,512]{2,1,0:T(8,128)(2,1)S(1)}) fusion(f32[512,32]{0,1:T(8,128)} %param.17), kind=kLoop, calls=%fused_computation.13 | loop fusion | flops 16384 | bytes 131072 | tf_op jit(solution)/shard_map/transpose | solution.py:417
  1.6 4.0 %collective-permute-start = (f16[32,512]{1,0:T(8,128)(2,1)S(1)}, f16[32,512]{1,0:T(8,128)(2,1)S(1)}, u32[]{:S(2)}, u32[]{:S(2)}) collective-permute-start(f16[32,512]{1,0:T(8,128)(2,1)S(1)} %get-tuple-element.24), channel_id=1, source_target_pairs={{0,2},{1,3},{2,0},{3,1},{4,6},{5,7},{6,4},{7,5},{8,10},{9,11},{10,... | collective-permute-start | bytes 98312 | tf_op jit(solution)/shard_map/ppermute | solution.py:383
  5.6 1.7 %pack.1 = (bf16[16,24,512]{2,1,0:T(8,128)(2,1)}, bf16[32,512]{1,0:T(8,128)(2,1)}) custom-call(f32[2,16,512]{2,1,0:T(8,128)} %source.1, bf16[4,4,512]{2,1,0:T(4,128)(2,1)} %refs_1_.1, s32[1,512]{1,0:T(1,128)} %bitcast.52, s32[1,512]{1,0:T(1,128)} %bitcast.53), custom_call_target="tpu_custom_call" | custom-call | tf_op jit(solution)/shard_map/pack/pallas_call | solution.py:354
  7.3 1.4 %collective-permute-start.4 = (bf16[32,512]{1,0:T(8,128)(2,1)}, bf16[32,512]{1,0:T(8,128)(2,1)S(1)}, u32[]{:S(2)}, u32[]{:S(2)}) collective-permute-start(bf16[32,512]{1,0:T(8,128)(2,1)} %get-tuple-element.15), channel_id=1, source_target_pairs={{0,3},{1,0},{2,1},{3,2},{4,7},{5,4},{6,5},{7,6},{8,11},{9,8},{10,9... | collective-permute-start | bytes 98312 | tf_op jit(solution)/shard_map/ppermute | solution.py:370
  8.7 0.7 collective-permute-start.3
  9.4 0.0 collective-permute-done
  9.4 1.6 %collective-permute-start.1 = (f16[2,32,512]{2,1,0:T(8,128)(2,1)S(1)}, f16[2,32,512]{2,1,0:T(8,128)(2,1)S(1)}, u32[]{:S(2)}, u32[]{:S(2)}) collective-permute-start(f16[2,32,512]{2,1,0:T(8,128)(2,1)S(1)} %maximum_select_fusion.4), channel_id=1, source_target_pairs={{0,1},{1,0},{2,3},{3,2},{4,5},{5,4},{6,7},{7,6},{8,9},{9,8},{10,11... | collective-permute-start | bytes 196616 | tf_op jit(solution)/shard_map/ppermute | solution.py:383
  11.1 0.8 collective-permute-done.4
  11.9 2.8 %collective-permute-done.3 = bf16[32,512]{1,0:T(8,128)(2,1)S(1)} collective-permute-done((bf16[32,512]{1,0:T(8,128)(2,1)}, bf16[32,512]{1,0:T(8,128)(2,1)S(1)}, u32[]{:S(2)}, u32[]{:S(2)}) %collective-permute-start.3) | collective-permute-done | bytes 32800 | tf_op jit(solution)/shard_map/ppermute | solution.py:370
  14.6 0.8 fusion
  15.4 0.1 collective-permute-start.6
  15.5 0.5 collective-permute-start.5
  16.0 3.6 %all-to-all-start = ((bf16[16,24,512]{2,1,0:T(8,128)(2,1)}), bf16[16,24,512]{2,1,0:T(8,128)(2,1)S(1)}, u32[]{:S(2)}, u32[]{:S(2)}) async-start(bf16[16,24,512]{2,1,0:T(8,128)(2,1)} %get-tuple-element.13), calls=%async_computation | async-start | bytes 786432 | tf_op jit(solution)/shard_map/all_to_all | solution.py:398
  19.5 0.0 collective-permute-done.1
  19.6 0.1 maximum_select_fusion.2
  19.6 1.9 %collective-permute-start.2 = (f16[2,2,32,512]{3,2,1,0:T(8,128)(2,1)S(1)}, f16[2,2,32,512]{3,2,1,0:T(8,128)(2,1)S(1)}, u32[]{:S(2)}, u32[]{:S(2)}) collective-permute-start(f16[2,2,32,512]{3,2,1,0:T(8,128)(2,1)S(1)} %maximum_select_fusion.2), channel_id=1, source_target_pairs={{0,8},{4,12},{8,0},{12,4},{1,9},{5,13},{9,1},{13,5},{2,10},{6,14},... | collective-permute-start | bytes 393224 | tf_op jit(solution)/shard_map/ppermute | solution.py:383
  21.5 0.1 maximum_select_fusion.3
  21.6 0.0 collective-permute-done.6
  21.6 0.0 collective-permute-done.5
  21.7 0.0 copy-start
  21.7 3.7 %copy-done = bf16[2,9,512,512]{3,2,1,0:T(8,128)(2,1)S(1)} copy-done((bf16[2,9,512,512]{3,2,1,0:T(8,128)(2,1)S(1)}, bf16[2,9,512,512]{3,2,1,0:T(8,128)(2,1)}, u32[]{:S(2)}) %copy-start) | copy-done | bytes 9437208
  25.3 0.8 %copy-done.2 = f32[2,16,512]{2,1,0:T(8,128)S(1)} copy-done((f32[2,16,512]{2,1,0:T(8,128)S(1)}, f32[2,16,512]{2,1,0:T(8,128)}, u32[]{:S(2)}) %copy-start.2) | copy-done | bytes 65560
  26.2 0.7 copy-done.4
  26.8 2.9 %near.2 = f32[16,2,512]{2,1,0:T(2,128)} custom-call(f32[2]{0:T(128)S(1)} %copy-done.4, bf16[9,32,512]{2,1,0:T(8,128)(2,1)S(1)} %bitcast.34, f32[2,16,512]{2,1,0:T(8,128)S(1)} %copy-done.2, bf16[2,9,512,512]{3,2,1,0:T(8,128)(2,1)S(1)} %copy-done), custom_call_target="tpu_custom_call" | custom-call | flops 301989888 | bytes 9437184 | tf_op jit(solution)/shard_map/near/pallas_call | solution.py:265
  29.7 0.0 collective-permute-done.2
  29.8 0.1 maximum_select_fusion.1
  29.9 0.1 collective-permute-start.7
  30.0 1.5 %collective-permute-done.7 = f16[2,2,2,32,512]{4,3,1,2,0:T(8,128)(2,1)S(1)} collective-permute-done((f16[2,2,2,32,512]{4,3,1,2,0:T(8,128)(2,1)S(1)}, f16[2,2,2,32,512]{4,3,1,2,0:T(8,128)(2,1)S(1)}, u32[]{:S(2)}, u32[]{:S(2)}) %collective-permute-start.7) | collective-permute-done | bytes 262176 | tf_op jit(solution)/shard_map/ppermute | solution.py:383
  31.5 0.2 convert_multiply_fusion
  31.7 0.3 copy.22.scale
  32.0 0.4 all-to-all-done.meta
  32.4 4.3 %all-to-all-start.1 = ((f32[16,2,512]{2,1,0:T(2,128)}), f32[16,2,512]{2,1,0:T(2,128)S(1)}, u32[]{:S(2)}, u32[]{:S(2)}) async-start(f32[16,2,512]{2,1,0:T(2,128)} %near.2), calls=%async_computation.1 | async-start | bytes 131072 | tf_op jit(solution)/shard_map/all_to_all | solution.py:398
  36.7 10.6 %recip.2.part = f32[16,2,512]{2,1,0:T(2,128)S(1)} custom-call(bf16[16,24,512]{2,1,0:T(8,128)(2,1)S(1)} %all-to-all-done.meta, f32[512,512]{1,0:T(8,128)S(1)} %copy.22.scale, bf16[4,2,2,2,128,128]{5,4,3,2,1,0:T(8,128)(2,1)S(1)} %copy-done.6, bf16[4,2,2,2,128,128]{5,4,3,2,1,0:T(8,128)(2,1)S(1)} %copy-done.6), custom_call_target="tpu_custom_call" | custom-call | flops 10000000000 | bytes 8000000 | tf_op jit(solution)/shard_map/recip/pallas_call | solution.py:209
  47.3 0.0 all-to-all-done.1.start
  47.4 1.2 %neighbour_rows.1 = (f32[16,2,512]{2,1,0:T(2,128)S(1)}, bf16[16,24,512]{2,1,0:T(8,128)(2,1)}) custom-call(f32[16,2,512]{2,1,0:T(2,128)S(1)} %recip.2.part, f32[16,2,512]{2,1,0:T(2,128)S(1)} %all-to-all-done.1.start), custom_call_target="tpu_custom_call" | custom-call | tf_op jit(solution)/shard_map/neighbour_rows/pallas_call | solution.py:303
  48.6 6.0 %all-to-all-start.2 = ((bf16[16,24,512]{2,1,0:T(8,128)(2,1)}), bf16[16,24,512]{2,1,0:T(8,128)(2,1)S(1)}, u32[]{:S(2)}, u32[]{:S(2)}) async-start(bf16[16,24,512]{2,1,0:T(8,128)(2,1)} %get-tuple-element.18), calls=%async_computation.2 | async-start | bytes 786432 | tf_op jit(solution)/shard_map/all_to_all | solution.py:398
  54.6 0.0 copy-start.5
  54.6 11.2 %recip.3 = f32[16,2,512]{2,1,0:T(2,128)} custom-call(bf16[16,24,512]{2,1,0:T(8,128)(2,1)S(1)} %all-to-all-done.meta, f32[512,512]{1,0:T(8,128)S(1)} %copy.22.scale, bf16[4,2,2,2,128,128]{5,4,3,2,1,0:T(8,128)(2,1)S(1)} %copy-done.6, bf16[4,2,2,2,128,128]{5,4,3,2,1,0:T(8,128)(2,1)S(1)} %copy-done.6, f32[16,2,512]{2,1,0:T(2,128)S(1)} %get-tuple-element.19.rest_0_), custom_call_target="tpu_custom_call" | custom-call | flops 10000000000 | bytes 8000000 | tf_op jit(solution)/shard_map/recip/pallas_call | solution.py:209
  65.8 1.7 %all-to-all-done.2 = bf16[16,24,512]{2,1,0:T(8,128)(2,1)S(1)} async-done(((bf16[16,24,512]{2,1,0:T(8,128)(2,1)}), bf16[16,24,512]{2,1,0:T(8,128)(2,1)S(1)}, u32[]{:S(2)}, u32[]{:S(2)}) %all-to-all-start.2) | async-done | bytes 393248 | tf_op jit(solution)/shard_map/all_to_all | solution.py:398
  67.5 0.1 copy.29
  67.6 4.4 %all-to-all-start.3 = ((f32[16,2,512]{2,1,0:T(2,128)}), f32[16,2,512]{2,1,0:T(2,128)S(1)}, u32[]{:S(2)}, u32[]{:S(2)}) async-start(f32[16,2,512]{2,1,0:T(2,128)} %recip.3), calls=%async_computation.3 | async-start | bytes 131072 | tf_op jit(solution)/shard_map/all_to_all | solution.py:398
  72.0 0.0 copy-start.3
  72.0 0.0 copy-start.1
  72.0 3.7 %copy-done.1 = bf16[2,9,512,512]{3,2,1,0:T(8,128)(2,1)S(1)} copy-done((bf16[2,9,512,512]{3,2,1,0:T(8,128)(2,1)S(1)}, bf16[2,9,512,512]{3,2,1,0:T(8,128)(2,1)}, u32[]{:S(2)}) %copy-start.1) | copy-done | bytes 9437208
  75.7 2.3 %near.3 = f32[2,16,512]{2,1,0:T(8,128)S(1)} custom-call(f32[2]{0:T(128)S(1)} %copy-done.5, bf16[9,32,512]{2,1,0:T(8,128)(2,1)S(1)} %bitcast.35, f32[2,16,512]{2,1,0:T(8,128)S(1)} %convert_add_fusion.source, bf16[2,9,512,512]{3,2,1,0:T(8,128)(2,1)S(1)} %copy-done.1), custom_call_target="tpu_custom_call" | custom-call | flops 301989888 | bytes 9437184 | tf_op jit(solution)/shard_map/near/pallas_call | solution.py:265
  78.0 0.6 all-to-all-done.3
  78.6 0.6 bitcast_add_fusion
  (10 shorter events, 0.1 us)
Async XLA Ops:
  0.6 36.1 %copy-start.6 = (bf16[4,2,2,2,128,128]{5,4,3,2,1,0:T(8,128)(2,1)S(1)}, bf16[4,2,2,2,128,128]{5,4,3,2,1,0:T(8,128)(2,1)}, u32[]{:S(2)}) copy-start(bf16[4,2,2,2,128,128]{5,4,3,2,1,0:T(8,128)(2,1)} %constant.70.clone.tab1.tab2) | copy-start | bytes 3145732
  1.6 7.8 %collective-permute-start = (f16[32,512]{1,0:T(8,128)(2,1)S(1)}, f16[32,512]{1,0:T(8,128)(2,1)S(1)}, u32[]{:S(2)}, u32[]{:S(2)}) collective-permute-start(f16[32,512]{1,0:T(8,128)(2,1)S(1)} %get-tuple-element.24), channel_id=1, source_target_pairs={{0,2},{1,3},{2,0},{3,1},{4,6},{5,7},{6,4},{7,5},{8,10},{9,11},{10,... | collective-permute-start | bytes 98312 | tf_op jit(solution)/shard_map/ppermute | solution.py:383
  7.3 4.5 %collective-permute-start.4 = (bf16[32,512]{1,0:T(8,128)(2,1)}, bf16[32,512]{1,0:T(8,128)(2,1)S(1)}, u32[]{:S(2)}, u32[]{:S(2)}) collective-permute-start(bf16[32,512]{1,0:T(8,128)(2,1)} %get-tuple-element.15), channel_id=1, source_target_pairs={{0,3},{1,0},{2,1},{3,2},{4,7},{5,4},{6,5},{7,6},{8,11},{9,8},{10,9... | collective-permute-start | bytes 98312 | tf_op jit(solution)/shard_map/ppermute | solution.py:370
  8.7 5.9 %collective-permute-start.3 = (bf16[32,512]{1,0:T(8,128)(2,1)}, bf16[32,512]{1,0:T(8,128)(2,1)S(1)}, u32[]{:S(2)}, u32[]{:S(2)}) collective-permute-start(bf16[32,512]{1,0:T(8,128)(2,1)} %get-tuple-element.15), channel_id=1, source_target_pairs={{0,1},{1,2},{2,3},{3,0},{4,5},{5,6},{6,7},{7,4},{8,9},{9,10},{10,1... | collective-permute-start | bytes 98312 | tf_op jit(solution)/shard_map/ppermute | solution.py:370
  9.4 10.1 %collective-permute-start.1 = (f16[2,32,512]{2,1,0:T(8,128)(2,1)S(1)}, f16[2,32,512]{2,1,0:T(8,128)(2,1)S(1)}, u32[]{:S(2)}, u32[]{:S(2)}) collective-permute-start(f16[2,32,512]{2,1,0:T(8,128)(2,1)S(1)} %maximum_select_fusion.4), channel_id=1, source_target_pairs={{0,1},{1,0},{2,3},{3,2},{4,5},{5,4},{6,7},{7,6},{8,9},{9,8},{10,11... | collective-permute-start | bytes 196616 | tf_op jit(solution)/shard_map/ppermute | solution.py:383
  15.4 6.2 %collective-permute-start.6 = (bf16[3,32,512]{2,1,0:T(8,128)(2,1)S(1)}, bf16[3,32,512]{2,1,0:T(8,128)(2,1)S(1)}, u32[]{:S(2)}, u32[]{:S(2)}) collective-permute-start(bf16[3,32,512]{2,1,0:T(8,128)(2,1)S(1)} %get-tuple-element.23), channel_id=1, source_target_pairs={{0,12},{4,0},{8,4},{12,8},{1,13},{5,1},{9,5},{13,9},{2,14},{6,2},{... | collective-permute-start | bytes 294920 | tf_op jit(solution)/shard_map/ppermute | solution.py:370
  15.5 6.1 %collective-permute-start.5 = (bf16[3,32,512]{2,1,0:T(8,128)(2,1)S(1)}, bf16[3,32,512]{2,1,0:T(8,128)(2,1)S(1)}, u32[]{:S(2)}, u32[]{:S(2)}) collective-permute-start(bf16[3,32,512]{2,1,0:T(8,128)(2,1)S(1)} %get-tuple-element.23), channel_id=1, source_target_pairs={{0,4},{4,8},{8,12},{12,0},{1,5},{5,9},{9,13},{13,1},{2,6},{6,10},{... | collective-permute-start | bytes 294920 | tf_op jit(solution)/shard_map/ppermute | solution.py:370
  16.0 16.4 %all-to-all-start = ((bf16[16,24,512]{2,1,0:T(8,128)(2,1)}), bf16[16,24,512]{2,1,0:T(8,128)(2,1)S(1)}, u32[]{:S(2)}, u32[]{:S(2)}) async-start(bf16[16,24,512]{2,1,0:T(8,128)(2,1)} %get-tuple-element.13), calls=%async_computation | async-start | bytes 786432 | tf_op jit(solution)/shard_map/all_to_all | solution.py:398
  19.6 10.1 %collective-permute-start.2 = (f16[2,2,32,512]{3,2,1,0:T(8,128)(2,1)S(1)}, f16[2,2,32,512]{3,2,1,0:T(8,128)(2,1)S(1)}, u32[]{:S(2)}, u32[]{:S(2)}) collective-permute-start(f16[2,2,32,512]{3,2,1,0:T(8,128)(2,1)S(1)} %maximum_select_fusion.2), channel_id=1, source_target_pairs={{0,8},{4,12},{8,0},{12,4},{1,9},{5,13},{9,1},{13,5},{2,10},{6,14},... | collective-permute-start | bytes 393224 | tf_op jit(solution)/shard_map/ppermute | solution.py:383
  21.7 3.7 %copy-start = (bf16[2,9,512,512]{3,2,1,0:T(8,128)(2,1)S(1)}, bf16[2,9,512,512]{3,2,1,0:T(8,128)(2,1)}, u32[]{:S(2)}) copy-start(bf16[2,9,512,512]{3,2,1,0:T(8,128)(2,1)} %blocks.3) | copy-start | bytes 28311556
  25.3 0.8 %copy-start.2 = (f32[2,16,512]{2,1,0:T(8,128)S(1)}, f32[2,16,512]{2,1,0:T(8,128)}, u32[]{:S(2)}) copy-start(f32[2,16,512]{2,1,0:T(8,128)} %source.1) | copy-start | bytes 196612
  26.2 0.7 copy-start.4
  29.9 1.6 %collective-permute-start.7 = (f16[2,2,2,32,512]{4,3,1,2,0:T(8,128)(2,1)S(1)}, f16[2,2,2,32,512]{4,3,1,2,0:T(8,128)(2,1)S(1)}, u32[]{:S(2)}, u32[]{:S(2)}) collective-permute-start(f16[2,2,2,32,512]{4,3,1,2,0:T(8,128)(2,1)S(1)} %maximum_select_fusion.1), channel_id=1, source_target_pairs={{0,4},{4,0},{8,12},{12,8},{1,5},{5,1},{9,13},{13,9},{2,6},{6,2},{1... | collective-permute-start | bytes 786440 | tf_op jit(solution)/shard_map/ppermute | solution.py:383
  32.4 15.0 %all-to-all-start.1 = ((f32[16,2,512]{2,1,0:T(2,128)}), f32[16,2,512]{2,1,0:T(2,128)S(1)}, u32[]{:S(2)}, u32[]{:S(2)}) async-start(f32[16,2,512]{2,1,0:T(2,128)} %near.2), calls=%async_computation.1 | async-start | bytes 131072 | tf_op jit(solution)/shard_map/all_to_all | solution.py:398
  48.6 18.9 %all-to-all-start.2 = ((bf16[16,24,512]{2,1,0:T(8,128)(2,1)}), bf16[16,24,512]{2,1,0:T(8,128)(2,1)S(1)}, u32[]{:S(2)}, u32[]{:S(2)}) async-start(bf16[16,24,512]{2,1,0:T(8,128)(2,1)} %get-tuple-element.18), calls=%async_computation.2 | async-start | bytes 786432 | tf_op jit(solution)/shard_map/all_to_all | solution.py:398
  54.6 17.4 %copy-start.5 = (f32[2]{0:T(128)S(1)}, f32[2]{0:T(128)}, u32[]{:S(2)}) copy-start(f32[2]{0:T(128)} %bloch.3) | copy-start | bytes 28
  67.6 11.0 %all-to-all-start.3 = ((f32[16,2,512]{2,1,0:T(2,128)}), f32[16,2,512]{2,1,0:T(2,128)S(1)}, u32[]{:S(2)}, u32[]{:S(2)}) async-start(f32[16,2,512]{2,1,0:T(2,128)} %recip.3), calls=%async_computation.3 | async-start | bytes 131072 | tf_op jit(solution)/shard_map/all_to_all | solution.py:398
  72.0 7.3 %copy-start.3 = (f32[2,16,512]{2,1,0:T(8,128)}, f32[2,16,512]{2,1,0:T(8,128)S(1)}, u32[]{:S(2)}) copy-start(f32[2,16,512]{2,1,0:T(8,128)S(1)} %convert_add_fusion.source) | copy-start | bytes 196612
  72.0 3.7 %copy-start.1 = (bf16[2,9,512,512]{3,2,1,0:T(8,128)(2,1)S(1)}, bf16[2,9,512,512]{3,2,1,0:T(8,128)(2,1)}, u32[]{:S(2)}) copy-start(bf16[2,9,512,512]{3,2,1,0:T(8,128)(2,1)} %blocks.3) | copy-start | bytes 28311556
